TPU v7x, 256 devices: a whole 4x4x8 slice. The times are simulated.
256 devices in a mesh: band: 8 (over z_hi, y), row: 32 (over z_lo, x, core).
Axes of the slice: x: 4, y: 4, z: 8 (z_hi: 2, z_lo: 4; z = z_hi * 4 + z_lo), core: 2. Of those that a mesh axis runs over, the one named last changes fastest.
Arguments:
- gebhart: bfloat16 [8, 2048, 65536], P('band', None, 'row'), may hold values from -0.046875 to 0.046875
- temps: float32 [256, 65536], P(None, 'row'), may hold values from 150 to 400
- emissivity: float32 [8, 65536], P('band', 'row'), may hold values from 0.1 to 0.95
- band_edges: int32 [8, 2], P('band'), may hold values from 3000 to 26998, as said below
- conductance: float32 [2048], P('row'), may hold values from 0.0005 to 0.005
- neighbours: int32 [2048, 4], P('row'), may hold values from 0 to 2047, as said below
Outputs:
- absorbed: float32 [256, 2048], P(None, 'row')
- heating: float32 [256, 2048], P(None, 'row')
Inputs may be any that keep to these rules, and one draw needn't show every extreme that they name: `band_edges`: each band's lower edge lies below its upper edge; bands rise with the band index. `neighbours`: every neighbour lies at most 64 window indices away from its panel, counted cyclically over 2048; that distance is reached.
All inputs are finite; a program needn't handle non-finite values.
Results may differ from a plain program's by a relative error of at most 0.0029.
Values sent between devices are 32-bit elements; how exact they have to be, the bound alone decides.
No kernel may reach another device: no remote copies, remote signals or barrier semaphores. Data moves between devices by JAX's collectives and lax.ppermute only.
A program may use at most 64 MiB of HBM per device.

v0:
```python
import math

import jax
import jax.numpy as jnp
from jax import lax
from jax.sharding import PartitionSpec as P


def with_halo(block, sides, width):
    for axis, dim in sides:
        count = lax.axis_size(axis)
        forward = [(i, i + 1) for i in range(count - 1)]
        forward.append((count - 1, 0))
        backward = [(target, source) for source, target in forward]
        low = lax.ppermute(
            lax.slice_in_dim(block, block.shape[dim] - width, None, axis=dim), axis, forward
        )
        high = lax.ppermute(lax.slice_in_dim(block, 0, width, axis=dim), axis, backward)
        block = jnp.concatenate([low, block, high], axis=dim)
    return block


def cumulative(edge, temps):
    z = 14388000.0 / (edge * temps)
    return 15.0 / math.pi**4 * jnp.exp(-z) * (((z + 3.0) * z + 6.0) * z + 6.0)


def band_power(temps, emissivity, band_edges):
    lower = band_edges[:, 0].astype(jnp.float32)[:, None, None]
    upper = band_edges[:, 1].astype(jnp.float32)[:, None, None]
    heat = temps[None, :, :]
    fraction = cumulative(upper, heat) - cumulative(lower, heat)
    scale = (heat / 300.0) ** 4
    return (emissivity[:, None, :] * fraction * scale).astype(jnp.bfloat16)


def conduct(extended, window, conductance, neighbours, rows, parts, mine):
    base = mine * rows - rows
    local_index = jnp.mod(neighbours - base, rows * parts)
    nearby = extended[:, local_index]
    return conductance[None, :] * jnp.sum(nearby - window[:, :, None], axis=2)


def body(gebhart, temps, emissivity, band_edges, conductance, neighbours):
    rows = conductance.shape[0]
    parts = lax.axis_size("row")
    mine = lax.axis_index("row")
    local_power = band_power(temps, emissivity, band_edges)
    own_power = local_power[:, :, :rows]
    emitted_part = jnp.sum(own_power.astype(jnp.float32), axis=0)
    absorbed_rows = lax.psum_scatter(
        jnp.einsum("brn,bkn->rk", gebhart, local_power, preferred_element_type=jnp.float32),
        "row",
        scatter_dimension=0,
        tiled=True,
    )
    absorbed, emitted = lax.psum((absorbed_rows.T, emitted_part), "band")
    window = temps[:, :rows]
    extended = with_halo(window, (("row", 1),), rows)
    heating = (
        absorbed - emitted + conduct(extended, window, conductance, neighbours, rows, parts, mine)
    )
    return (absorbed, heating)


def solution(mesh):
    return jax.shard_map(
        body,
        mesh=mesh,
        in_specs=(
            P("band", None, "row"),
            P(None, "row"),
            P("band", "row"),
            P("band", None),
            P("row"),
            P("row", None),
        ),
        out_specs=(P(None, "row"), P(None, "row")),
        check_vma=False,
    )
```

profile of v0, /device:TPU:6, one launch (start us, length us, event | category | flops | bytes accessed | tf_op | source)
XLA Modules:
  0.0 289.7 jit_solution(9215876241561155928)
XLA Ops:
  7.2 0.0 reduce-scatter.4.cloned.1.call-start
  7.2 1.3 fusion.20
  9.8 0.0 copy-start
  9.8 1.9 copy.15
  11.8 0.0 copy-done
  11.8 9.1 %fusion.2 = f32[2048,256]{0,1:T(8,128)} fusion(bf16[1,2048,2048]{2,1,0:T(8,128)(2,1)} %param.6, f32[256,2048]{0,1:T(8,128)S(1)} %copy.15, f32[]{:T(128)} %bitcast.2, f32[]{:T(128)} %bitcast.1, f32[2048]{0:T(1024)S(1)} %bitcast.25), kind=kOutput, calls=%fused_computation.5 | convolution fusion | flops 2161639424 | bytes 12591112 | tf_op jit(solution)/shard_map/brn,bkn->rk/dot_general | solution.py:52
  20.9 2.9 %copy.21 = f32[2048,256]{1,0:T(8,128)} copy(f32[2048,256]{0,1:T(8,128)} %fusion.2) | data formatting | bytes 4194304
  23.9 0.0 copy-start.1
  23.9 0.0 reduce-scatter.4.cloned.1.call-update
  23.9 0.0 all-reduce.3.cloned.1.call-start
  23.9 0.3 collective-permute-start.1
  24.3 0.2 collective-permute-start
  24.5 0.0 copy-done.1
  24.5 0.1 copy.20
  24.6 0.1 reshape.59
  24.8 2.3 fusion.22
  27.0 0.6 fusion.18
  27.7 129.2 %reduce-scatter.4.cloned.1.call-done = f32[64,256]{1,0:T(8,128)} async-done(((f32[2048,256]{1,0:T(8,128)}), f32[64,256]{1,0:T(8,128)}) %reduce-scatter.4.cloned.1.call-update) | async-done | bytes 65552 | tf_op jit(solution)/shard_map/reduce_scatter | solution.py:51
  156.9 0.0 all-reduce.3.cloned.1.call-update
  156.9 0.0 collective-permute-done.1
  156.9 0.0 collective-permute-done
  157.0 0.0 copy-start.2
  157.0 1.0 gather_fusion
  158.0 0.1 reshape.62
  158.0 0.2 fusion.17
  158.2 121.6 %all-reduce.3.cloned.1.call-done = (f32[256,64]{0,1:T(8,128)}, f32[256,64]{0,1:T(8,128)}) async-done(((f32[256,64]{0,1:T(8,128)}, f32[256,64]{0,1:T(8,128)}), (f32[256,64]{0,1:T(8,128)}, f32[256,64]{0,1:T(8,128)})) %all-reduce.3.cloned.1.call-update) | async-done | bytes 131088 | tf_op jit(solution)/shard_map/psum | solution.py:57
  279.8 0.0 copy-done.2
  279.8 1.6 multiply_add_fusion
  281.4 1.5 copy.25
  (4 shorter events, 0.0 us)
Async XLA Ops:
  7.2 149.7 %reduce-scatter.4.cloned.1.call-start = ((), (), s32[]{:S(2)}) async-start(), calls=%async_computation.1 | async-start | bytes 2162688 | tf_op jit(solution)/shard_map/reduce_scatter | solution.py:51
  9.8 1.9 copy-start
  23.9 0.7 copy-start.1
  23.9 255.9 %all-reduce.3.cloned.1.call-start = ((), (), s32[]{:S(2)}) async-start(), calls=%async_computation.2 | async-start | bytes 262144 | tf_op jit(solution)/shard_map/psum | solution.py:57
  23.9 133.0 %collective-permute-start.1 = (f32[256,64]{0,1:T(8,128)S(1)}, f32[256,64]{0,1:T(8,128)S(1)}, u32[]{:S(2)}, u32[]{:S(2)}) collective-permute-start(f32[256,64]{0,1:T(8,128)S(1)} %slice.19), channel_id=1, source_target_pairs={{1,0},{2,1},{3,2},{4,3},{5,4},{6,5},{7,6},{8,7},{9,8},{10,9},{11,1... | collective-permute-start | bytes 196616 | tf_op jit(solution)/shard_map/ppermute | solution.py:18
  24.3 132.7 %collective-permute-start = (f32[256,64]{0,1:T(8,128)S(1)}, f32[256,64]{0,1:T(8,128)S(1)}, u32[]{:S(2)}, u32[]{:S(2)}) collective-permute-start(f32[256,64]{0,1:T(8,128)S(1)} %slice.19), channel_id=1, source_target_pairs={{0,1},{1,2},{2,3},{3,4},{4,5},{5,6},{6,7},{7,8},{8,9},{9,10},{10,1... | collective-permute-start | bytes 196616 | tf_op jit(solution)/shard_map/ppermute | solution.py:15
  157.0 122.8 %copy-start.2 = (f32[64]{0:T(128)S(1)}, f32[64]{0:T(128)}, u32[]{:S(2)}) copy-start(f32[64]{0:T(128)} %param.10) | copy-start | bytes 772
Sparse Core Ops, SparseCore 0:
  24.0 132.8 reduce-scatter.3
  160.3 119.4 all-reduce.2
where the time goes:
time: 290 us
  waiting for transfers between devices  251 us (87%)
  between operations  15.4 us (5%)
  matrix products  9.14 us (3%)
  local copies, waits for them, and re-layouts  8.92 us (3%)
  other arithmetic  4.7 us (2%)
    reduce_scatter x1, waiting for transfers between devices, body(): lax.psum_scatter(jnp.einsum('brn,bkn->rk', gebhart, local_power, preferre...  129 us
    psum x1, waiting for transfers between devices, body(): absorbed, emitted = lax.psum((absorbed_rows.T, emitted_part), 'band')  122 us
    dot_general x1, matrix products, body(): jnp.einsum('brn,bkn->rk', gebhart, local_power, preferred_element_type=jn...  9.14 us
    unnamed x9, local copies, waits for them, and re-layouts  6.35 us
  transfers between devices with their start and end apart: 4, of which 2 were waited for; matrix products, arithmetic and copies ran while one was open for 2% of the time, Pallas kernels for 0%

commit v1 on v0

v1 whole, which is shorter than its diff:
```python
import math

import jax
import jax.numpy as jnp
from jax import lax
from jax.experimental import pallas as pl
from jax.experimental.pallas import tpu as pltpu
from jax.sharding import PartitionSpec as P

ROWS = 64
NX, NZ, NY = 4, 4, 4
F32 = jnp.float32
VMEM = pltpu.VMEM
LOG2E = 1.0 / math.log(2.0)
PARAMS = dict(vmem_limit_bytes=48 * 2**20)


def vspec(count):
    return [pl.BlockSpec(memory_space=VMEM)] * count


def sds(*shape, dtype=F32):
    return jax.ShapeDtypeStruct(shape, dtype)


def place():
    row = lax.axis_index("row")
    return row // (2 * NX), (row // 2) % NX, row % 2


def power_chunk(t, emis, a_lo, a_hi):
    r = pl.reciprocal(t, approx=True)
    r = r * (2.0 - t * r)
    lo = a_lo * r
    hi = a_hi * r
    cum_lo = jnp.exp2(lo * -LOG2E) * (((lo + 3.0) * lo + 6.0) * lo + 6.0)
    cum_hi = jnp.exp2(hi * -LOG2E) * (((hi + 3.0) * hi + 6.0) * hi + 6.0)
    square = t * t
    return (cum_hi - cum_lo) * (square * square) * emis


def dot_nt(a, b):
    return lax.dot_general(a, b, (((1,), (1,)), ((), ())), preferred_element_type=F32)


def gather_rows(g_hbm, gbuf, sems, x, core):
    return [
        pltpu.make_async_copy(g_hbm.at[:, (x + d) % NX, core], gbuf.at[d], sems.at[d])
        for d in range(NX)
    ]


def first_kernel(edges, emis, t_hbm, g_hbm, u, p, em, win, tbuf, gbuf, scaled, tsem, gsem):
    z, x, core = place()
    orbits = tbuf.shape[0]
    part = orbits // 4
    tcopies = [
        pltpu.make_async_copy(
            t_hbm.at[pl.ds(i * part, part)], tbuf.at[pl.ds(i * part, part)], tsem.at[i]
        )
        for i in range(4)
    ]
    for c in tcopies:
        c.start()
    gcopies = gather_rows(g_hbm, gbuf, gsem, x, 1 - core)
    for c in gcopies:
        c.start()
    a_lo = 14388000.0 / jnp.full((1, 512), edges[0, 0].astype(F32))
    a_hi = 14388000.0 / jnp.full((1, 512), edges[0, 1].astype(F32))
    scaled[...] = emis[...] * (15.0 / math.pi**4 / 300.0**4)
    for i in range(4):
        tcopies[i].wait()

        @pl.loop(0, part // 16)
        def _(j):
            rows = pl.ds(i * part + j * 16, 16)
            for c in range(4):
                cols = pl.ds(c * 512, 512)
                p[rows, cols] = power_chunk(
                    tbuf[rows, cols], scaled[:, cols], a_lo, a_hi
                ).astype(jnp.bfloat16)

    win[...] = tbuf[:, :128].T[:ROWS]
    em[...] = p[:, :128].astype(F32).T[:ROWS]
    for d in range(NX):
        gcopies[d].wait()
        g = gbuf[d].reshape(NZ * ROWS, gbuf.shape[3])
        u[d] = dot_nt(g, p[...])


def second_kernel(p, g_hbm, t, gbuf, gsem):
    z, x, core = place()
    gcopies = gather_rows(g_hbm, gbuf, gsem, x, core)
    for c in gcopies:
        c.start()
    for d in range(NX):
        gcopies[d].wait()
        g = gbuf[d].reshape(NZ * ROWS, gbuf.shape[3])
        t[d] = dot_nt(g, p[...])


def add_kernel(t, u, *outs):
    for d in range(NX):
        outs[d][...] = t[d] + u[d]


def x_sum_kernel(a, b, c, d, *outs):
    z, x, core = place()
    for i in range(NZ):
        rows = pl.ds(pl.multiple_of(((z + i) % NZ) * ROWS, ROWS), ROWS)
        outs[i][...] = (a[rows] + b[rows]) + (c[rows] + d[rows])


def sum_kernel(a, b, c, d, out):
    out[...] = (a[...] + b[...]) + (c[...] + d[...])


def pair_kernel(a, b, c, d, e, out):
    out[:ROWS] = (a[...] + b[...]) + (c[...] + d[...])
    out[ROWS:] = e[...]


def conduct_kernel(neighbours, low, window, high, out):
    z, x, core = place()
    mine = (z * NX + x) * 2 + core
    total = 32 * ROWS
    local = neighbours[...] - (mine * ROWS - ROWS)
    local = jnp.where(local < 0, local + total, local)
    local = jnp.where(local >= total, local - total, local)
    column = lax.broadcasted_iota(jnp.int32, (ROWS, ROWS), 1)
    acc = -4.0 * window[...]
    for i, block in enumerate((low, window, high)):
        count = jnp.zeros((ROWS, ROWS), F32)
        for j in range(4):
            count += jnp.where(local[:, j : j + 1] == column + i * ROWS, 1.0, 0.0)
        acc += jnp.dot(
            count, block[...], precision=lax.Precision.HIGHEST, preferred_element_type=F32
        )
    out[...] = acc


def last_kernel(mine, other, lap, conductance, absorbed, heating):
    a = mine[:ROWS] + other[:ROWS]
    e = mine[ROWS:] + other[ROWS:]
    at = a.T
    absorbed[...] = at
    heating[...] = at - e.T + conductance[...] * lap[...].T


def call(kernel, count, out_shape, scratch=(), in_specs=None, cost=None):
    single = not isinstance(out_shape, (list, tuple))
    return pl.pallas_call(
        kernel,
        out_shape=out_shape,
        in_specs=in_specs if in_specs is not None else vspec(count),
        out_specs=vspec(1)[0] if single else vspec(len(out_shape)),
        scratch_shapes=list(scratch),
        compiler_params=pltpu.CompilerParams(**PARAMS),
        cost_estimate=cost,
    )


def row_perm(move):
    return [
        ((z * NX + x) * 2 + c, (lambda a: (a[0] * NX + a[1]) * 2 + a[2])(move(z, x, c)))
        for z in range(NZ)
        for x in range(NX)
        for c in range(2)
    ]


CORE = row_perm(lambda z, x, c: (z, x, 1 - c))
XS = [row_perm(lambda z, x, c, d=d: (z, (x + d) % NX, c)) for d in range(NX)]
ZS = [row_perm(lambda z, x, c, d=d: ((z + d) % NZ, x, c)) for d in range(NZ)]
UP = [(i, (i + 1) % 32) for i in range(32)]
DOWN = [(i, (i - 1) % 32) for i in range(32)]
YS = [[(h * NY + y, h * NY + (y + d) % NY) for h in range(2) for y in range(NY)] for d in range(NY)]
HI = [(i, (i + NY) % (2 * NY)) for i in range(2 * NY)]


def body(gebhart, temps, emissivity, band_edges, conductance, neighbours):
    orbits, panels = temps.shape
    g = gebhart.reshape(NZ, NX, 2, ROWS, panels)
    half = NZ * ROWS
    hbm = pl.BlockSpec(memory_space=pl.ANY)
    gb = [VMEM((NX, NZ, ROWS, panels), jnp.bfloat16)]
    cost = pl.CostEstimate(
        flops=2 * NX * half * panels * orbits, bytes_accessed=8 * 2**20, transcendentals=0
    )
    u, p, em, win = call(
        first_kernel,
        4,
        [
            sds(NX, half, orbits),
            sds(orbits, panels, dtype=jnp.bfloat16),
            sds(ROWS, orbits),
            sds(ROWS, orbits),
        ],
        in_specs=[pl.BlockSpec(memory_space=pltpu.SMEM), vspec(1)[0], hbm, hbm],
        scratch=[
            VMEM((orbits, panels), F32),
            *gb,
            VMEM((1, panels), F32),
            pltpu.SemaphoreType.DMA((4,)),
            pltpu.SemaphoreType.DMA((NX,)),
        ],
        cost=cost,
    )(band_edges, emissivity, temps, g)
    u_in = lax.ppermute(u, "row", CORE)
    t = call(
        second_kernel,
        2,
        sds(NX, half, orbits),
        in_specs=[vspec(1)[0], hbm],
        scratch=[*gb, pltpu.SemaphoreType.DMA((NX,))],
        cost=cost,
    )(p, g)
    s = call(add_kernel, 2, [sds(half, orbits)] * NX)(t, u_in)
    x2 = lax.ppermute(s[2], "row", XS[2])
    x1 = lax.ppermute(s[1], "row", XS[1])
    x3 = lax.ppermute(s[3], "row", XS[3])
    low = lax.ppermute(win, "row", UP)
    high = lax.ppermute(win, "row", DOWN)
    e_in = [lax.ppermute(em, "band", YS[d]) for d in (1, 2, 3)]
    e = call(sum_kernel, 4, sds(ROWS, orbits))(em, *e_in)
    lap = call(conduct_kernel, 4, sds(ROWS, orbits))(neighbours, low, win, high)
    zs = call(x_sum_kernel, 4, [sds(ROWS, orbits)] * NZ)(s[0], x1, x2, x3)
    z_in = [lax.ppermute(zs[d], "row", ZS[d]) for d in (1, 2, 3)]
    ysum = call(sum_kernel, 4, sds(ROWS, orbits))(zs[0], *z_in)
    y_in = [lax.ppermute(ysum, "band", YS[d]) for d in (1, 2, 3)]
    pair = call(pair_kernel, 5, sds(2 * ROWS, orbits))(ysum, *y_in, e)
    other = lax.ppermute(pair, "band", HI)
    absorbed, heating = call(last_kernel, 4, [sds(orbits, ROWS)] * 2)(
        pair, other, lap, conductance.reshape(1, ROWS)
    )
    return absorbed, heating


def solution(mesh):
    return jax.shard_map(
        body,
        mesh=mesh,
        in_specs=(
            P("band", None, "row"),
            P(None, "row"),
            P("band", "row"),
            P("band", None),
            P("row"),
            P("row", None),
        ),
        out_specs=(P(None, "row"), P(None, "row")),
        check_vma=False,
    )
```

time: 290 us -> 66.1 us (0.23)
  the two profiles are of different devices: /device:TPU:6 before, /device:TPU:24 now
where the time goes in v1:
time: 66.1 us; the launch traced here: 65.9 us
  starting transfers between devices  30.1 us (46%)
  waiting for transfers between devices  19.7 us (30%)
  Pallas kernels  10.9 us (16%)
  local copies, waits for them, and re-layouts  4.47 us (7%)
  between operations  0.76 us (1%)
    ppermute x1, waiting for transfers between devices, body(): x2 = lax.ppermute(s[2], 'row', XS[2])  6.6 us
    ppermute x3, starting transfers between devices, body(): z_in = [lax.ppermute(zs[d], 'row', ZS[d]) for d in (1, 2, 3)]  6.27 us
    pallas_call x1, Pallas kernels, body(): call(first_kernel, 4, [sds(NX, half, orbits), sds(orbits, panels, dtype=j...  5.97 us
    ppermute x1, starting transfers between devices, body(): high = lax.ppermute(win, 'row', DOWN)  5.65 us
    ppermute x1, starting transfers between devices, body(): other = lax.ppermute(pair, 'band', HI)  5.48 us
    ppermute x1, waiting for transfers between devices, body(): x1 = lax.ppermute(s[1], 'row', XS[1])  4.24 us
    pallas_call x1, Pallas kernels, body(): call(second_kernel, 2, sds(NX, half, orbits), in_specs=[vspec(1)[0], hbm]...  4.18 us
    ppermute x3, starting transfers between devices, body(): y_in = [lax.ppermute(ysum, 'band', YS[d]) for d in (1, 2, 3)]  4.02 us
  transfers between devices with their start and end apart: 16, of which 8 were waited for; matrix products, arithmetic and copies ran while one was open for 0% of the time, Pallas kernels for 7%

profile of v1, /device:TPU:24, one launch (start us, length us, event | category | flops | bytes accessed | tf_op | source)
XLA Modules:
  0.0 65.9 jit_solution(4548603430699321853)
XLA Ops:
  0.6 1.6 %copy-done = f32[256,2048]{1,0:T(8,128)S(1)} copy-done((f32[256,2048]{1,0:T(8,128)S(1)}, f32[256,2048]{1,0:T(8,128)}, u32[]{:S(2)}) %copy-start) | copy-done | bytes 2097176
  2.2 0.7 %copy-done.1 = f32[1,2048]{1,0:T(1,128)S(1)} copy-done((f32[1,2048]{1,0:T(1,128)S(1)}, f32[1,2048]{1,0:T(1,128)}, u32[]{:S(2)}) %copy-start.1) | copy-done | bytes 8216
  2.9 0.7 copy-done.2
  3.6 6.0 %shard_map.77 = (f32[4,256,256]{2,1,0:T(8,128)S(1)}, bf16[256,2048]{1,0:T(8,128)(2,1)S(1)}, f32[64,256]{1,0:T(8,128)S(1)}, f32[64,256]{1,0:T(8,128)S(1)}) custom-call(s32[1,2]{1,0:T(1,128)S(1)} %copy-done.2, f32[1,2048]{1,0:T(1,128)S(1)} %copy-done.1, f32[256,2048]{1,0:T(8,128)S(1)} %copy-done, bf16[4,4,2,64,2048]{4,3,2,1,0:T(8,128)(2,1)} %bitcast.3), custom_call_target="tpu_custom_call" | custom-call | flops 1073741824 | bytes 8388608 | tf_op jit(solution)/shard_map/pallas_call | solution.py:190
  9.7 4.2 %shard_map.78.t = f32[4,256,256]{2,1,0:T(8,128)S(1)} custom-call(bf16[256,2048]{1,0:T(8,128)(2,1)S(1)} %get-tuple-element.14.p, bf16[4,4,2,64,2048]{4,3,2,1,0:T(8,128)(2,1)} %bitcast.4), custom_call_target="tpu_custom_call" | custom-call | flops 1073741824 | bytes 8388608 | tf_op jit(solution)/shard_map/pallas_call | solution.py:210
  13.9 0.1 shard_map.79
  14.0 1.6 %collective-permute-start.1 = (f32[256,256]{1,0:T(8,128)S(1)}, f32[256,256]{1,0:T(8,128)S(1)}, u32[]{:S(2)}, u32[]{:S(2)}) collective-permute-start(f32[256,256]{1,0:T(8,128)S(1)} %get-tuple-element.17), channel_id=1, source_target_pairs={{0,2},{1,3},{2,4},{3,5},{4,6},{5,7},{6,0},{7,1},{8,10},{9,11},{10,... | collective-permute-start | bytes 786440 | tf_op jit(solution)/shard_map/ppermute | solution.py:220
  15.6 2.7 %collective-permute-start.2 = (f32[256,256]{1,0:T(8,128)S(1)}, f32[256,256]{1,0:T(8,128)S(1)}, u32[]{:S(2)}, u32[]{:S(2)}) collective-permute-start(f32[256,256]{1,0:T(8,128)S(1)} %get-tuple-element.18), channel_id=1, source_target_pairs={{0,4},{1,5},{2,6},{3,7},{4,0},{5,1},{6,2},{7,3},{8,12},{9,13},{10,... | collective-permute-start | bytes 786440 | tf_op jit(solution)/shard_map/ppermute | solution.py:219
  18.3 1.4 %collective-permute-start.3 = (f32[256,256]{1,0:T(8,128)S(1)}, f32[256,256]{1,0:T(8,128)S(1)}, u32[]{:S(2)}, u32[]{:S(2)}) collective-permute-start(f32[256,256]{1,0:T(8,128)S(1)} %get-tuple-element.19), channel_id=1, source_target_pairs={{0,6},{1,7},{2,0},{3,1},{4,2},{5,3},{6,4},{7,5},{8,14},{9,15},{10,... | collective-permute-start | bytes 786440 | tf_op jit(solution)/shard_map/ppermute | solution.py:221
  19.7 4.2 %collective-permute-done.1.b = f32[256,256]{1,0:T(8,128)S(1)} collective-permute-done((f32[256,256]{1,0:T(8,128)S(1)}, f32[256,256]{1,0:T(8,128)S(1)}, u32[]{:S(2)}, u32[]{:S(2)}) %collective-permute-start.1) | collective-permute-done | bytes 262176 | tf_op jit(solution)/shard_map/ppermute | solution.py:220
  24.0 6.6 %collective-permute-done.2.c = f32[256,256]{1,0:T(8,128)S(1)} collective-permute-done((f32[256,256]{1,0:T(8,128)S(1)}, f32[256,256]{1,0:T(8,128)S(1)}, u32[]{:S(2)}, u32[]{:S(2)}) %collective-permute-start.2) | collective-permute-done | bytes 262176 | tf_op jit(solution)/shard_map/ppermute | solution.py:219
  30.6 2.0 %collective-permute-start.4 = (f32[64,256]{1,0:T(8,128)S(1)}, f32[64,256]{1,0:T(8,128)S(1)}, u32[]{:S(2)}, u32[]{:S(2)}) collective-permute-start(f32[64,256]{1,0:T(8,128)S(1)} %get-tuple-element.21), channel_id=1, source_target_pairs={{0,8},{1,9},{2,10},{3,11},{4,12},{5,13},{6,14},{7,15},{8,16},{9,17... | collective-permute-start | bytes 196616 | tf_op jit(solution)/shard_map/ppermute | solution.py:228
  32.6 3.3 %collective-permute-start.5 = (f32[64,256]{1,0:T(8,128)S(1)}, f32[64,256]{1,0:T(8,128)S(1)}, u32[]{:S(2)}, u32[]{:S(2)}) collective-permute-start(f32[64,256]{1,0:T(8,128)S(1)} %get-tuple-element.22), channel_id=1, source_target_pairs={{0,16},{1,17},{2,18},{3,19},{4,20},{5,21},{6,22},{7,23},{8,24},{9,... | collective-permute-start | bytes 196616 | tf_op jit(solution)/shard_map/ppermute | solution.py:228
  35.9 1.0 %collective-permute-start.6 = (f32[64,256]{1,0:T(8,128)S(1)}, f32[64,256]{1,0:T(8,128)S(1)}, u32[]{:S(2)}, u32[]{:S(2)}) collective-permute-start(f32[64,256]{1,0:T(8,128)S(1)} %get-tuple-element.23), channel_id=1, source_target_pairs={{0,24},{1,25},{2,26},{3,27},{4,28},{5,29},{6,30},{7,31},{8,0},{9,1... | collective-permute-start | bytes 196616 | tf_op jit(solution)/shard_map/ppermute | solution.py:228
  36.9 0.2 collective-permute-start.10
  37.1 2.6 %collective-permute-start.11 = (f32[64,256]{1,0:T(8,128)S(1)}, f32[64,256]{1,0:T(8,128)S(1)}, u32[]{:S(2)}, u32[]{:S(2)}) collective-permute-start(f32[64,256]{1,0:T(8,128)S(1)} %get-tuple-element.24.a), channel_id=1, source_target_pairs={{0,64},{32,96},{64,0},{96,32},{128,192},{160,224},{192,128},{224,1... | collective-permute-start | bytes 196616 | tf_op jit(solution)/shard_map/ppermute | solution.py:224
  39.7 0.7 %collective-permute-done.5.c = f32[64,256]{1,0:T(8,128)S(1)} collective-permute-done((f32[64,256]{1,0:T(8,128)S(1)}, f32[64,256]{1,0:T(8,128)S(1)}, u32[]{:S(2)}, u32[]{:S(2)}) %collective-permute-start.5) | collective-permute-done | bytes 65568 | tf_op jit(solution)/shard_map/ppermute | solution.py:228
  40.4 0.2 collective-permute-done.6.d
  40.6 2.5 %collective-permute-start.7 = (f32[64,256]{1,0:T(8,128)S(1)}, f32[64,256]{1,0:T(8,128)S(1)}, u32[]{:S(2)}, u32[]{:S(2)}) collective-permute-start(f32[64,256]{1,0:T(8,128)S(1)} %shard_map.81.a), channel_id=1, source_target_pairs={{0,32},{32,64},{64,96},{96,0},{128,160},{160,192},{192,224},{224,1... | collective-permute-start | bytes 196616 | tf_op jit(solution)/shard_map/ppermute | solution.py:230
  43.1 0.4 collective-permute-start.8
  43.5 1.1 %collective-permute-start.9 = (f32[64,256]{1,0:T(8,128)S(1)}, f32[64,256]{1,0:T(8,128)S(1)}, u32[]{:S(2)}, u32[]{:S(2)}) collective-permute-start(f32[64,256]{1,0:T(8,128)S(1)} %shard_map.81.a), channel_id=1, source_target_pairs={{0,96},{32,0},{64,32},{96,64},{128,224},{160,128},{192,160},{224,1... | collective-permute-start | bytes 196616 | tf_op jit(solution)/shard_map/ppermute | solution.py:230
  44.6 0.9 %collective-permute-done.12.d = f32[64,256]{1,0:T(8,128)S(1)} collective-permute-done((f32[64,256]{1,0:T(8,128)S(1)}, f32[64,256]{1,0:T(8,128)S(1)}, u32[]{:S(2)}, u32[]{:S(2)}) %collective-permute-start.12) | collective-permute-done | bytes 65568 | tf_op jit(solution)/shard_map/ppermute | solution.py:224
  45.5 3.4 %collective-permute-done.8.c = f32[64,256]{1,0:T(8,128)S(1)} collective-permute-done((f32[64,256]{1,0:T(8,128)S(1)}, f32[64,256]{1,0:T(8,128)S(1)}, u32[]{:S(2)}, u32[]{:S(2)}) %collective-permute-start.8) | collective-permute-done | bytes 65568 | tf_op jit(solution)/shard_map/ppermute | solution.py:230
  48.9 0.6 collective-permute-done.9.d
  49.6 5.5 %collective-permute-start.13 = (f32[128,256]{1,0:T(8,128)S(1)}, f32[128,256]{1,0:T(8,128)S(1)}, u32[]{:S(2)}, u32[]{:S(2)}) collective-permute-start(f32[128,256]{1,0:T(8,128)S(1)} %shard_map.83.mine), channel_id=1, source_target_pairs={{0,128},{32,160},{64,192},{96,224},{128,0},{160,32},{192,64},{224,... | collective-permute-start | bytes 393224 | tf_op jit(solution)/shard_map/ppermute | solution.py:232
  55.0 5.7 %collective-permute-start.15 = (f32[64,256]{1,0:T(8,128)S(1)}, f32[64,256]{1,0:T(8,128)S(1)}, u32[]{:S(2)}, u32[]{:S(2)}) collective-permute-start(f32[64,256]{1,0:T(8,128)S(1)} %get-tuple-element.25.window), channel_id=1, source_target_pairs={{0,31},{1,0},{2,1},{3,2},{4,3},{5,4},{6,5},{7,6},{8,7},{9,8},{10,9... | collective-permute-start | bytes 196616 | tf_op jit(solution)/shard_map/ppermute | solution.py:223
  60.7 0.1 copy.8.neighbours
  60.8 3.1 %collective-permute-done.14.low = f32[64,256]{1,0:T(8,128)S(1)} collective-permute-done((f32[64,256]{1,0:T(8,128)S(1)}, f32[64,256]{1,0:T(8,128)S(1)}, u32[]{:S(2)}, u32[]{:S(2)}) %collective-permute-start.14) | collective-permute-done | bytes 65568 | tf_op jit(solution)/shard_map/ppermute | solution.py:222
  63.9 0.4 shard_map.84.lap
  64.3 0.2 shard_map.85
  64.5 0.7 %copy.10 = f32[256,64]{0,1:T(8,128)} copy(f32[256,64]{1,0:T(8,128)S(1)} %get-tuple-element.27) | data formatting | bytes 131072 | tf_op jit(solution)/shard_map/pallas_call | solution.py:233
  65.2 0.7 %copy.9 = f32[256,64]{0,1:T(8,128)} copy(f32[256,64]{1,0:T(8,128)S(1)} %get-tuple-element.26) | data formatting | bytes 131072 | tf_op jit(solution)/shard_map/pallas_call | solution.py:233
  (22 shorter events, 0.2 us)
Async XLA Ops:
  0.6 1.6 %copy-start = (f32[256,2048]{1,0:T(8,128)S(1)}, f32[256,2048]{1,0:T(8,128)}, u32[]{:S(2)}) copy-start(f32[256,2048]{1,0:T(8,128)} %t_hbm.1) | copy-start | bytes 6291460
  2.2 0.7 %copy-start.1 = (f32[1,2048]{1,0:T(1,128)S(1)}, f32[1,2048]{1,0:T(1,128)}, u32[]{:S(2)}) copy-start(f32[1,2048]{1,0:T(1,128)} %emis.1) | copy-start | bytes 24580
  2.9 0.7 copy-start.2
  9.6 51.1 %copy-start.4 = (s32[64,4]{0,1:T(4,128)S(1)}, s32[64,4]{0,1:T(4,128)}, u32[]{:S(2)}) copy-start(s32[64,4]{0,1:T(4,128)} %param.11) | copy-start | bytes 3076
  9.6 54.7 %copy-start.3 = (f32[64]{0:T(128)S(1)}, f32[64]{0:T(128)}, u32[]{:S(2)}) copy-start(f32[64]{0:T(128)} %param.10) | copy-start | bytes 772
  9.6 4.3 %collective-permute-start = (f32[4,256,256]{2,1,0:T(8,128)S(1)}, f32[4,256,256]{2,1,0:T(8,128)S(1)}, u32[]{:S(2)}, u32[]{:S(2)}) collective-permute-start(f32[4,256,256]{2,1,0:T(8,128)S(1)} %get-tuple-element.15), channel_id=1, source_target_pairs={{0,1},{1,0},{2,3},{3,2},{4,5},{5,4},{6,7},{7,6},{8,9},{9,8},{10,11... | collective-permute-start | bytes 3145736 | tf_op jit(solution)/shard_map/ppermute | solution.py:209
  14.0 10.0 %collective-permute-start.1 = (f32[256,256]{1,0:T(8,128)S(1)}, f32[256,256]{1,0:T(8,128)S(1)}, u32[]{:S(2)}, u32[]{:S(2)}) collective-permute-start(f32[256,256]{1,0:T(8,128)S(1)} %get-tuple-element.17), channel_id=1, source_target_pairs={{0,2},{1,3},{2,4},{3,5},{4,6},{5,7},{6,0},{7,1},{8,10},{9,11},{10,... | collective-permute-start | bytes 786440 | tf_op jit(solution)/shard_map/ppermute | solution.py:220
  15.6 15.0 %collective-permute-start.2 = (f32[256,256]{1,0:T(8,128)S(1)}, f32[256,256]{1,0:T(8,128)S(1)}, u32[]{:S(2)}, u32[]{:S(2)}) collective-permute-start(f32[256,256]{1,0:T(8,128)S(1)} %get-tuple-element.18), channel_id=1, source_target_pairs={{0,4},{1,5},{2,6},{3,7},{4,0},{5,1},{6,2},{7,3},{8,12},{9,13},{10,... | collective-permute-start | bytes 786440 | tf_op jit(solution)/shard_map/ppermute | solution.py:219
  18.3 12.3 %collective-permute-start.3 = (f32[256,256]{1,0:T(8,128)S(1)}, f32[256,256]{1,0:T(8,128)S(1)}, u32[]{:S(2)}, u32[]{:S(2)}) collective-permute-start(f32[256,256]{1,0:T(8,128)S(1)} %get-tuple-element.19), channel_id=1, source_target_pairs={{0,6},{1,7},{2,0},{3,1},{4,2},{5,3},{6,4},{7,5},{8,14},{9,15},{10,... | collective-permute-start | bytes 786440 | tf_op jit(solution)/shard_map/ppermute | solution.py:221
  30.6 9.1 %collective-permute-start.4 = (f32[64,256]{1,0:T(8,128)S(1)}, f32[64,256]{1,0:T(8,128)S(1)}, u32[]{:S(2)}, u32[]{:S(2)}) collective-permute-start(f32[64,256]{1,0:T(8,128)S(1)} %get-tuple-element.21), channel_id=1, source_target_pairs={{0,8},{1,9},{2,10},{3,11},{4,12},{5,13},{6,14},{7,15},{8,16},{9,17... | collective-permute-start | bytes 196616 | tf_op jit(solution)/shard_map/ppermute | solution.py:228
  32.6 7.8 %collective-permute-start.5 = (f32[64,256]{1,0:T(8,128)S(1)}, f32[64,256]{1,0:T(8,128)S(1)}, u32[]{:S(2)}, u32[]{:S(2)}) collective-permute-start(f32[64,256]{1,0:T(8,128)S(1)} %get-tuple-element.22), channel_id=1, source_target_pairs={{0,16},{1,17},{2,18},{3,19},{4,20},{5,21},{6,22},{7,23},{8,24},{9,... | collective-permute-start | bytes 196616 | tf_op jit(solution)/shard_map/ppermute | solution.py:228
  35.9 4.7 %collective-permute-start.6 = (f32[64,256]{1,0:T(8,128)S(1)}, f32[64,256]{1,0:T(8,128)S(1)}, u32[]{:S(2)}, u32[]{:S(2)}) collective-permute-start(f32[64,256]{1,0:T(8,128)S(1)} %get-tuple-element.23), channel_id=1, source_target_pairs={{0,24},{1,25},{2,26},{3,27},{4,28},{5,29},{6,30},{7,31},{8,0},{9,1... | collective-permute-start | bytes 196616 | tf_op jit(solution)/shard_map/ppermute | solution.py:228
  36.9 6.6 %collective-permute-start.10 = (f32[64,256]{1,0:T(8,128)S(1)}, f32[64,256]{1,0:T(8,128)S(1)}, u32[]{:S(2)}, u32[]{:S(2)}) collective-permute-start(f32[64,256]{1,0:T(8,128)S(1)} %get-tuple-element.24.a), channel_id=1, source_target_pairs={{0,32},{32,64},{64,96},{96,0},{128,160},{160,192},{192,224},{224,1... | collective-permute-start | bytes 196616 | tf_op jit(solution)/shard_map/ppermute | solution.py:224
  37.1 7.5 %collective-permute-start.11 = (f32[64,256]{1,0:T(8,128)S(1)}, f32[64,256]{1,0:T(8,128)S(1)}, u32[]{:S(2)}, u32[]{:S(2)}) collective-permute-start(f32[64,256]{1,0:T(8,128)S(1)} %get-tuple-element.24.a), channel_id=1, source_target_pairs={{0,64},{32,96},{64,0},{96,32},{128,192},{160,224},{192,128},{224,1... | collective-permute-start | bytes 196616 | tf_op jit(solution)/shard_map/ppermute | solution.py:224
  39.7 5.8 %collective-permute-start.12 = (f32[64,256]{1,0:T(8,128)S(1)}, f32[64,256]{1,0:T(8,128)S(1)}, u32[]{:S(2)}, u32[]{:S(2)}) collective-permute-start(f32[64,256]{1,0:T(8,128)S(1)} %get-tuple-element.24.a), channel_id=1, source_target_pairs={{0,96},{32,0},{64,32},{96,64},{128,224},{160,128},{192,160},{224,1... | collective-permute-start | bytes 196616 | tf_op jit(solution)/shard_map/ppermute | solution.py:224
  40.6 5.0 %collective-permute-start.7 = (f32[64,256]{1,0:T(8,128)S(1)}, f32[64,256]{1,0:T(8,128)S(1)}, u32[]{:S(2)}, u32[]{:S(2)}) collective-permute-start(f32[64,256]{1,0:T(8,128)S(1)} %shard_map.81.a), channel_id=1, source_target_pairs={{0,32},{32,64},{64,96},{96,0},{128,160},{160,192},{192,224},{224,1... | collective-permute-start | bytes 196616 | tf_op jit(solution)/shard_map/ppermute | solution.py:230
  43.1 5.8 %collective-permute-start.8 = (f32[64,256]{1,0:T(8,128)S(1)}, f32[64,256]{1,0:T(8,128)S(1)}, u32[]{:S(2)}, u32[]{:S(2)}) collective-permute-start(f32[64,256]{1,0:T(8,128)S(1)} %shard_map.81.a), channel_id=1, source_target_pairs={{0,64},{32,96},{64,0},{96,32},{128,192},{160,224},{192,128},{224,1... | collective-permute-start | bytes 196616 | tf_op jit(solution)/shard_map/ppermute | solution.py:230
  43.5 6.1 %collective-permute-start.9 = (f32[64,256]{1,0:T(8,128)S(1)}, f32[64,256]{1,0:T(8,128)S(1)}, u32[]{:S(2)}, u32[]{:S(2)}) collective-permute-start(f32[64,256]{1,0:T(8,128)S(1)} %shard_map.81.a), channel_id=1, source_target_pairs={{0,96},{32,0},{64,32},{96,64},{128,224},{160,128},{192,160},{224,1... | collective-permute-start | bytes 196616 | tf_op jit(solution)/shard_map/ppermute | solution.py:230
  49.6 14.7 %collective-permute-start.13 = (f32[128,256]{1,0:T(8,128)S(1)}, f32[128,256]{1,0:T(8,128)S(1)}, u32[]{:S(2)}, u32[]{:S(2)}) collective-permute-start(f32[128,256]{1,0:T(8,128)S(1)} %shard_map.83.mine), channel_id=1, source_target_pairs={{0,128},{32,160},{64,192},{96,224},{128,0},{160,32},{192,64},{224,... | collective-permute-start | bytes 393224 | tf_op jit(solution)/shard_map/ppermute | solution.py:232
  55.0 8.8 %collective-permute-start.14 = (f32[64,256]{1,0:T(8,128)S(1)}, f32[64,256]{1,0:T(8,128)S(1)}, u32[]{:S(2)}, u32[]{:S(2)}) collective-permute-start(f32[64,256]{1,0:T(8,128)S(1)} %get-tuple-element.25.window), channel_id=1, source_target_pairs={{0,1},{1,2},{2,3},{3,4},{4,5},{5,6},{6,7},{7,8},{8,9},{9,10},{10,1... | collective-permute-start | bytes 196616 | tf_op jit(solution)/shard_map/ppermute | solution.py:222
  55.0 8.8 %collective-permute-start.15 = (f32[64,256]{1,0:T(8,128)S(1)}, f32[64,256]{1,0:T(8,128)S(1)}, u32[]{:S(2)}, u32[]{:S(2)}) collective-permute-start(f32[64,256]{1,0:T(8,128)S(1)} %get-tuple-element.25.window), channel_id=1, source_target_pairs={{0,31},{1,0},{2,1},{3,2},{4,3},{5,4},{6,5},{7,6},{8,7},{9,8},{10,9... | collective-permute-start | bytes 196616 | tf_op jit(solution)/shard_map/ppermute | solution.py:223

commit v2 on v1

v2 whole, which is shorter than its diff:
```python
import math

import jax
import jax.numpy as jnp
from jax import lax
from jax.experimental import pallas as pl
from jax.experimental.pallas import tpu as pltpu
from jax.sharding import PartitionSpec as P

ROWS = 64
NX, NZ, NY = 4, 4, 4
F32 = jnp.float32
VMEM = pltpu.VMEM
LOG2E = 1.0 / math.log(2.0)
PARAMS = dict(vmem_limit_bytes=24 * 2**20)


def vspec(count):
    return [pl.BlockSpec(memory_space=VMEM)] * count


def sds(*shape, dtype=F32):
    return jax.ShapeDtypeStruct(shape, dtype)


def place():
    row = lax.axis_index("row")
    return row // (2 * NX), (row // 2) % NX, row % 2


def power_chunk(t, emis, a_lo, a_hi):
    r = pl.reciprocal(t, approx=True)
    r = r * (2.0 - t * r)
    lo = a_lo * r
    hi = a_hi * r
    cum_lo = jnp.exp2(lo * -LOG2E) * (((lo + 3.0) * lo + 6.0) * lo + 6.0)
    cum_hi = jnp.exp2(hi * -LOG2E) * (((hi + 3.0) * hi + 6.0) * hi + 6.0)
    square = t * t
    return (cum_hi - cum_lo) * (square * square) * emis


def dot_nt(a, b):
    return lax.dot_general(a, b, (((1,), (1,)), ((), ())), preferred_element_type=F32)


def gather_rows(g_hbm, gbuf, sems, x, core):
    return [
        pltpu.make_async_copy(g_hbm.at[:, (x + d) % NX, core], gbuf.at[d], sems.at[d])
        for d in range(NX)
    ]


def first_kernel(
    edges_hbm, emis_hbm, t_hbm, g_hbm, u, p, gown, win, par, tbuf, gbuf, scaled, edges, tsem, gsem, osem, ssem
):
    z, x, core = place()
    part = tbuf.shape[0] // 4
    small = [
        pltpu.make_async_copy(edges_hbm, edges, ssem.at[0]),
        pltpu.make_async_copy(emis_hbm, scaled, ssem.at[1]),
    ]
    tcopies = [
        pltpu.make_async_copy(
            t_hbm.at[pl.ds(i * part, part)], tbuf.at[pl.ds(i * part, part)], tsem.at[i]
        )
        for i in range(4)
    ]
    gcopies = gather_rows(g_hbm, gbuf, gsem, x, 1 - core)
    ocopies = gather_rows(g_hbm, gown, osem, x, core)
    for c in small + tcopies + gcopies + ocopies:
        c.start()
    for c in small:
        c.wait()
    a_lo = 14388000.0 / jnp.full((1, 512), edges[0, 0].astype(F32))
    a_hi = 14388000.0 / jnp.full((1, 512), edges[0, 1].astype(F32))
    scaled[...] = scaled[...] * (15.0 / math.pi**4 / 300.0**4)
    lane = lax.broadcasted_iota(jnp.int32, (8, 256), 1)
    line = jnp.broadcast_to(scaled[:, :256], (8, 256))
    line = jnp.where(lane == ROWS, a_lo[:, :256], line)
    par[...] = jnp.where(lane == ROWS + 1, a_hi[:, :256], line)
    for i in range(4):
        tcopies[i].wait()

        @pl.loop(0, part // 16)
        def _(j):
            rows = pl.ds(i * part + j * 16, 16)
            for c in range(4):
                cols = pl.ds(c * 512, 512)
                p[rows, cols] = power_chunk(
                    tbuf[rows, cols], scaled[:, cols], a_lo, a_hi
                ).astype(jnp.bfloat16)

    half = NZ * ROWS
    w = tbuf[:, :128].T[:ROWS]
    win[...] = w
    u[NX * half :] = w
    for d in range(NX):
        gcopies[d].wait()
        u[d * half : (d + 1) * half] = dot_nt(gbuf[d].reshape(half, gbuf.shape[3]), p[...])
    for c in ocopies:
        c.wait()


def second_kernel(p, g, t):
    for d in range(NX):
        t[d] = dot_nt(g[d].reshape(NZ * ROWS, g.shape[3]), p[...])


def add_kernel(t, u, *outs):
    half = NZ * ROWS
    for d in range(NX):
        outs[d][...] = t[d] + u[d * half : (d + 1) * half]
    outs[NX][...] = u[NX * half :]


def x_sum_kernel(a, b, c, d, *outs):
    z, x, core = place()
    for i in range(NZ):
        rows = pl.ds(pl.multiple_of(((z + i) % NZ) * ROWS, ROWS), ROWS)
        outs[i][...] = (a[rows] + b[rows]) + (c[rows] + d[rows])


def z_sum_kernel(a, b, c, d, par, cross, out):
    out[:ROWS] = (a[...] + b[...]) + (c[...] + d[...])
    out[ROWS:] = par[...]


def y_sum_kernel(a, b, c, d, out):
    out[:ROWS] = (a[:ROWS] + b[:ROWS]) + (c[:ROWS] + d[:ROWS])
    for i, ref in enumerate((a, b, c, d)):
        out[ROWS + i : ROWS + i + 1] = ref[ROWS : ROWS + 1]
    out[ROWS + NY :] = jnp.zeros((8 - NY, out.shape[1]), F32)


def emitted(par, win):
    total = jnp.zeros(win.shape, F32)
    columns = jnp.broadcast_to(par, (8, par.shape[1]))[:, :128].T
    for i in range(NY):
        part = power_chunk(
            win, columns[:ROWS, i : i + 1], par[i, ROWS], par[i, ROWS + 1]
        )
        total += part.astype(jnp.bfloat16).astype(F32)
    return total


def side_kernel(neighbours, conductance, swapped, window, cross, mine, out):
    z, x, core = place()
    me = (z * NX + x) * 2 + core
    total = 32 * ROWS
    local = neighbours[...] - (me * ROWS - ROWS)
    local = jnp.where(local < 0, local + total, local)
    local = jnp.where(local >= total, local - total, local)
    row = lax.broadcasted_iota(jnp.int32, (ROWS, ROWS), 0)
    lane = lax.broadcasted_iota(jnp.int32, (ROWS, ROWS), 1)
    low = jnp.where(core == 0, cross[...], swapped[...])
    high = jnp.where(core == 0, swapped[...], cross[...])
    acc = -emitted(mine[ROWS:], window[...])
    for i, block in enumerate((low, window[...], high)):
        count = jnp.where(row == lane, -4.0, 0.0) if i == 1 else jnp.zeros((ROWS, ROWS), F32)
        for j in range(4):
            count += jnp.where(local[j : j + 1] == row + i * ROWS, 1.0, 0.0)
        acc += lax.dot_general(
            count * conductance[...],
            block,
            (((0,), (0,)), ((), ())),
            precision=lax.Precision.HIGHEST,
            preferred_element_type=F32,
        )
    out[...] = acc


def last_kernel(mine, other, side, window, absorbed, heating):
    a = mine[:ROWS] + other[:ROWS]
    absorbed[...] = a
    heating[...] = a + side[...] - emitted(other[ROWS:], window[...])


def call(kernel, count, out_shape, scratch=(), in_specs=None, cost=None):
    single = not isinstance(out_shape, (list, tuple))
    return pl.pallas_call(
        kernel,
        out_shape=out_shape,
        in_specs=in_specs if in_specs is not None else vspec(count),
        out_specs=vspec(1)[0] if single else vspec(len(out_shape)),
        scratch_shapes=list(scratch),
        compiler_params=pltpu.CompilerParams(**PARAMS),
        cost_estimate=cost,
    )


def row_perm(move):
    return [
        ((z * NX + x) * 2 + c, (lambda a: (a[0] * NX + a[1]) * 2 + a[2])(move(z, x, c)))
        for z in range(NZ)
        for x in range(NX)
        for c in range(2)
    ]


CORE = row_perm(lambda z, x, c: (z, x, 1 - c))
XS = [row_perm(lambda z, x, c, d=d: (z, (x + d) % NX, c)) for d in range(NX)]
ZS = [row_perm(lambda z, x, c, d=d: ((z + d) % NZ, x, c)) for d in range(NZ)]
CROSS = [(i, (i + 1 if i % 2 else i - 1) % 32) for i in range(32)]
YS = [[(h * NY + y, h * NY + (y + d) % NY) for h in range(2) for y in range(NY)] for d in range(NY)]
HI = [(i, (i + NY) % (2 * NY)) for i in range(2 * NY)]


def body(gebhart, temps, emissivity, band_edges, conductance, neighbours):
    orbits, panels = temps.shape
    g = gebhart.reshape(NZ, NX, 2, ROWS, panels)
    half = NZ * ROWS
    hbm = pl.BlockSpec(memory_space=pltpu.HBM)
    bf = jnp.bfloat16
    dma = pltpu.SemaphoreType.DMA
    block = sds(ROWS, orbits)
    message = sds(ROWS + 8, orbits)
    cost = pl.CostEstimate(
        flops=2 * NX * half * panels * orbits, bytes_accessed=8 * 2**20, transcendentals=0
    )
    far = [
        pltpu.with_memory_space_constraint(a, pltpu.HBM)
        for a in (band_edges, emissivity, temps, g)
    ]
    u, p, gown, win, par = call(
        first_kernel,
        4,
        [
            sds(NX * half + ROWS, orbits),
            sds(orbits, panels, dtype=bf),
            sds(NX, NZ, ROWS, panels, dtype=bf),
            block,
            sds(8, orbits),
        ],
        in_specs=[hbm] * 4,
        scratch=[
            VMEM((orbits, panels), F32),
            VMEM((NX, NZ, ROWS, panels), bf),
            VMEM((1, panels), F32),
            pltpu.SMEM((1, 2), jnp.int32),
            dma((4,)),
            dma((NX,)),
            dma((NX,)),
            dma((2,)),
        ],
        cost=cost,
    )(*far)
    u_in = lax.ppermute(u, "row", CORE)
    t = call(second_kernel, 2, sds(NX, half, orbits), cost=cost)(p, gown)
    *s, swapped = call(add_kernel, 2, [sds(half, orbits)] * NX + [block])(t, u_in)
    x2 = lax.ppermute(s[2], "row", XS[2])
    x1 = lax.ppermute(s[1], "row", XS[1])
    x3 = lax.ppermute(s[3], "row", XS[3])
    cross = lax.ppermute(win, "row", CROSS)
    zs = call(x_sum_kernel, 4, [block] * NZ)(s[0], x1, x2, x3)
    z_in = [lax.ppermute(zs[d], "row", ZS[d]) for d in (1, 2, 3)]
    zsum = call(z_sum_kernel, 6, message)(zs[0], *z_in, par, cross)
    y_in = [lax.ppermute(zsum, "band", YS[d]) for d in (1, 2, 3)]
    mine = call(y_sum_kernel, 4, message)(zsum, *y_in)
    other = lax.ppermute(mine, "band", HI)
    side = call(side_kernel, 6, block)(
        neighbours.T, conductance.reshape(1, ROWS), swapped, win, cross, mine
    )
    absorbed, heating = call(last_kernel, 4, [block] * 2)(mine, other, side, win)
    return absorbed.T, heating.T


def solution(mesh):
    return jax.shard_map(
        body,
        mesh=mesh,
        in_specs=(
            P("band", None, "row"),
            P(None, "row"),
            P("band", "row"),
            P("band", None),
            P("row"),
            P("row", None),
        ),
        out_specs=(P(None, "row"), P(None, "row")),
        check_vma=False,
    )
```

time: 66.1 us -> 58.7 us (0.89)
  the two profiles are of different devices: /device:TPU:24 before, /device:TPU:6 now
where the time goes in v2:
time: 58.7 us; the launch traced here: 57.8 us
  waiting for transfers between devices  26.2 us (45%)
  starting transfers between devices  19.6 us (33%)
  Pallas kernels  11.3 us (19%)
  between operations  0.7 us (1%)
    ppermute x1, waiting for transfers between devices, body(): x1 = lax.ppermute(s[1], 'row', XS[1])  9.55 us
    pallas_call x1, Pallas kernels, body(): call(first_kernel, 4, [sds(NX * half + ROWS, orbits), sds(orbits, panels,...  8.3 us
    ppermute x1, starting transfers between devices, body(): other = lax.ppermute(mine, 'band', HI)  5.8 us
    ppermute x3, waiting for transfers between devices, body(): y_in = [lax.ppermute(zsum, 'band', YS[d]) for d in (1, 2, 3)]  5.04 us
    ppermute x3, starting transfers between devices, body(): z_in = [lax.ppermute(zs[d], 'row', ZS[d]) for d in (1, 2, 3)]  4.54 us
    ppermute x3, starting transfers between devices, body(): y_in = [lax.ppermute(zsum, 'band', YS[d]) for d in (1, 2, 3)]  4.44 us
    ppermute x3, waiting for transfers between devices, body(): z_in = [lax.ppermute(zs[d], 'row', ZS[d]) for d in (1, 2, 3)]  4.24 us
    ppermute x1, waiting for transfers between devices, body(): x3 = lax.ppermute(s[3], 'row', XS[3])  3.95 us
  transfers between devices with their start and end apart: 12, of which 9 were waited for; matrix products, arithmetic and copies ran while one was open for 0% of the time, Pallas kernels for 3%

profile of v2, /device:TPU:6, one launch (start us, length us, event | category | flops | bytes accessed | tf_op | source)
XLA Modules:
  0.0 57.8 jit_solution(11191286776599388712)
XLA Ops:
  0.6 8.3 %shard_map.77 = (f32[1088,256]{1,0:T(8,128)S(1)}, bf16[256,2048]{1,0:T(8,128)(2,1)S(1)}, bf16[4,4,64,2048]{3,2,1,0:T(8,128)(2,1)S(1)}, f32[64,256]{1,0:T(8,128)S(1)}, f32[8,256]{1,0:T(8,128)S(1)}) custom-call(s32[1,2]{1,0:T(1,128)} %edges_hbm.1, f32[1,2048]{1,0:T(1,128)} %emis_hbm.1, f32[256,2048]{1,0:T(8,128)} %t_hbm.1, bf16[4,4,2,64,2048]{4,3,2,1,0:T(8,128)(2,1)} %bitcast.7), custom_call_target="tpu_custom_call" | custom-call | flops 1073741824 | bytes 8388608 | tf_op jit(solution)/shard_map/pallas_call | solution.py:224
  8.9 0.1 collective-permute-start
  9.0 1.3 %shard_map.78.t = f32[4,256,256]{2,1,0:T(8,128)S(1)} custom-call(bf16[256,2048]{1,0:T(8,128)(2,1)S(1)} %get-tuple-element.18.p, bf16[4,4,64,2048]{3,2,1,0:T(8,128)(2,1)S(1)} %get-tuple-element.19.g), custom_call_target="tpu_custom_call" | custom-call | flops 1073741824 | bytes 8388608 | tf_op jit(solution)/shard_map/pallas_call | solution.py:248
  10.3 0.0 copy-start
  10.4 0.0 copy-start.1
  10.4 1.4 %collective-permute-done.u = f32[1088,256]{1,0:T(8,128)S(1)} collective-permute-done((f32[1088,256]{1,0:T(8,128)S(1)}, f32[1088,256]{1,0:T(8,128)S(1)}, u32[]{:S(2)}, u32[]{:S(2)}) %collective-permute-start) | collective-permute-done | bytes 1114144 | tf_op jit(solution)/shard_map/ppermute | solution.py:247
  11.8 0.1 shard_map.79
  11.9 2.3 %collective-permute-start.1 = (f32[256,256]{1,0:T(8,128)S(1)}, f32[256,256]{1,0:T(8,128)S(1)}, u32[]{:S(2)}, u32[]{:S(2)}) collective-permute-start(f32[256,256]{1,0:T(8,128)S(1)} %get-tuple-element.22), channel_id=1, source_target_pairs={{0,2},{1,3},{2,4},{3,5},{4,6},{5,7},{6,0},{7,1},{8,10},{9,11},{10,... | collective-permute-start | bytes 786440 | tf_op jit(solution)/shard_map/ppermute | solution.py:251
  14.2 0.7 %collective-permute-start.2 = (f32[256,256]{1,0:T(8,128)S(1)}, f32[256,256]{1,0:T(8,128)S(1)}, u32[]{:S(2)}, u32[]{:S(2)}) collective-permute-start(f32[256,256]{1,0:T(8,128)S(1)} %get-tuple-element.23), channel_id=1, source_target_pairs={{0,4},{1,5},{2,6},{3,7},{4,0},{5,1},{6,2},{7,3},{8,12},{9,13},{10,... | collective-permute-start | bytes 786440 | tf_op jit(solution)/shard_map/ppermute | solution.py:250
  14.9 0.3 collective-permute-start.3
  15.1 1.4 %collective-permute-start.7 = (f32[64,256]{1,0:T(8,128)S(1)}, f32[64,256]{1,0:T(8,128)S(1)}, u32[]{:S(2)}, u32[]{:S(2)}) collective-permute-start(f32[64,256]{1,0:T(8,128)S(1)} %get-tuple-element.30.window), channel_id=1, source_target_pairs={{0,31},{1,2},{2,1},{3,4},{4,3},{5,6},{6,5},{7,8},{8,7},{9,10},{10,... | collective-permute-start | bytes 196616 | tf_op jit(solution)/shard_map/ppermute | solution.py:253
  16.6 9.5 %collective-permute-done.1.b = f32[256,256]{1,0:T(8,128)S(1)} collective-permute-done((f32[256,256]{1,0:T(8,128)S(1)}, f32[256,256]{1,0:T(8,128)S(1)}, u32[]{:S(2)}, u32[]{:S(2)}) %collective-permute-start.1) | collective-permute-done | bytes 262176 | tf_op jit(solution)/shard_map/ppermute | solution.py:251
  26.1 0.0 collective-permute-done.2.c
  26.1 3.9 %collective-permute-done.3.d = f32[256,256]{1,0:T(8,128)S(1)} collective-permute-done((f32[256,256]{1,0:T(8,128)S(1)}, f32[256,256]{1,0:T(8,128)S(1)}, u32[]{:S(2)}, u32[]{:S(2)}) %collective-permute-start.3) | collective-permute-done | bytes 262176 | tf_op jit(solution)/shard_map/ppermute | solution.py:252
  30.1 0.1 shard_map.80
  30.1 0.3 collective-permute-start.4
  30.4 3.3 %collective-permute-start.5 = (f32[64,256]{1,0:T(8,128)S(1)}, f32[64,256]{1,0:T(8,128)S(1)}, u32[]{:S(2)}, u32[]{:S(2)}) collective-permute-start(f32[64,256]{1,0:T(8,128)S(1)} %get-tuple-element.27), channel_id=1, source_target_pairs={{0,16},{1,17},{2,18},{3,19},{4,20},{5,21},{6,22},{7,23},{8,24},{9,... | collective-permute-start | bytes 196616 | tf_op jit(solution)/shard_map/ppermute | solution.py:255
  33.7 1.0 %collective-permute-start.6 = (f32[64,256]{1,0:T(8,128)S(1)}, f32[64,256]{1,0:T(8,128)S(1)}, u32[]{:S(2)}, u32[]{:S(2)}) collective-permute-start(f32[64,256]{1,0:T(8,128)S(1)} %get-tuple-element.28), channel_id=1, source_target_pairs={{0,24},{1,25},{2,26},{3,27},{4,28},{5,29},{6,30},{7,31},{8,0},{9,1... | collective-permute-start | bytes 196616 | tf_op jit(solution)/shard_map/ppermute | solution.py:255
  34.7 0.0 collective-permute-done.7.cross
  34.7 2.4 %collective-permute-done.4.b = f32[64,256]{1,0:T(8,128)S(1)} collective-permute-done((f32[64,256]{1,0:T(8,128)S(1)}, f32[64,256]{1,0:T(8,128)S(1)}, u32[]{:S(2)}, u32[]{:S(2)}) %collective-permute-start.4) | collective-permute-done | bytes 65568 | tf_op jit(solution)/shard_map/ppermute | solution.py:255
  37.1 1.8 %collective-permute-done.5.c = f32[64,256]{1,0:T(8,128)S(1)} collective-permute-done((f32[64,256]{1,0:T(8,128)S(1)}, f32[64,256]{1,0:T(8,128)S(1)}, u32[]{:S(2)}, u32[]{:S(2)}) %collective-permute-start.5) | collective-permute-done | bytes 65568 | tf_op jit(solution)/shard_map/ppermute | solution.py:255
  38.9 0.0 collective-permute-done.6.d
  38.9 2.8 %collective-permute-start.10 = (f32[72,256]{1,0:T(8,128)S(1)}, f32[72,256]{1,0:T(8,128)S(1)}, u32[]{:S(2)}, u32[]{:S(2)}) collective-permute-start(f32[72,256]{1,0:T(8,128)S(1)} %shard_map.81.a), channel_id=1, source_target_pairs={{0,96},{32,0},{64,32},{96,64},{128,224},{160,128},{192,160},{224,1... | collective-permute-start | bytes 221192 | tf_op jit(solution)/shard_map/ppermute | solution.py:257
  41.8 0.6 %collective-permute-start.9 = (f32[72,256]{1,0:T(8,128)S(1)}, f32[72,256]{1,0:T(8,128)S(1)}, u32[]{:S(2)}, u32[]{:S(2)}) collective-permute-start(f32[72,256]{1,0:T(8,128)S(1)} %shard_map.81.a), channel_id=1, source_target_pairs={{0,64},{32,96},{64,0},{96,32},{128,192},{160,224},{192,128},{224,1... | collective-permute-start | bytes 221192 | tf_op jit(solution)/shard_map/ppermute | solution.py:257
  42.4 1.0 %collective-permute-start.8 = (f32[72,256]{1,0:T(8,128)S(1)}, f32[72,256]{1,0:T(8,128)S(1)}, u32[]{:S(2)}, u32[]{:S(2)}) collective-permute-start(f32[72,256]{1,0:T(8,128)S(1)} %shard_map.81.a), channel_id=1, source_target_pairs={{0,32},{32,64},{64,96},{96,0},{128,160},{160,192},{192,224},{224,1... | collective-permute-start | bytes 221192 | tf_op jit(solution)/shard_map/ppermute | solution.py:257
  43.4 0.6 %collective-permute-done.10.d = f32[72,256]{1,0:T(8,128)S(1)} collective-permute-done((f32[72,256]{1,0:T(8,128)S(1)}, f32[72,256]{1,0:T(8,128)S(1)}, u32[]{:S(2)}, u32[]{:S(2)}) %collective-permute-start.10) | collective-permute-done | bytes 73760 | tf_op jit(solution)/shard_map/ppermute | solution.py:257
  44.0 3.7 %collective-permute-done.9.c = f32[72,256]{1,0:T(8,128)S(1)} collective-permute-done((f32[72,256]{1,0:T(8,128)S(1)}, f32[72,256]{1,0:T(8,128)S(1)}, u32[]{:S(2)}, u32[]{:S(2)}) %collective-permute-start.9) | collective-permute-done | bytes 73760 | tf_op jit(solution)/shard_map/ppermute | solution.py:257
  47.7 0.7 %collective-permute-done.8.b = f32[72,256]{1,0:T(8,128)S(1)} collective-permute-done((f32[72,256]{1,0:T(8,128)S(1)}, f32[72,256]{1,0:T(8,128)S(1)}, u32[]{:S(2)}, u32[]{:S(2)}) %collective-permute-start.8) | collective-permute-done | bytes 73760 | tf_op jit(solution)/shard_map/ppermute | solution.py:257
  48.5 5.8 %collective-permute-start.11 = (f32[72,256]{1,0:T(8,128)S(1)}, f32[72,256]{1,0:T(8,128)S(1)}, u32[]{:S(2)}, u32[]{:S(2)}) collective-permute-start(f32[72,256]{1,0:T(8,128)S(1)} %shard_map.82.mine), channel_id=1, source_target_pairs={{0,128},{32,160},{64,192},{96,224},{128,0},{160,32},{192,64},{224,... | collective-permute-start | bytes 221192 | tf_op jit(solution)/shard_map/ppermute | solution.py:259
  54.3 0.5 shard_map.83.side
  54.8 2.0 %collective-permute-done.11.other = f32[72,256]{1,0:T(8,128)S(1)} collective-permute-done((f32[72,256]{1,0:T(8,128)S(1)}, f32[72,256]{1,0:T(8,128)S(1)}, u32[]{:S(2)}, u32[]{:S(2)}) %collective-permute-start.11) | collective-permute-done | bytes 73760 | tf_op jit(solution)/shard_map/ppermute | solution.py:259
  56.8 1.0 %shard_map.84 = (f32[64,256]{1,0:T(8,128)}, f32[64,256]{1,0:T(8,128)}) custom-call(f32[72,256]{1,0:T(8,128)S(1)} %shard_map.82.mine, f32[72,256]{1,0:T(8,128)S(1)} %collective-permute-done.11.other, f32[64,256]{1,0:T(8,128)S(1)} %shard_map.83.side, f32[64,256]{1,0:T(8,128)S(1)} %get-tuple-element.30.window), custom_call_target="tpu_custom_call" | custom-call | tf_op jit(solution)/shard_map/pallas_call | solution.py:263
  (4 shorter events, 0.0 us)
Async XLA Ops:
  8.9 2.8 %collective-permute-start = (f32[1088,256]{1,0:T(8,128)S(1)}, f32[1088,256]{1,0:T(8,128)S(1)}, u32[]{:S(2)}, u32[]{:S(2)}) collective-permute-start(f32[1088,256]{1,0:T(8,128)S(1)} %get-tuple-element.20), channel_id=1, source_target_pairs={{0,1},{1,0},{2,3},{3,2},{4,5},{5,4},{6,7},{7,6},{8,9},{9,8},{10,11... | collective-permute-start | bytes 3342344 | tf_op jit(solution)/shard_map/ppermute | solution.py:247
  10.3 43.9 %copy-start = (s32[64,4]{0,1:T(4,128)S(1)}, s32[64,4]{0,1:T(4,128)}, u32[]{:S(2)}) copy-start(s32[64,4]{0,1:T(4,128)} %param.11) | copy-start | bytes 3076
  10.4 43.9 %copy-start.1 = (f32[64]{0:T(128)S(1)}, f32[64]{0:T(128)}, u32[]{:S(2)}) copy-start(f32[64]{0:T(128)} %param.10) | copy-start | bytes 772
  11.9 14.2 %collective-permute-start.1 = (f32[256,256]{1,0:T(8,128)S(1)}, f32[256,256]{1,0:T(8,128)S(1)}, u32[]{:S(2)}, u32[]{:S(2)}) collective-permute-start(f32[256,256]{1,0:T(8,128)S(1)} %get-tuple-element.22), channel_id=1, source_target_pairs={{0,2},{1,3},{2,4},{3,5},{4,6},{5,7},{6,0},{7,1},{8,10},{9,11},{10,... | collective-permute-start | bytes 786440 | tf_op jit(solution)/shard_map/ppermute | solution.py:251
  14.2 11.9 %collective-permute-start.2 = (f32[256,256]{1,0:T(8,128)S(1)}, f32[256,256]{1,0:T(8,128)S(1)}, u32[]{:S(2)}, u32[]{:S(2)}) collective-permute-start(f32[256,256]{1,0:T(8,128)S(1)} %get-tuple-element.23), channel_id=1, source_target_pairs={{0,4},{1,5},{2,6},{3,7},{4,0},{5,1},{6,2},{7,3},{8,12},{9,13},{10,... | collective-permute-start | bytes 786440 | tf_op jit(solution)/shard_map/ppermute | solution.py:250
  14.9 15.2 %collective-permute-start.3 = (f32[256,256]{1,0:T(8,128)S(1)}, f32[256,256]{1,0:T(8,128)S(1)}, u32[]{:S(2)}, u32[]{:S(2)}) collective-permute-start(f32[256,256]{1,0:T(8,128)S(1)} %get-tuple-element.24), channel_id=1, source_target_pairs={{0,6},{1,7},{2,0},{3,1},{4,2},{5,3},{6,4},{7,5},{8,14},{9,15},{10,... | collective-permute-start | bytes 786440 | tf_op jit(solution)/shard_map/ppermute | solution.py:252
  15.1 19.5 %collective-permute-start.7 = (f32[64,256]{1,0:T(8,128)S(1)}, f32[64,256]{1,0:T(8,128)S(1)}, u32[]{:S(2)}, u32[]{:S(2)}) collective-permute-start(f32[64,256]{1,0:T(8,128)S(1)} %get-tuple-element.30.window), channel_id=1, source_target_pairs={{0,31},{1,2},{2,1},{3,4},{4,3},{5,6},{6,5},{7,8},{8,7},{9,10},{10,... | collective-permute-start | bytes 196616 | tf_op jit(solution)/shard_map/ppermute | solution.py:253
  30.1 7.0 %collective-permute-start.4 = (f32[64,256]{1,0:T(8,128)S(1)}, f32[64,256]{1,0:T(8,128)S(1)}, u32[]{:S(2)}, u32[]{:S(2)}) collective-permute-start(f32[64,256]{1,0:T(8,128)S(1)} %get-tuple-element.26), channel_id=1, source_target_pairs={{0,8},{1,9},{2,10},{3,11},{4,12},{5,13},{6,14},{7,15},{8,16},{9,17... | collective-permute-start | bytes 196616 | tf_op jit(solution)/shard_map/ppermute | solution.py:255
  30.4 8.5 %collective-permute-start.5 = (f32[64,256]{1,0:T(8,128)S(1)}, f32[64,256]{1,0:T(8,128)S(1)}, u32[]{:S(2)}, u32[]{:S(2)}) collective-permute-start(f32[64,256]{1,0:T(8,128)S(1)} %get-tuple-element.27), channel_id=1, source_target_pairs={{0,16},{1,17},{2,18},{3,19},{4,20},{5,21},{6,22},{7,23},{8,24},{9,... | collective-permute-start | bytes 196616 | tf_op jit(solution)/shard_map/ppermute | solution.py:255
  33.7 5.3 %collective-permute-start.6 = (f32[64,256]{1,0:T(8,128)S(1)}, f32[64,256]{1,0:T(8,128)S(1)}, u32[]{:S(2)}, u32[]{:S(2)}) collective-permute-start(f32[64,256]{1,0:T(8,128)S(1)} %get-tuple-element.28), channel_id=1, source_target_pairs={{0,24},{1,25},{2,26},{3,27},{4,28},{5,29},{6,30},{7,31},{8,0},{9,1... | collective-permute-start | bytes 196616 | tf_op jit(solution)/shard_map/ppermute | solution.py:255
  38.9 5.0 %collective-permute-start.10 = (f32[72,256]{1,0:T(8,128)S(1)}, f32[72,256]{1,0:T(8,128)S(1)}, u32[]{:S(2)}, u32[]{:S(2)}) collective-permute-start(f32[72,256]{1,0:T(8,128)S(1)} %shard_map.81.a), channel_id=1, source_target_pairs={{0,96},{32,0},{64,32},{96,64},{128,224},{160,128},{192,160},{224,1... | collective-permute-start | bytes 221192 | tf_op jit(solution)/shard_map/ppermute | solution.py:257
  41.8 5.9 %collective-permute-start.9 = (f32[72,256]{1,0:T(8,128)S(1)}, f32[72,256]{1,0:T(8,128)S(1)}, u32[]{:S(2)}, u32[]{:S(2)}) collective-permute-start(f32[72,256]{1,0:T(8,128)S(1)} %shard_map.81.a), channel_id=1, source_target_pairs={{0,64},{32,96},{64,0},{96,32},{128,192},{160,224},{192,128},{224,1... | collective-permute-start | bytes 221192 | tf_op jit(solution)/shard_map/ppermute | solution.py:257
  42.4 6.0 %collective-permute-start.8 = (f32[72,256]{1,0:T(8,128)S(1)}, f32[72,256]{1,0:T(8,128)S(1)}, u32[]{:S(2)}, u32[]{:S(2)}) collective-permute-start(f32[72,256]{1,0:T(8,128)S(1)} %shard_map.81.a), channel_id=1, source_target_pairs={{0,32},{32,64},{64,96},{96,0},{128,160},{160,192},{192,224},{224,1... | collective-permute-start | bytes 221192 | tf_op jit(solution)/shard_map/ppermute | solution.py:257
  48.5 8.3 %collective-permute-start.11 = (f32[72,256]{1,0:T(8,128)S(1)}, f32[72,256]{1,0:T(8,128)S(1)}, u32[]{:S(2)}, u32[]{:S(2)}) collective-permute-start(f32[72,256]{1,0:T(8,128)S(1)} %shard_map.82.mine), channel_id=1, source_target_pairs={{0,128},{32,160},{64,192},{96,224},{128,0},{160,32},{192,64},{224,... | collective-permute-start | bytes 221192 | tf_op jit(solution)/shard_map/ppermute | solution.py:259

commit v3 on v2

--- a/solution.py
+++ b/solution.py
@@ -11,6 +11,11 @@
 NX, NZ, NY = 4, 4, 4
 F32 = jnp.float32
 VMEM = pltpu.VMEM
+PART = 2 * NX * ROWS
+FIRST, SECOND = (2, 1), (3, 0)
+PRODUCT_FLOPS = 2 * PART * 2048 * 16
+PAUSE_FLOPS = 4 * 10**9
+POWER_SCALE = 6.0 * 15.0 / math.pi**4 / 300.0**4
 LOG2E = 1.0 / math.log(2.0)
 PARAMS = dict(vmem_limit_bytes=24 * 2**20)
 
@@ -28,30 +33,37 @@
     return row // (2 * NX), (row // 2) % NX, row % 2
 
 
-def power_chunk(t, emis, a_lo, a_hi):
+def edge_terms(a):
+    return a * -LOG2E, a, a * a * 0.5, a * a * a * (1.0 / 6.0)
+
+
+def power_chunk(t, emis, lo, hi):
     r = pl.reciprocal(t, approx=True)
     r = r * (2.0 - t * r)
-    lo = a_lo * r
-    hi = a_hi * r
-    cum_lo = jnp.exp2(lo * -LOG2E) * (((lo + 3.0) * lo + 6.0) * lo + 6.0)
-    cum_hi = jnp.exp2(hi * -LOG2E) * (((hi + 3.0) * hi + 6.0) * hi + 6.0)
-    square = t * t
-    return (cum_hi - cum_lo) * (square * square) * emis
+    parts = [
+        jnp.exp2(scale * r) * (((a + t) * t + half_square) * t + sixth_cube)
+        for scale, a, half_square, sixth_cube in (lo, hi)
+    ]
+    return (parts[1] - parts[0]) * (t * emis)
 
 
 def dot_nt(a, b):
     return lax.dot_general(a, b, (((1,), (1,)), ((), ())), preferred_element_type=F32)
 
 
-def gather_rows(g_hbm, gbuf, sems, x, core):
+def fetch_rows(g_hbm, buf, sems, z, core, offsets):
     return [
-        pltpu.make_async_copy(g_hbm.at[:, (x + d) % NX, core], gbuf.at[d], sems.at[d])
-        for d in range(NX)
-    ]
+        pltpu.make_async_copy(g_hbm.at[(z + d) % NZ, :, core], buf.at[i], sems.at[i])
+        for i, d in enumerate(offsets)
+    ]
+
+
+def flat(g):
+    return g[...].reshape(g.shape[0] * NX * ROWS, g.shape[3])
 
 
 def first_kernel(
-    edges_hbm, emis_hbm, t_hbm, g_hbm, u, p, gown, win, par, tbuf, gbuf, scaled, edges, tsem, gsem, osem, ssem
+    edges_hbm, emis_hbm, t_hbm, g_hbm, u, p, g1, g2, g3, win, par, tbuf, gbuf, scaled, edges, tsem, gsem, ssem
 ):
     z, x, core = place()
     part = tbuf.shape[0] // 4
@@ -65,58 +77,81 @@
         )
         for i in range(4)
     ]
-    gcopies = gather_rows(g_hbm, gbuf, gsem, x, 1 - core)
-    ocopies = gather_rows(g_hbm, gown, osem, x, core)
-    for c in small + tcopies + gcopies + ocopies:
+    gcopies = [
+        fetch_rows(g_hbm, gbuf, gsem.at[0], z, 1 - core, FIRST),
+        fetch_rows(g_hbm, g1, gsem.at[1], z, 1 - core, SECOND),
+        fetch_rows(g_hbm, g2, gsem.at[2], z, core, FIRST),
+        fetch_rows(g_hbm, g3, gsem.at[3], z, core, SECOND),
+    ]
+    for c in small + tcopies:
         c.start()
     for c in small:
         c.wait()
     a_lo = 14388000.0 / jnp.full((1, 512), edges[0, 0].astype(F32))
     a_hi = 14388000.0 / jnp.full((1, 512), edges[0, 1].astype(F32))
-    scaled[...] = scaled[...] * (15.0 / math.pi**4 / 300.0**4)
+    scaled[...] = scaled[...] * POWER_SCALE
     lane = lax.broadcasted_iota(jnp.int32, (8, 256), 1)
     line = jnp.broadcast_to(scaled[:, :256], (8, 256))
     line = jnp.where(lane == ROWS, a_lo[:, :256], line)
     par[...] = jnp.where(lane == ROWS + 1, a_hi[:, :256], line)
+    lo, hi = edge_terms(a_lo), edge_terms(a_hi)
     for i in range(4):
         tcopies[i].wait()
+        if i == 1:
+            for c in gcopies[0] + gcopies[1] + gcopies[2] + gcopies[3]:
+                c.start()
 
         @pl.loop(0, part // 16)
         def _(j):
             rows = pl.ds(i * part + j * 16, 16)
             for c in range(4):
                 cols = pl.ds(c * 512, 512)
-                p[rows, cols] = power_chunk(
-                    tbuf[rows, cols], scaled[:, cols], a_lo, a_hi
-                ).astype(jnp.bfloat16)
-
-    half = NZ * ROWS
+                p[rows, cols] = power_chunk(tbuf[rows, cols], scaled[:, cols], lo, hi).astype(
+                    jnp.bfloat16
+                )
+
     w = tbuf[:, :128].T[:ROWS]
     win[...] = w
-    u[NX * half :] = w
+    u[PART:] = w
+    for c in gcopies[0]:
+        c.wait()
+    u[:PART] = dot_nt(flat(gbuf), p[...])
+    for c in gcopies[1] + gcopies[2] + gcopies[3]:
+        c.wait()
+
+
+def product_kernel(p, g, *refs):
+    t = refs[-1]
+    t[...] = dot_nt(flat(g), p[...])
+
+
+def spread(value, outs):
+    z, x, core = place()
     for d in range(NX):
-        gcopies[d].wait()
-        u[d * half : (d + 1) * half] = dot_nt(gbuf[d].reshape(half, gbuf.shape[3]), p[...])
-    for c in ocopies:
-        c.wait()
-
-
-def second_kernel(p, g, t):
-    for d in range(NX):
-        t[d] = dot_nt(g[d].reshape(NZ * ROWS, g.shape[3]), p[...])
+        for i in range(2):
+            rows = pl.ds(pl.multiple_of((i * NX + (x + d) % NX) * ROWS, ROWS), ROWS)
+            outs[d][i * ROWS : (i + 1) * ROWS] = value(rows)
 
 
 def add_kernel(t, u, *outs):
-    half = NZ * ROWS
-    for d in range(NX):
-        outs[d][...] = t[d] + u[d * half : (d + 1) * half]
-    outs[NX][...] = u[NX * half :]
+    spread(lambda rows: t[rows] + u[rows], outs)
+    outs[NX][...] = u[PART:]
+
+
+def product_add_kernel(p, g, u, s, *refs):
+    outs, t = refs[:-1], refs[-1]
+    t[...] = dot_nt(flat(g), p[...])
+    spread(lambda rows: t[rows] + u[rows], outs)
+
+
+def x_sum_carry_kernel(a, b, c, d, win, *outs):
+    x_sum_kernel(a, b, c, d, *outs)
+    outs[2][...] = win[...]
 
 
 def x_sum_kernel(a, b, c, d, *outs):
-    z, x, core = place()
-    for i in range(NZ):
-        rows = pl.ds(pl.multiple_of(((z + i) % NZ) * ROWS, ROWS), ROWS)
+    for i in range(2):
+        rows = pl.ds(i * ROWS, ROWS)
         outs[i][...] = (a[rows] + b[rows]) + (c[rows] + d[rows])
 
 
@@ -137,7 +172,10 @@
     columns = jnp.broadcast_to(par, (8, par.shape[1]))[:, :128].T
     for i in range(NY):
         part = power_chunk(
-            win, columns[:ROWS, i : i + 1], par[i, ROWS], par[i, ROWS + 1]
+            win,
+            columns[:ROWS, i : i + 1],
+            edge_terms(par[i, ROWS]),
+            edge_terms(par[i, ROWS + 1]),
         )
         total += part.astype(jnp.bfloat16).astype(F32)
     return total
@@ -214,46 +252,47 @@
     dma = pltpu.SemaphoreType.DMA
     block = sds(ROWS, orbits)
     message = sds(ROWS + 8, orbits)
-    cost = pl.CostEstimate(
-        flops=2 * NX * half * panels * orbits, bytes_accessed=8 * 2**20, transcendentals=0
-    )
+    rows = sds(2, NX, ROWS, panels, dtype=bf)
+    pair = sds(2 * ROWS, orbits)
+    cost = pl.CostEstimate(flops=PRODUCT_FLOPS, bytes_accessed=0, transcendentals=0)
+    pause = pl.CostEstimate(flops=PAUSE_FLOPS, bytes_accessed=0, transcendentals=0)
     far = [
         pltpu.with_memory_space_constraint(a, pltpu.HBM)
         for a in (band_edges, emissivity, temps, g)
     ]
-    u, p, gown, win, par = call(
+    u_a, p, g1, g2, g3, win, par = call(
         first_kernel,
         4,
-        [
-            sds(NX * half + ROWS, orbits),
-            sds(orbits, panels, dtype=bf),
-            sds(NX, NZ, ROWS, panels, dtype=bf),
-            block,
-            sds(8, orbits),
-        ],
+        [sds(PART + ROWS, orbits), sds(orbits, panels, dtype=bf), *[rows] * 3, block, sds(8, orbits)],
         in_specs=[hbm] * 4,
         scratch=[
             VMEM((orbits, panels), F32),
-            VMEM((NX, NZ, ROWS, panels), bf),
+            VMEM(rows.shape, bf),
             VMEM((1, panels), F32),
             pltpu.SMEM((1, 2), jnp.int32),
             dma((4,)),
-            dma((NX,)),
-            dma((NX,)),
+            dma((4, 2)),
             dma((2,)),
         ],
         cost=cost,
     )(*far)
-    u_in = lax.ppermute(u, "row", CORE)
-    t = call(second_kernel, 2, sds(NX, half, orbits), cost=cost)(p, gown)
-    *s, swapped = call(add_kernel, 2, [sds(half, orbits)] * NX + [block])(t, u_in)
-    x2 = lax.ppermute(s[2], "row", XS[2])
-    x1 = lax.ppermute(s[1], "row", XS[1])
-    x3 = lax.ppermute(s[3], "row", XS[3])
+    u_a = lax.ppermute(u_a, "row", CORE)
+    t_a = call(product_kernel, 2, sds(PART, orbits), cost=cost)(p, g2)
+    u_b = call(product_kernel, 3, sds(PART, orbits), cost=cost)(p, g1, t_a)
+    u_b = lax.ppermute(u_b, "row", CORE)
+    *s_a, swapped = call(add_kernel, 2, [pair] * NX + [block])(t_a, u_a)
+    x_a = [lax.ppermute(s_a[d], "row", XS[d]) for d in (2, 1, 3)]
+    s_b = call(product_add_kernel, 4, [pair] * NX, scratch=[VMEM((PART, orbits), F32)], cost=cost)(
+        p, g3, u_b, s_a[0]
+    )
+    x_b = [lax.ppermute(s_b[d], "row", XS[d]) for d in (2, 1, 3)]
+    z2, z1, win = call(x_sum_carry_kernel, 5, [block] * 3)(s_a[0], *x_a, win)
+    z2 = lax.ppermute(z2, "row", ZS[2])
+    z1 = lax.ppermute(z1, "row", ZS[1])
     cross = lax.ppermute(win, "row", CROSS)
-    zs = call(x_sum_kernel, 4, [block] * NZ)(s[0], x1, x2, x3)
-    z_in = [lax.ppermute(zs[d], "row", ZS[d]) for d in (1, 2, 3)]
-    zsum = call(z_sum_kernel, 6, message)(zs[0], *z_in, par, cross)
+    z3, z0 = call(x_sum_kernel, 4, [block] * 2, cost=pause)(s_b[0], *x_b)
+    z3 = lax.ppermute(z3, "row", ZS[3])
+    zsum = call(z_sum_kernel, 6, message)(z0, z1, z2, z3, par, cross)
     y_in = [lax.ppermute(zsum, "band", YS[d]) for d in (1, 2, 3)]
     mine = call(y_sum_kernel, 4, message)(zsum, *y_in)
     other = lax.ppermute(mine, "band", HI)

time: 58.7 us -> 51.2 us (0.87); the launches traced: 57.8 us -> 51.1 us
  waiting for transfers between devices: 26.2 us -> 13.8 us
  starting transfers between devices: 19.6 us -> 27.4 us
  Pallas kernels: 11.3 us -> 9.08 us
    ppermute x7 -> x11, waiting for transfers between devices: 19.2 us -> 5.63 us  [the longest x3 4.11 us: body(): x_a = [lax.ppermute(s_a[d], 'row', XS[d]) for d in (2, 1, 3)]]
    ppermute x7 -> x11, starting transfers between devices: 7.88 us -> 16.2 us  [the longest x3 4.38 us: body(): x_b = [lax.ppermute(s_b[d], 'row', XS[d]) for d in (2, 1, 3)]]
    pallas_call x5 -> x8, Pallas kernels: 9.78 us -> 7.59 us  [the longest x1 5.16 us: body(): call(first_kernel, 4, [sds(PART + ROWS, orbits), sds(orbits, panels, dtyp...]
    ppermute x1, starting transfers between devices: 1.43 us -> 0.01 us  [body(): cross = lax.ppermute(win, 'row', CROSS)]
    ppermute x1, waiting for transfers between devices: 0.01 us -> 1.31 us  [body(): cross = lax.ppermute(win, 'row', CROSS)]
    ppermute x1, starting transfers between devices: 5.8 us -> 6.55 us  [body(): other = lax.ppermute(mine, 'band', HI)]
  transfers between devices with their start and end apart: 12 -> 16, of which waited for: 9 -> 9; matrix products, arithmetic and copies ran while one was open for 0% -> 0% of each run, Pallas kernels for 3% -> 6%
where the time goes in v3:
time: 51.2 us; the launch traced here: 51.1 us
  starting transfers between devices  27.4 us (54%)
  waiting for transfers between devices  13.8 us (27%)
  Pallas kernels  9.08 us (18%)
  between operations  0.74 us (1%)
    ppermute x1, starting transfers between devices, body(): other = lax.ppermute(mine, 'band', HI)  6.55 us
    pallas_call x1, Pallas kernels, body(): call(first_kernel, 4, [sds(PART + ROWS, orbits), sds(orbits, panels, dtyp...  5.16 us
    ppermute x3, waiting for transfers between devices, body(): y_in = [lax.ppermute(zsum, 'band', YS[d]) for d in (1, 2, 3)]  5.04 us
    ppermute x3, starting transfers between devices, body(): y_in = [lax.ppermute(zsum, 'band', YS[d]) for d in (1, 2, 3)]  4.69 us
    ppermute x3, starting transfers between devices, body(): x_b = [lax.ppermute(s_b[d], 'row', XS[d]) for d in (2, 1, 3)]  4.38 us
    ppermute x3, waiting for transfers between devices, body(): x_a = [lax.ppermute(s_a[d], 'row', XS[d]) for d in (2, 1, 3)]  4.11 us
    ppermute x3, starting transfers between devices, body(): x_a = [lax.ppermute(s_a[d], 'row', XS[d]) for d in (2, 1, 3)]  3.59 us
    ppermute x1, starting transfers between devices, body(): z2 = lax.ppermute(z2, 'row', ZS[2])  3.28 us
  transfers between devices with their start and end apart: 16, of which 9 were waited for; matrix products, arithmetic and copies ran while one was open for 0% of the time, Pallas kernels for 6%

profile of v3, /device:TPU:6, one launch (start us, length us, event | category | flops | bytes accessed | tf_op | source)
XLA Modules:
  0.0 51.1 jit_solution(7274265761079304690)
XLA Ops:
  0.6 5.2 %shard_map.77 = (f32[576,256]{1,0:T(8,128)S(1)}, bf16[256,2048]{1,0:T(8,128)(2,1)S(1)}, bf16[2,4,64,2048]{3,2,1,0:T(8,128)(2,1)S(1)}, bf16[2,4,64,2048]{3,2,1,0:...) custom-call(s32[1,2]{1,0:T(1,128)} %edges_hbm.1, ...), custom_call_target="tpu_custom_call" | custom-call | flops 33554432 | tf_op jit(solution)/shard_map/pallas_call | solution.py:263
  5.8 0.1 collective-permute-start.1
  5.9 0.7 %shard_map.78.refs_0_.t = f32[512,256]{1,0:T(8,128)S(1)} custom-call(bf16[256,2048]{1,0:T(8,128)(2,1)S(1)} %get-tuple-element.25.p, bf16[2,4,64,2048]{3,2,1,0:T(8,128)(2,1)S(1)} %get-tuple-element.28.g), custom_call_target="tpu_custom_call" | custom-call | flops 33554432 | tf_op jit(solution)/shard_map/pallas_call | solution.py:280
  6.6 0.7 %shard_map.79 = f32[512,256]{1,0:T(8,128)S(1)} custom-call(bf16[256,2048]{1,0:T(8,128)(2,1)S(1)} %get-tuple-element.25.p, bf16[2,4,64,2048]{3,2,1,0:T(8,128)(2,1)S(1)} %get-tuple-element.27.g, f32[512,256]{1,0:T(8,128)S(1)} %shard_map.78.refs_0_.t), custom_call_target="tpu_custom_call" | custom-call | flops 33554432 | tf_op jit(solution)/shard_map/pallas_call | solution.py:281
  7.4 0.6 %collective-permute-start = (f32[512,256]{1,0:T(8,128)S(1)}, f32[512,256]{1,0:T(8,128)S(1)}, u32[]{:S(2)}, u32[]{:S(2)}) collective-permute-start(f32[512,256]{1,0:T(8,128)S(1)} %shard_map.79), channel_id=1, source_target_pairs={{0,1},{1,0},{2,3},{3,2},{4,5},{5,4},{6,7},{7,6},{8,9},{9,8},{10,11... | collective-permute-start | bytes 1572872 | tf_op jit(solution)/shard_map/ppermute | solution.py:282
  8.0 0.1 shard_map.80
  8.1 1.5 %collective-permute-start.5 = (f32[128,256]{1,0:T(8,128)S(1)}, f32[128,256]{1,0:T(8,128)S(1)}, u32[]{:S(2)}, u32[]{:S(2)}) collective-permute-start(f32[128,256]{1,0:T(8,128)S(1)} %get-tuple-element.36), channel_id=1, source_target_pairs={{0,4},{1,5},{2,6},{3,7},{4,0},{5,1},{6,2},{7,3},{8,12},{9,13},{10,... | collective-permute-start | bytes 393224 | tf_op jit(solution)/shard_map/ppermute | solution.py:284
  9.6 2.1 %collective-permute-start.6 = (f32[128,256]{1,0:T(8,128)S(1)}, f32[128,256]{1,0:T(8,128)S(1)}, u32[]{:S(2)}, u32[]{:S(2)}) collective-permute-start(f32[128,256]{1,0:T(8,128)S(1)} %get-tuple-element.37), channel_id=1, source_target_pairs={{0,2},{1,3},{2,4},{3,5},{4,6},{5,7},{6,0},{7,1},{8,10},{9,11},{10,... | collective-permute-start | bytes 393224 | tf_op jit(solution)/shard_map/ppermute | solution.py:284
  11.7 0.8 %shard_map.81 = (f32[128,256]{1,0:T(8,128)S(1)}, f32[128,256]{1,0:T(8,128)S(1)}, f32[128,256]{1,0:T(8,128)S(1)}, f32[128,256]{1,0:T(8,128)S(1)}) custom-call(bf16[256,2048]{1,0:T(8,128)(2,1)S(1)} %get-tuple-element.25.p, bf16[2,4,64,2048]{3,2,1,0:T(8,128)(2,1)S(1)} %get-tuple-element.26.g, f32[512,256]{1,0:T(8,128)S(1)} %collective-permute-done.u, ...), custom_call_target="tpu_custom_call" | custom-call | flops 33554432 | tf_op jit(solution)/shard_map/pallas_call | solution.py:285
  12.5 2.1 %collective-permute-start.2 = (f32[128,256]{1,0:T(8,128)S(1)}, f32[128,256]{1,0:T(8,128)S(1)}, u32[]{:S(2)}, u32[]{:S(2)}) collective-permute-start(f32[128,256]{1,0:T(8,128)S(1)} %get-tuple-element.32), channel_id=1, source_target_pairs={{0,4},{1,5},{2,6},{3,7},{4,0},{5,1},{6,2},{7,3},{8,12},{9,13},{10,... | collective-permute-start | bytes 393224 | tf_op jit(solution)/shard_map/ppermute | solution.py:288
  14.6 2.2 %collective-permute-start.3 = (f32[128,256]{1,0:T(8,128)S(1)}, f32[128,256]{1,0:T(8,128)S(1)}, u32[]{:S(2)}, u32[]{:S(2)}) collective-permute-start(f32[128,256]{1,0:T(8,128)S(1)} %get-tuple-element.33), channel_id=1, source_target_pairs={{0,2},{1,3},{2,4},{3,5},{4,6},{5,7},{6,0},{7,1},{8,10},{9,11},{10,... | collective-permute-start | bytes 393224 | tf_op jit(solution)/shard_map/ppermute | solution.py:288
  16.8 0.0 collective-permute-start.4
  16.9 1.5 %collective-permute-done.6.c = f32[128,256]{1,0:T(8,128)S(1)} collective-permute-done((f32[128,256]{1,0:T(8,128)S(1)}, f32[128,256]{1,0:T(8,128)S(1)}, u32[]{:S(2)}, u32[]{:S(2)}) %collective-permute-start.6) | collective-permute-done | bytes 131104 | tf_op jit(solution)/shard_map/ppermute | solution.py:284
  18.4 2.6 %collective-permute-done.7.d = f32[128,256]{1,0:T(8,128)S(1)} collective-permute-done((f32[128,256]{1,0:T(8,128)S(1)}, f32[128,256]{1,0:T(8,128)S(1)}, u32[]{:S(2)}, u32[]{:S(2)}) %collective-permute-start.7) | collective-permute-done | bytes 131104 | tf_op jit(solution)/shard_map/ppermute | solution.py:284
  21.0 2.4 %collective-permute-start.8 = (f32[64,256]{1,0:T(8,128)S(1)}, f32[64,256]{1,0:T(8,128)S(1)}, u32[]{:S(2)}, u32[]{:S(2)}) collective-permute-start(f32[64,256]{1,0:T(8,128)S(1)} %get-tuple-element.40), channel_id=1, source_target_pairs={{0,8},{1,9},{2,10},{3,11},{4,12},{5,13},{6,14},{7,15},{8,16},{9,17... | collective-permute-start | bytes 196616 | tf_op jit(solution)/shard_map/ppermute | solution.py:291
  23.4 3.3 %collective-permute-start.9 = (f32[64,256]{1,0:T(8,128)S(1)}, f32[64,256]{1,0:T(8,128)S(1)}, u32[]{:S(2)}, u32[]{:S(2)}) collective-permute-start(f32[64,256]{1,0:T(8,128)S(1)} %get-tuple-element.41), channel_id=1, source_target_pairs={{0,16},{1,17},{2,18},{3,19},{4,20},{5,21},{6,22},{7,23},{8,24},{9,... | collective-permute-start | bytes 196616 | tf_op jit(solution)/shard_map/ppermute | solution.py:290
  26.7 0.0 copy-start
  26.7 0.0 copy-start.1
  26.8 1.9 %collective-permute-start.10 = (f32[64,256]{1,0:T(8,128)S(1)}, f32[64,256]{1,0:T(8,128)S(1)}, u32[]{:S(2)}, u32[]{:S(2)}) collective-permute-start(f32[64,256]{1,0:T(8,128)S(1)} %get-tuple-element.42), channel_id=1, source_target_pairs={{0,24},{1,25},{2,26},{3,27},{4,28},{5,29},{6,30},{7,31},{8,0},{9,1... | collective-permute-start | bytes 196616 | tf_op jit(solution)/shard_map/ppermute | solution.py:294
  28.6 0.4 collective-permute-done.9.c
  29.1 1.3 %collective-permute-done.11.cross = f32[64,256]{1,0:T(8,128)S(1)} collective-permute-done((f32[64,256]{1,0:T(8,128)S(1)}, f32[64,256]{1,0:T(8,128)S(1)}, u32[]{:S(2)}, u32[]{:S(2)}) %collective-permute-start.11) | collective-permute-done | bytes 65568 | tf_op jit(solution)/shard_map/ppermute | solution.py:292
  30.4 1.1 %collective-permute-done.10.d = f32[64,256]{1,0:T(8,128)S(1)} collective-permute-done((f32[64,256]{1,0:T(8,128)S(1)}, f32[64,256]{1,0:T(8,128)S(1)}, u32[]{:S(2)}, u32[]{:S(2)}) %collective-permute-start.10) | collective-permute-done | bytes 65568 | tf_op jit(solution)/shard_map/ppermute | solution.py:294
  31.5 3.1 %collective-permute-start.14 = (f32[72,256]{1,0:T(8,128)S(1)}, f32[72,256]{1,0:T(8,128)S(1)}, u32[]{:S(2)}, u32[]{:S(2)}) collective-permute-start(f32[72,256]{1,0:T(8,128)S(1)} %shard_map.84.a), channel_id=1, source_target_pairs={{0,96},{32,0},{64,32},{96,64},{128,224},{160,128},{192,160},{224,1... | collective-permute-start | bytes 221192 | tf_op jit(solution)/shard_map/ppermute | solution.py:296
  34.6 0.6 %collective-permute-start.13 = (f32[72,256]{1,0:T(8,128)S(1)}, f32[72,256]{1,0:T(8,128)S(1)}, u32[]{:S(2)}, u32[]{:S(2)}) collective-permute-start(f32[72,256]{1,0:T(8,128)S(1)} %shard_map.84.a), channel_id=1, source_target_pairs={{0,64},{32,96},{64,0},{96,32},{128,192},{160,224},{192,128},{224,1... | collective-permute-start | bytes 221192 | tf_op jit(solution)/shard_map/ppermute | solution.py:296
  35.2 1.0 %collective-permute-start.12 = (f32[72,256]{1,0:T(8,128)S(1)}, f32[72,256]{1,0:T(8,128)S(1)}, u32[]{:S(2)}, u32[]{:S(2)}) collective-permute-start(f32[72,256]{1,0:T(8,128)S(1)} %shard_map.84.a), channel_id=1, source_target_pairs={{0,32},{32,64},{64,96},{96,0},{128,160},{160,192},{192,224},{224,1... | collective-permute-start | bytes 221192 | tf_op jit(solution)/shard_map/ppermute | solution.py:296
  36.2 0.4 collective-permute-done.14.d
  36.5 3.9 %collective-permute-done.13.c = f32[72,256]{1,0:T(8,128)S(1)} collective-permute-done((f32[72,256]{1,0:T(8,128)S(1)}, f32[72,256]{1,0:T(8,128)S(1)}, u32[]{:S(2)}, u32[]{:S(2)}) %collective-permute-start.13) | collective-permute-done | bytes 73760 | tf_op jit(solution)/shard_map/ppermute | solution.py:296
  40.5 0.7 %collective-permute-done.12.b = f32[72,256]{1,0:T(8,128)S(1)} collective-permute-done((f32[72,256]{1,0:T(8,128)S(1)}, f32[72,256]{1,0:T(8,128)S(1)}, u32[]{:S(2)}, u32[]{:S(2)}) %collective-permute-start.12) | collective-permute-done | bytes 73760 | tf_op jit(solution)/shard_map/ppermute | solution.py:296
  41.2 6.5 %collective-permute-start.15 = (f32[72,256]{1,0:T(8,128)S(1)}, f32[72,256]{1,0:T(8,128)S(1)}, u32[]{:S(2)}, u32[]{:S(2)}) collective-permute-start(f32[72,256]{1,0:T(8,128)S(1)} %shard_map.85.mine), channel_id=1, source_target_pairs={{0,128},{32,160},{64,192},{96,224},{128,0},{160,32},{192,64},{224,... | collective-permute-start | bytes 221192 | tf_op jit(solution)/shard_map/ppermute | solution.py:298
  47.8 0.5 shard_map.86.side
  48.3 1.8 %collective-permute-done.15.other = f32[72,256]{1,0:T(8,128)S(1)} collective-permute-done((f32[72,256]{1,0:T(8,128)S(1)}, f32[72,256]{1,0:T(8,128)S(1)}, u32[]{:S(2)}, u32[]{:S(2)}) %collective-permute-start.15) | collective-permute-done | bytes 73760 | tf_op jit(solution)/shard_map/ppermute | solution.py:298
  50.1 1.0 %shard_map.87 = (f32[64,256]{1,0:T(8,128)}, f32[64,256]{1,0:T(8,128)}) custom-call(f32[72,256]{1,0:T(8,128)S(1)} %shard_map.85.mine, f32[72,256]{1,0:T(8,128)S(1)} %collective-permute-done.15.other, f32[64,256]{1,0:T(8,128)S(1)} %shard_map.86.side, f32[64,256]{1,0:T(8,128)S(1)} %get-tuple-element.44.window), custom_call_target="tpu_custom_call" | custom-call | tf_op jit(solution)/shard_map/pallas_call | solution.py:302
  (15 shorter events, 0.1 us)
Async XLA Ops:
  5.8 2.2 %collective-permute-start.1 = (f32[576,256]{1,0:T(8,128)S(1)}, f32[576,256]{1,0:T(8,128)S(1)}, u32[]{:S(2)}, u32[]{:S(2)}) collective-permute-start(f32[576,256]{1,0:T(8,128)S(1)} %get-tuple-element.29), channel_id=1, source_target_pairs={{0,1},{1,0},{2,3},{3,2},{4,5},{5,4},{6,7},{7,6},{8,9},{9,8},{10,11... | collective-permute-start | bytes 1769480 | tf_op jit(solution)/shard_map/ppermute | solution.py:279
  7.4 4.3 %collective-permute-start = (f32[512,256]{1,0:T(8,128)S(1)}, f32[512,256]{1,0:T(8,128)S(1)}, u32[]{:S(2)}, u32[]{:S(2)}) collective-permute-start(f32[512,256]{1,0:T(8,128)S(1)} %shard_map.79), channel_id=1, source_target_pairs={{0,1},{1,0},{2,3},{3,2},{4,5},{5,4},{6,7},{7,6},{8,9},{9,8},{10,11... | collective-permute-start | bytes 1572872 | tf_op jit(solution)/shard_map/ppermute | solution.py:282
  8.1 8.7 %collective-permute-start.5 = (f32[128,256]{1,0:T(8,128)S(1)}, f32[128,256]{1,0:T(8,128)S(1)}, u32[]{:S(2)}, u32[]{:S(2)}) collective-permute-start(f32[128,256]{1,0:T(8,128)S(1)} %get-tuple-element.36), channel_id=1, source_target_pairs={{0,4},{1,5},{2,6},{3,7},{4,0},{5,1},{6,2},{7,3},{8,12},{9,13},{10,... | collective-permute-start | bytes 393224 | tf_op jit(solution)/shard_map/ppermute | solution.py:284
  9.6 8.8 %collective-permute-start.6 = (f32[128,256]{1,0:T(8,128)S(1)}, f32[128,256]{1,0:T(8,128)S(1)}, u32[]{:S(2)}, u32[]{:S(2)}) collective-permute-start(f32[128,256]{1,0:T(8,128)S(1)} %get-tuple-element.37), channel_id=1, source_target_pairs={{0,2},{1,3},{2,4},{3,5},{4,6},{5,7},{6,0},{7,1},{8,10},{9,11},{10,... | collective-permute-start | bytes 393224 | tf_op jit(solution)/shard_map/ppermute | solution.py:284
  11.7 9.3 %collective-permute-start.7 = (f32[128,256]{1,0:T(8,128)S(1)}, f32[128,256]{1,0:T(8,128)S(1)}, u32[]{:S(2)}, u32[]{:S(2)}) collective-permute-start(f32[128,256]{1,0:T(8,128)S(1)} %get-tuple-element.38), channel_id=1, source_target_pairs={{0,6},{1,7},{2,0},{3,1},{4,2},{5,3},{6,4},{7,5},{8,14},{9,15},{10,... | collective-permute-start | bytes 393224 | tf_op jit(solution)/shard_map/ppermute | solution.py:284
  12.5 14.2 %collective-permute-start.2 = (f32[128,256]{1,0:T(8,128)S(1)}, f32[128,256]{1,0:T(8,128)S(1)}, u32[]{:S(2)}, u32[]{:S(2)}) collective-permute-start(f32[128,256]{1,0:T(8,128)S(1)} %get-tuple-element.32), channel_id=1, source_target_pairs={{0,4},{1,5},{2,6},{3,7},{4,0},{5,1},{6,2},{7,3},{8,12},{9,13},{10,... | collective-permute-start | bytes 393224 | tf_op jit(solution)/shard_map/ppermute | solution.py:288
  14.6 12.1 %collective-permute-start.3 = (f32[128,256]{1,0:T(8,128)S(1)}, f32[128,256]{1,0:T(8,128)S(1)}, u32[]{:S(2)}, u32[]{:S(2)}) collective-permute-start(f32[128,256]{1,0:T(8,128)S(1)} %get-tuple-element.33), channel_id=1, source_target_pairs={{0,2},{1,3},{2,4},{3,5},{4,6},{5,7},{6,0},{7,1},{8,10},{9,11},{10,... | collective-permute-start | bytes 393224 | tf_op jit(solution)/shard_map/ppermute | solution.py:288
  16.8 9.9 %collective-permute-start.4 = (f32[128,256]{1,0:T(8,128)S(1)}, f32[128,256]{1,0:T(8,128)S(1)}, u32[]{:S(2)}, u32[]{:S(2)}) collective-permute-start(f32[128,256]{1,0:T(8,128)S(1)} %get-tuple-element.34), channel_id=1, source_target_pairs={{0,6},{1,7},{2,0},{3,1},{4,2},{5,3},{6,4},{7,5},{8,14},{9,15},{10,... | collective-permute-start | bytes 393224 | tf_op jit(solution)/shard_map/ppermute | solution.py:288
  21.0 7.6 %collective-permute-start.8 = (f32[64,256]{1,0:T(8,128)S(1)}, f32[64,256]{1,0:T(8,128)S(1)}, u32[]{:S(2)}, u32[]{:S(2)}) collective-permute-start(f32[64,256]{1,0:T(8,128)S(1)} %get-tuple-element.40), channel_id=1, source_target_pairs={{0,8},{1,9},{2,10},{3,11},{4,12},{5,13},{6,14},{7,15},{8,16},{9,17... | collective-permute-start | bytes 196616 | tf_op jit(solution)/shard_map/ppermute | solution.py:291
  23.4 5.7 %collective-permute-start.9 = (f32[64,256]{1,0:T(8,128)S(1)}, f32[64,256]{1,0:T(8,128)S(1)}, u32[]{:S(2)}, u32[]{:S(2)}) collective-permute-start(f32[64,256]{1,0:T(8,128)S(1)} %get-tuple-element.41), channel_id=1, source_target_pairs={{0,16},{1,17},{2,18},{3,19},{4,20},{5,21},{6,22},{7,23},{8,24},{9,... | collective-permute-start | bytes 196616 | tf_op jit(solution)/shard_map/ppermute | solution.py:290
  26.7 3.7 %collective-permute-start.11 = (f32[64,256]{1,0:T(8,128)S(1)}, f32[64,256]{1,0:T(8,128)S(1)}, u32[]{:S(2)}, u32[]{:S(2)}) collective-permute-start(f32[64,256]{1,0:T(8,128)S(1)} %get-tuple-element.44.window), channel_id=1, source_target_pairs={{0,31},{1,2},{2,1},{3,4},{4,3},{5,6},{6,5},{7,8},{8,7},{9,10},{10,... | collective-permute-start | bytes 196616 | tf_op jit(solution)/shard_map/ppermute | solution.py:292
  26.7 21.1 %copy-start = (s32[64,4]{0,1:T(4,128)S(1)}, s32[64,4]{0,1:T(4,128)}, u32[]{:S(2)}) copy-start(s32[64,4]{0,1:T(4,128)} %param.11) | copy-start | bytes 3076
  26.7 21.1 %copy-start.1 = (f32[64]{0:T(128)S(1)}, f32[64]{0:T(128)}, u32[]{:S(2)}) copy-start(f32[64]{0:T(128)} %param.10) | copy-start | bytes 772
  26.8 4.7 %collective-permute-start.10 = (f32[64,256]{1,0:T(8,128)S(1)}, f32[64,256]{1,0:T(8,128)S(1)}, u32[]{:S(2)}, u32[]{:S(2)}) collective-permute-start(f32[64,256]{1,0:T(8,128)S(1)} %get-tuple-element.42), channel_id=1, source_target_pairs={{0,24},{1,25},{2,26},{3,27},{4,28},{5,29},{6,30},{7,31},{8,0},{9,1... | collective-permute-start | bytes 196616 | tf_op jit(solution)/shard_map/ppermute | solution.py:294
  31.5 5.1 %collective-permute-start.14 = (f32[72,256]{1,0:T(8,128)S(1)}, f32[72,256]{1,0:T(8,128)S(1)}, u32[]{:S(2)}, u32[]{:S(2)}) collective-permute-start(f32[72,256]{1,0:T(8,128)S(1)} %shard_map.84.a), channel_id=1, source_target_pairs={{0,96},{32,0},{64,32},{96,64},{128,224},{160,128},{192,160},{224,1... | collective-permute-start | bytes 221192 | tf_op jit(solution)/shard_map/ppermute | solution.py:296
  34.6 5.9 %collective-permute-start.13 = (f32[72,256]{1,0:T(8,128)S(1)}, f32[72,256]{1,0:T(8,128)S(1)}, u32[]{:S(2)}, u32[]{:S(2)}) collective-permute-start(f32[72,256]{1,0:T(8,128)S(1)} %shard_map.84.a), channel_id=1, source_target_pairs={{0,64},{32,96},{64,0},{96,32},{128,192},{160,224},{192,128},{224,1... | collective-permute-start | bytes 221192 | tf_op jit(solution)/shard_map/ppermute | solution.py:296
  35.2 6.0 %collective-permute-start.12 = (f32[72,256]{1,0:T(8,128)S(1)}, f32[72,256]{1,0:T(8,128)S(1)}, u32[]{:S(2)}, u32[]{:S(2)}) collective-permute-start(f32[72,256]{1,0:T(8,128)S(1)} %shard_map.84.a), channel_id=1, source_target_pairs={{0,32},{32,64},{64,96},{96,0},{128,160},{160,192},{192,224},{224,1... | collective-permute-start | bytes 221192 | tf_op jit(solution)/shard_map/ppermute | solution.py:296
  41.2 8.9 %collective-permute-start.15 = (f32[72,256]{1,0:T(8,128)S(1)}, f32[72,256]{1,0:T(8,128)S(1)}, u32[]{:S(2)}, u32[]{:S(2)}) collective-permute-start(f32[72,256]{1,0:T(8,128)S(1)} %shard_map.85.mine), channel_id=1, source_target_pairs={{0,128},{32,160},{64,192},{96,224},{128,0},{160,32},{192,64},{224,... | collective-permute-start | bytes 221192 | tf_op jit(solution)/shard_map/ppermute | solution.py:298

commit v4 on v3

--- a/solution.py
+++ b/solution.py
@@ -14,7 +14,6 @@
 PART = 2 * NX * ROWS
 FIRST, SECOND = (2, 1), (3, 0)
 PRODUCT_FLOPS = 2 * PART * 2048 * 16
-PAUSE_FLOPS = 4 * 10**9
 POWER_SCALE = 6.0 * 15.0 / math.pi**4 / 300.0**4
 LOG2E = 1.0 / math.log(2.0)
 PARAMS = dict(vmem_limit_bytes=24 * 2**20)
@@ -97,7 +96,7 @@
     lo, hi = edge_terms(a_lo), edge_terms(a_hi)
     for i in range(4):
         tcopies[i].wait()
-        if i == 1:
+        if i == 0:
             for c in gcopies[0] + gcopies[1] + gcopies[2] + gcopies[3]:
                 c.start()
 
@@ -144,9 +143,8 @@
     spread(lambda rows: t[rows] + u[rows], outs)
 
 
-def x_sum_carry_kernel(a, b, c, d, win, *outs):
+def x_sum_carry_kernel(a, b, c, d, cross, *outs):
     x_sum_kernel(a, b, c, d, *outs)
-    outs[2][...] = win[...]
 
 
 def x_sum_kernel(a, b, c, d, *outs):
@@ -155,7 +153,7 @@
         outs[i][...] = (a[rows] + b[rows]) + (c[rows] + d[rows])
 
 
-def z_sum_kernel(a, b, c, d, par, cross, out):
+def z_sum_kernel(a, b, c, d, par, out):
     out[:ROWS] = (a[...] + b[...]) + (c[...] + d[...])
     out[ROWS:] = par[...]
 
@@ -238,7 +236,12 @@
 CORE = row_perm(lambda z, x, c: (z, x, 1 - c))
 XS = [row_perm(lambda z, x, c, d=d: (z, (x + d) % NX, c)) for d in range(NX)]
 ZS = [row_perm(lambda z, x, c, d=d: ((z + d) % NZ, x, c)) for d in range(NZ)]
-CROSS = [(i, (i + 1 if i % 2 else i - 1) % 32) for i in range(32)]
+CROSS = [
+    (band * 32 + i, (band + 4 * ((i + step) // 32 != 0)) % 8 * 32 + (i + step) % 32)
+    for band in range(8)
+    for i in range(32)
+    for step in [1 if i % 2 else -1]
+]
 YS = [[(h * NY + y, h * NY + (y + d) % NY) for h in range(2) for y in range(NY)] for d in range(NY)]
 HI = [(i, (i + NY) % (2 * NY)) for i in range(2 * NY)]
 
@@ -255,7 +258,6 @@
     rows = sds(2, NX, ROWS, panels, dtype=bf)
     pair = sds(2 * ROWS, orbits)
     cost = pl.CostEstimate(flops=PRODUCT_FLOPS, bytes_accessed=0, transcendentals=0)
-    pause = pl.CostEstimate(flops=PAUSE_FLOPS, bytes_accessed=0, transcendentals=0)
     far = [
         pltpu.with_memory_space_constraint(a, pltpu.HBM)
         for a in (band_edges, emissivity, temps, g)
@@ -282,17 +284,17 @@
     u_b = lax.ppermute(u_b, "row", CORE)
     *s_a, swapped = call(add_kernel, 2, [pair] * NX + [block])(t_a, u_a)
     x_a = [lax.ppermute(s_a[d], "row", XS[d]) for d in (2, 1, 3)]
+    cross = lax.ppermute(win, ("band", "row"), CROSS)
     s_b = call(product_add_kernel, 4, [pair] * NX, scratch=[VMEM((PART, orbits), F32)], cost=cost)(
         p, g3, u_b, s_a[0]
     )
     x_b = [lax.ppermute(s_b[d], "row", XS[d]) for d in (2, 1, 3)]
-    z2, z1, win = call(x_sum_carry_kernel, 5, [block] * 3)(s_a[0], *x_a, win)
+    z2, z1 = call(x_sum_carry_kernel, 5, [block] * 2)(s_a[0], *x_a, cross)
     z2 = lax.ppermute(z2, "row", ZS[2])
     z1 = lax.ppermute(z1, "row", ZS[1])
-    cross = lax.ppermute(win, "row", CROSS)
-    z3, z0 = call(x_sum_kernel, 4, [block] * 2, cost=pause)(s_b[0], *x_b)
+    z3, z0 = call(x_sum_kernel, 4, [block] * 2)(s_b[0], *x_b)
     z3 = lax.ppermute(z3, "row", ZS[3])
-    zsum = call(z_sum_kernel, 6, message)(z0, z1, z2, z3, par, cross)
+    zsum = call(z_sum_kernel, 5, message)(z0, z1, z2, z3, par)
     y_in = [lax.ppermute(zsum, "band", YS[d]) for d in (1, 2, 3)]
     mine = call(y_sum_kernel, 4, message)(zsum, *y_in)
     other = lax.ppermute(mine, "band", HI)

time: 51.2 us -> 50.9 us (level)
    ppermute x3, starting transfers between devices: 3.59 us -> 8.35 us  [body(): x_a = [lax.ppermute(s_a[d], 'row', XS[d]) for d in (2, 1, 3)]]
    ppermute x1, starting transfers between devices: 3.28 us -> 0.09 us  [body(): z2 = lax.ppermute(z2, 'row', ZS[2])]
    ppermute x1, starting transfers between devices: 2.42 us -> 0.08 us  [body(): z1 = lax.ppermute(z1, 'row', ZS[1])]
    ppermute x1, starting transfers between devices: 6.55 us -> 4.4 us  [body(): other = lax.ppermute(mine, 'band', HI)]
    ppermute x3, waiting for transfers between devices: 5.04 us -> 3 us  [body(): y_in = [lax.ppermute(zsum, 'band', YS[d]) for d in (1, 2, 3)]]
    ppermute x3, waiting for transfers between devices: 0.01 us -> 1.7 us  [body(): x_b = [lax.ppermute(s_b[d], 'row', XS[d]) for d in (2, 1, 3)]]
    ppermute x1, waiting for transfers between devices: 1.84 us -> 3.45 us  [body(): other = lax.ppermute(mine, 'band', HI)]
    ppermute x1, waiting for transfers between devices: 0.01 us -> 1.49 us  [body(): z1 = lax.ppermute(z1, 'row', ZS[1])]
  transfers between devices with their start and end apart: 16 -> 16, of which waited for: 9 -> 10; matrix products, arithmetic and copies ran while one was open for 0% -> 0% of each run, Pallas kernels for 6% -> 6%
where the time goes in v4:
time: 50.9 us; the launch traced here: 50.8 us
  starting transfers between devices  27.1 us (53%)
  waiting for transfers between devices  14.3 us (28%)
  Pallas kernels  8.68 us (17%)
  between operations  0.74 us (1%)
    ppermute x3, starting transfers between devices, body(): x_a = [lax.ppermute(s_a[d], 'row', XS[d]) for d in (2, 1, 3)]  8.35 us
    ppermute x3, starting transfers between devices, body(): y_in = [lax.ppermute(zsum, 'band', YS[d]) for d in (1, 2, 3)]  5.9 us
    pallas_call x1, Pallas kernels, body(): call(first_kernel, 4, [sds(PART + ROWS, orbits), sds(orbits, panels, dtyp...  4.76 us
    ppermute x1, starting transfers between devices, body(): other = lax.ppermute(mine, 'band', HI)  4.4 us
    ppermute x3, starting transfers between devices, body(): x_b = [lax.ppermute(s_b[d], 'row', XS[d]) for d in (2, 1, 3)]  4.25 us
    ppermute x1, waiting for transfers between devices, body(): other = lax.ppermute(mine, 'band', HI)  3.45 us
    ppermute x3, waiting for transfers between devices, body(): x_a = [lax.ppermute(s_a[d], 'row', XS[d]) for d in (2, 1, 3)]  3.41 us
    ppermute x3, waiting for transfers between devices, body(): y_in = [lax.ppermute(zsum, 'band', YS[d]) for d in (1, 2, 3)]  3 us
  transfers between devices with their start and end apart: 16, of which 10 were waited for; matrix products, arithmetic and copies ran while one was open for 0% of the time, Pallas kernels for 6%

profile of v4, /device:TPU:6, one launch (start us, length us, event | category | flops | bytes accessed | tf_op | source)
XLA Modules:
  0.0 50.8 jit_solution(2592511104066133197)
XLA Ops:
  0.6 4.8 %shard_map.77 = (f32[576,256]{1,0:T(8,128)S(1)}, bf16[256,2048]{1,0:T(8,128)(2,1)S(1)}, bf16[2,4,64,2048]{3,2,1,0:T(8,128)(2,1)S(1)}, bf16[2,4,64,2048]{3,2,1,0:...) custom-call(s32[1,2]{1,0:T(1,128)} %edges_hbm.1, ...), custom_call_target="tpu_custom_call" | custom-call | flops 33554432 | tf_op jit(solution)/shard_map/pallas_call | solution.py:265
  5.4 0.1 collective-permute-start.1
  5.5 0.7 %shard_map.78.refs_0_.t = f32[512,256]{1,0:T(8,128)S(1)} custom-call(bf16[256,2048]{1,0:T(8,128)(2,1)S(1)} %get-tuple-element.24.p, bf16[2,4,64,2048]{3,2,1,0:T(8,128)(2,1)S(1)} %get-tuple-element.27.g), custom_call_target="tpu_custom_call" | custom-call | flops 33554432 | tf_op jit(solution)/shard_map/pallas_call | solution.py:282
  6.3 0.7 %shard_map.79 = f32[512,256]{1,0:T(8,128)S(1)} custom-call(bf16[256,2048]{1,0:T(8,128)(2,1)S(1)} %get-tuple-element.24.p, bf16[2,4,64,2048]{3,2,1,0:T(8,128)(2,1)S(1)} %get-tuple-element.26.g, f32[512,256]{1,0:T(8,128)S(1)} %shard_map.78.refs_0_.t), custom_call_target="tpu_custom_call" | custom-call | flops 33554432 | tf_op jit(solution)/shard_map/pallas_call | solution.py:283
  7.0 0.6 %collective-permute-start = (f32[512,256]{1,0:T(8,128)S(1)}, f32[512,256]{1,0:T(8,128)S(1)}, u32[]{:S(2)}, u32[]{:S(2)}) collective-permute-start(f32[512,256]{1,0:T(8,128)S(1)} %shard_map.79), channel_id=1, source_target_pairs={{0,1},{1,0},{2,3},{3,2},{4,5},{5,4},{6,7},{7,6},{8,9},{9,8},{10,11... | collective-permute-start | bytes 1572872 | tf_op jit(solution)/shard_map/ppermute | solution.py:284
  7.6 0.1 shard_map.80
  7.7 1.5 %collective-permute-start.5 = (f32[128,256]{1,0:T(8,128)S(1)}, f32[128,256]{1,0:T(8,128)S(1)}, u32[]{:S(2)}, u32[]{:S(2)}) collective-permute-start(f32[128,256]{1,0:T(8,128)S(1)} %get-tuple-element.35), channel_id=1, source_target_pairs={{0,4},{1,5},{2,6},{3,7},{4,0},{5,1},{6,2},{7,3},{8,12},{9,13},{10,... | collective-permute-start | bytes 393224 | tf_op jit(solution)/shard_map/ppermute | solution.py:286
  9.2 1.0 %collective-permute-start.8 = (f32[64,256]{1,0:T(8,128)S(1)}, f32[64,256]{1,0:T(8,128)S(1)}, u32[]{:S(2)}, u32[]{:S(2)}) collective-permute-start(f32[64,256]{1,0:T(8,128)S(1)} %get-tuple-element.38.window), channel_id=1, source_target_pairs={{0,159},{1,2},{2,1},{3,4},{4,3},{5,6},{6,5},{7,8},{8,7},{9,10},{10... | collective-permute-start | bytes 196616 | tf_op jit(solution)/shard_map/ppermute | solution.py:287
  10.2 6.9 %collective-permute-start.6 = (f32[128,256]{1,0:T(8,128)S(1)}, f32[128,256]{1,0:T(8,128)S(1)}, u32[]{:S(2)}, u32[]{:S(2)}) collective-permute-start(f32[128,256]{1,0:T(8,128)S(1)} %get-tuple-element.36), channel_id=1, source_target_pairs={{0,2},{1,3},{2,4},{3,5},{4,6},{5,7},{6,0},{7,1},{8,10},{9,11},{10,... | collective-permute-start | bytes 393224 | tf_op jit(solution)/shard_map/ppermute | solution.py:286
  17.1 0.8 %shard_map.81 = (f32[128,256]{1,0:T(8,128)S(1)}, f32[128,256]{1,0:T(8,128)S(1)}, f32[128,256]{1,0:T(8,128)S(1)}, f32[128,256]{1,0:T(8,128)S(1)}) custom-call(bf16[256,2048]{1,0:T(8,128)(2,1)S(1)} %get-tuple-element.24.p, bf16[2,4,64,2048]{3,2,1,0:T(8,128)(2,1)S(1)} %get-tuple-element.25.g, f32[512,256]{1,0:T(8,128)S(1)} %collective-permute-done.u, ...), custom_call_target="tpu_custom_call" | custom-call | flops 33554432 | tf_op jit(solution)/shard_map/pallas_call | solution.py:288
  17.9 1.5 %collective-permute-start.2 = (f32[128,256]{1,0:T(8,128)S(1)}, f32[128,256]{1,0:T(8,128)S(1)}, u32[]{:S(2)}, u32[]{:S(2)}) collective-permute-start(f32[128,256]{1,0:T(8,128)S(1)} %get-tuple-element.31), channel_id=1, source_target_pairs={{0,4},{1,5},{2,6},{3,7},{4,0},{5,1},{6,2},{7,3},{8,12},{9,13},{10,... | collective-permute-start | bytes 393224 | tf_op jit(solution)/shard_map/ppermute | solution.py:291
  19.4 1.9 %collective-permute-start.3 = (f32[128,256]{1,0:T(8,128)S(1)}, f32[128,256]{1,0:T(8,128)S(1)}, u32[]{:S(2)}, u32[]{:S(2)}) collective-permute-start(f32[128,256]{1,0:T(8,128)S(1)} %get-tuple-element.32), channel_id=1, source_target_pairs={{0,2},{1,3},{2,4},{3,5},{4,6},{5,7},{6,0},{7,1},{8,10},{9,11},{10,... | collective-permute-start | bytes 393224 | tf_op jit(solution)/shard_map/ppermute | solution.py:291
  21.3 0.8 %collective-permute-start.4 = (f32[128,256]{1,0:T(8,128)S(1)}, f32[128,256]{1,0:T(8,128)S(1)}, u32[]{:S(2)}, u32[]{:S(2)}) collective-permute-start(f32[128,256]{1,0:T(8,128)S(1)} %get-tuple-element.33), channel_id=1, source_target_pairs={{0,6},{1,7},{2,0},{3,1},{4,2},{5,3},{6,4},{7,5},{8,14},{9,15},{10,... | collective-permute-start | bytes 393224 | tf_op jit(solution)/shard_map/ppermute | solution.py:291
  22.1 3.4 %collective-permute-done.7.d = f32[128,256]{1,0:T(8,128)S(1)} collective-permute-done((f32[128,256]{1,0:T(8,128)S(1)}, f32[128,256]{1,0:T(8,128)S(1)}, u32[]{:S(2)}, u32[]{:S(2)}) %collective-permute-start.7) | collective-permute-done | bytes 131104 | tf_op jit(solution)/shard_map/ppermute | solution.py:286
  25.6 0.1 collective-permute-start.10
  25.7 0.1 collective-permute-start.9
  25.8 0.7 %collective-permute-done.3.c = f32[128,256]{1,0:T(8,128)S(1)} collective-permute-done((f32[128,256]{1,0:T(8,128)S(1)}, f32[128,256]{1,0:T(8,128)S(1)}, u32[]{:S(2)}, u32[]{:S(2)}) %collective-permute-start.3) | collective-permute-done | bytes 131104 | tf_op jit(solution)/shard_map/ppermute | solution.py:291
  26.4 1.0 %collective-permute-done.4.d = f32[128,256]{1,0:T(8,128)S(1)} collective-permute-done((f32[128,256]{1,0:T(8,128)S(1)}, f32[128,256]{1,0:T(8,128)S(1)}, u32[]{:S(2)}, u32[]{:S(2)}) %collective-permute-start.4) | collective-permute-done | bytes 131104 | tf_op jit(solution)/shard_map/ppermute | solution.py:291
  27.5 2.3 %collective-permute-start.11 = (f32[64,256]{1,0:T(8,128)S(1)}, f32[64,256]{1,0:T(8,128)S(1)}, u32[]{:S(2)}, u32[]{:S(2)}) collective-permute-start(f32[64,256]{1,0:T(8,128)S(1)} %get-tuple-element.41), channel_id=1, source_target_pairs={{0,24},{1,25},{2,26},{3,27},{4,28},{5,29},{6,30},{7,31},{8,0},{9,1... | collective-permute-start | bytes 196616 | tf_op jit(solution)/shard_map/ppermute | solution.py:296
  29.8 1.0 %collective-permute-done.10.c = f32[64,256]{1,0:T(8,128)S(1)} collective-permute-done((f32[64,256]{1,0:T(8,128)S(1)}, f32[64,256]{1,0:T(8,128)S(1)}, u32[]{:S(2)}, u32[]{:S(2)}) %collective-permute-start.10) | collective-permute-done | bytes 65568 | tf_op jit(solution)/shard_map/ppermute | solution.py:293
  30.8 1.5 %collective-permute-done.9.b = f32[64,256]{1,0:T(8,128)S(1)} collective-permute-done((f32[64,256]{1,0:T(8,128)S(1)}, f32[64,256]{1,0:T(8,128)S(1)}, u32[]{:S(2)}, u32[]{:S(2)}) %collective-permute-start.9) | collective-permute-done | bytes 65568 | tf_op jit(solution)/shard_map/ppermute | solution.py:294
  32.3 0.2 collective-permute-done.11.d
  32.5 1.7 %collective-permute-start.12 = (f32[72,256]{1,0:T(8,128)S(1)}, f32[72,256]{1,0:T(8,128)S(1)}, u32[]{:S(2)}, u32[]{:S(2)}) collective-permute-start(f32[72,256]{1,0:T(8,128)S(1)} %shard_map.84.a), channel_id=1, source_target_pairs={{0,32},{32,64},{64,96},{96,0},{128,160},{160,192},{192,224},{224,1... | collective-permute-start | bytes 221192 | tf_op jit(solution)/shard_map/ppermute | solution.py:298
  34.2 2.9 %collective-permute-start.13 = (f32[72,256]{1,0:T(8,128)S(1)}, f32[72,256]{1,0:T(8,128)S(1)}, u32[]{:S(2)}, u32[]{:S(2)}) collective-permute-start(f32[72,256]{1,0:T(8,128)S(1)} %shard_map.84.a), channel_id=1, source_target_pairs={{0,64},{32,96},{64,0},{96,32},{128,192},{160,224},{192,128},{224,1... | collective-permute-start | bytes 221192 | tf_op jit(solution)/shard_map/ppermute | solution.py:298
  37.1 1.3 %collective-permute-start.14 = (f32[72,256]{1,0:T(8,128)S(1)}, f32[72,256]{1,0:T(8,128)S(1)}, u32[]{:S(2)}, u32[]{:S(2)}) collective-permute-start(f32[72,256]{1,0:T(8,128)S(1)} %shard_map.84.a), channel_id=1, source_target_pairs={{0,96},{32,0},{64,32},{96,64},{128,224},{160,128},{192,160},{224,1... | collective-permute-start | bytes 221192 | tf_op jit(solution)/shard_map/ppermute | solution.py:298
  38.4 0.1 collective-permute-done.12.b
  38.5 1.7 %collective-permute-done.13.c = f32[72,256]{1,0:T(8,128)S(1)} collective-permute-done((f32[72,256]{1,0:T(8,128)S(1)}, f32[72,256]{1,0:T(8,128)S(1)}, u32[]{:S(2)}, u32[]{:S(2)}) %collective-permute-start.13) | collective-permute-done | bytes 73760 | tf_op jit(solution)/shard_map/ppermute | solution.py:298
  40.2 1.2 %collective-permute-done.14.d = f32[72,256]{1,0:T(8,128)S(1)} collective-permute-done((f32[72,256]{1,0:T(8,128)S(1)}, f32[72,256]{1,0:T(8,128)S(1)}, u32[]{:S(2)}, u32[]{:S(2)}) %collective-permute-start.14) | collective-permute-done | bytes 73760 | tf_op jit(solution)/shard_map/ppermute | solution.py:298
  41.5 4.4 %collective-permute-start.15 = (f32[72,256]{1,0:T(8,128)S(1)}, f32[72,256]{1,0:T(8,128)S(1)}, u32[]{:S(2)}, u32[]{:S(2)}) collective-permute-start(f32[72,256]{1,0:T(8,128)S(1)} %shard_map.85.mine), channel_id=1, source_target_pairs={{0,128},{32,160},{64,192},{96,224},{128,0},{160,32},{192,64},{224,... | collective-permute-start | bytes 221192 | tf_op jit(solution)/shard_map/ppermute | solution.py:300
  45.9 0.5 shard_map.86.side
  46.4 3.5 %collective-permute-done.15.other = f32[72,256]{1,0:T(8,128)S(1)} collective-permute-done((f32[72,256]{1,0:T(8,128)S(1)}, f32[72,256]{1,0:T(8,128)S(1)}, u32[]{:S(2)}, u32[]{:S(2)}) %collective-permute-start.15) | collective-permute-done | bytes 73760 | tf_op jit(solution)/shard_map/ppermute | solution.py:300
  49.8 1.0 %shard_map.87 = (f32[64,256]{1,0:T(8,128)}, f32[64,256]{1,0:T(8,128)}) custom-call(f32[72,256]{1,0:T(8,128)S(1)} %shard_map.85.mine, f32[72,256]{1,0:T(8,128)S(1)} %collective-permute-done.15.other, f32[64,256]{1,0:T(8,128)S(1)} %shard_map.86.side, f32[64,256]{1,0:T(8,128)S(1)} %get-tuple-element.38.window), custom_call_target="tpu_custom_call" | custom-call | tf_op jit(solution)/shard_map/pallas_call | solution.py:304
  (15 shorter events, 0.1 us)
Async XLA Ops:
  5.4 2.2 %collective-permute-start.1 = (f32[576,256]{1,0:T(8,128)S(1)}, f32[576,256]{1,0:T(8,128)S(1)}, u32[]{:S(2)}, u32[]{:S(2)}) collective-permute-start(f32[576,256]{1,0:T(8,128)S(1)} %get-tuple-element.28), channel_id=1, source_target_pairs={{0,1},{1,0},{2,3},{3,2},{4,5},{5,4},{6,7},{7,6},{8,9},{9,8},{10,11... | collective-permute-start | bytes 1769480 | tf_op jit(solution)/shard_map/ppermute | solution.py:281
  7.0 10.1 %collective-permute-start = (f32[512,256]{1,0:T(8,128)S(1)}, f32[512,256]{1,0:T(8,128)S(1)}, u32[]{:S(2)}, u32[]{:S(2)}) collective-permute-start(f32[512,256]{1,0:T(8,128)S(1)} %shard_map.79), channel_id=1, source_target_pairs={{0,1},{1,0},{2,3},{3,2},{4,5},{5,4},{6,7},{7,6},{8,9},{9,8},{10,11... | collective-permute-start | bytes 1572872 | tf_op jit(solution)/shard_map/ppermute | solution.py:284
  7.7 13.6 %collective-permute-start.5 = (f32[128,256]{1,0:T(8,128)S(1)}, f32[128,256]{1,0:T(8,128)S(1)}, u32[]{:S(2)}, u32[]{:S(2)}) collective-permute-start(f32[128,256]{1,0:T(8,128)S(1)} %get-tuple-element.35), channel_id=1, source_target_pairs={{0,4},{1,5},{2,6},{3,7},{4,0},{5,1},{6,2},{7,3},{8,12},{9,13},{10,... | collective-permute-start | bytes 393224 | tf_op jit(solution)/shard_map/ppermute | solution.py:286
  9.2 10.2 %collective-permute-start.8 = (f32[64,256]{1,0:T(8,128)S(1)}, f32[64,256]{1,0:T(8,128)S(1)}, u32[]{:S(2)}, u32[]{:S(2)}) collective-permute-start(f32[64,256]{1,0:T(8,128)S(1)} %get-tuple-element.38.window), channel_id=1, source_target_pairs={{0,159},{1,2},{2,1},{3,4},{4,3},{5,6},{6,5},{7,8},{8,7},{9,10},{10... | collective-permute-start | bytes 196616 | tf_op jit(solution)/shard_map/ppermute | solution.py:287
  10.2 11.9 %collective-permute-start.6 = (f32[128,256]{1,0:T(8,128)S(1)}, f32[128,256]{1,0:T(8,128)S(1)}, u32[]{:S(2)}, u32[]{:S(2)}) collective-permute-start(f32[128,256]{1,0:T(8,128)S(1)} %get-tuple-element.36), channel_id=1, source_target_pairs={{0,2},{1,3},{2,4},{3,5},{4,6},{5,7},{6,0},{7,1},{8,10},{9,11},{10,... | collective-permute-start | bytes 393224 | tf_op jit(solution)/shard_map/ppermute | solution.py:286
  17.1 8.5 %collective-permute-start.7 = (f32[128,256]{1,0:T(8,128)S(1)}, f32[128,256]{1,0:T(8,128)S(1)}, u32[]{:S(2)}, u32[]{:S(2)}) collective-permute-start(f32[128,256]{1,0:T(8,128)S(1)} %get-tuple-element.37), channel_id=1, source_target_pairs={{0,6},{1,7},{2,0},{3,1},{4,2},{5,3},{6,4},{7,5},{8,14},{9,15},{10,... | collective-permute-start | bytes 393224 | tf_op jit(solution)/shard_map/ppermute | solution.py:286
  17.1 28.8 %copy-start = (s32[64,4]{0,1:T(4,128)S(1)}, s32[64,4]{0,1:T(4,128)}, u32[]{:S(2)}) copy-start(s32[64,4]{0,1:T(4,128)} %param.11) | copy-start | bytes 3076
  17.1 28.8 %copy-start.1 = (f32[64]{0:T(128)S(1)}, f32[64]{0:T(128)}, u32[]{:S(2)}) copy-start(f32[64]{0:T(128)} %param.10) | copy-start | bytes 772
  17.9 7.9 %collective-permute-start.2 = (f32[128,256]{1,0:T(8,128)S(1)}, f32[128,256]{1,0:T(8,128)S(1)}, u32[]{:S(2)}, u32[]{:S(2)}) collective-permute-start(f32[128,256]{1,0:T(8,128)S(1)} %get-tuple-element.31), channel_id=1, source_target_pairs={{0,4},{1,5},{2,6},{3,7},{4,0},{5,1},{6,2},{7,3},{8,12},{9,13},{10,... | collective-permute-start | bytes 393224 | tf_op jit(solution)/shard_map/ppermute | solution.py:291
  19.4 7.0 %collective-permute-start.3 = (f32[128,256]{1,0:T(8,128)S(1)}, f32[128,256]{1,0:T(8,128)S(1)}, u32[]{:S(2)}, u32[]{:S(2)}) collective-permute-start(f32[128,256]{1,0:T(8,128)S(1)} %get-tuple-element.32), channel_id=1, source_target_pairs={{0,2},{1,3},{2,4},{3,5},{4,6},{5,7},{6,0},{7,1},{8,10},{9,11},{10,... | collective-permute-start | bytes 393224 | tf_op jit(solution)/shard_map/ppermute | solution.py:291
  21.3 6.2 %collective-permute-start.4 = (f32[128,256]{1,0:T(8,128)S(1)}, f32[128,256]{1,0:T(8,128)S(1)}, u32[]{:S(2)}, u32[]{:S(2)}) collective-permute-start(f32[128,256]{1,0:T(8,128)S(1)} %get-tuple-element.33), channel_id=1, source_target_pairs={{0,6},{1,7},{2,0},{3,1},{4,2},{5,3},{6,4},{7,5},{8,14},{9,15},{10,... | collective-permute-start | bytes 393224 | tf_op jit(solution)/shard_map/ppermute | solution.py:291
  25.6 5.3 %collective-permute-start.10 = (f32[64,256]{1,0:T(8,128)S(1)}, f32[64,256]{1,0:T(8,128)S(1)}, u32[]{:S(2)}, u32[]{:S(2)}) collective-permute-start(f32[64,256]{1,0:T(8,128)S(1)} %get-tuple-element.40), channel_id=1, source_target_pairs={{0,16},{1,17},{2,18},{3,19},{4,20},{5,21},{6,22},{7,23},{8,24},{9,... | collective-permute-start | bytes 196616 | tf_op jit(solution)/shard_map/ppermute | solution.py:293
  25.7 6.6 %collective-permute-start.9 = (f32[64,256]{1,0:T(8,128)S(1)}, f32[64,256]{1,0:T(8,128)S(1)}, u32[]{:S(2)}, u32[]{:S(2)}) collective-permute-start(f32[64,256]{1,0:T(8,128)S(1)} %get-tuple-element.39), channel_id=1, source_target_pairs={{0,8},{1,9},{2,10},{3,11},{4,12},{5,13},{6,14},{7,15},{8,16},{9,17... | collective-permute-start | bytes 196616 | tf_op jit(solution)/shard_map/ppermute | solution.py:294
  27.5 5.0 %collective-permute-start.11 = (f32[64,256]{1,0:T(8,128)S(1)}, f32[64,256]{1,0:T(8,128)S(1)}, u32[]{:S(2)}, u32[]{:S(2)}) collective-permute-start(f32[64,256]{1,0:T(8,128)S(1)} %get-tuple-element.41), channel_id=1, source_target_pairs={{0,24},{1,25},{2,26},{3,27},{4,28},{5,29},{6,30},{7,31},{8,0},{9,1... | collective-permute-start | bytes 196616 | tf_op jit(solution)/shard_map/ppermute | solution.py:296
  32.5 6.0 %collective-permute-start.12 = (f32[72,256]{1,0:T(8,128)S(1)}, f32[72,256]{1,0:T(8,128)S(1)}, u32[]{:S(2)}, u32[]{:S(2)}) collective-permute-start(f32[72,256]{1,0:T(8,128)S(1)} %shard_map.84.a), channel_id=1, source_target_pairs={{0,32},{32,64},{64,96},{96,0},{128,160},{160,192},{192,224},{224,1... | collective-permute-start | bytes 221192 | tf_op jit(solution)/shard_map/ppermute | solution.py:298
  34.2 6.0 %collective-permute-start.13 = (f32[72,256]{1,0:T(8,128)S(1)}, f32[72,256]{1,0:T(8,128)S(1)}, u32[]{:S(2)}, u32[]{:S(2)}) collective-permute-start(f32[72,256]{1,0:T(8,128)S(1)} %shard_map.84.a), channel_id=1, source_target_pairs={{0,64},{32,96},{64,0},{96,32},{128,192},{160,224},{192,128},{224,1... | collective-permute-start | bytes 221192 | tf_op jit(solution)/shard_map/ppermute | solution.py:298
  37.1 4.4 %collective-permute-start.14 = (f32[72,256]{1,0:T(8,128)S(1)}, f32[72,256]{1,0:T(8,128)S(1)}, u32[]{:S(2)}, u32[]{:S(2)}) collective-permute-start(f32[72,256]{1,0:T(8,128)S(1)} %shard_map.84.a), channel_id=1, source_target_pairs={{0,96},{32,0},{64,32},{96,64},{128,224},{160,128},{192,160},{224,1... | collective-permute-start | bytes 221192 | tf_op jit(solution)/shard_map/ppermute | solution.py:298
  41.5 8.3 %collective-permute-start.15 = (f32[72,256]{1,0:T(8,128)S(1)}, f32[72,256]{1,0:T(8,128)S(1)}, u32[]{:S(2)}, u32[]{:S(2)}) collective-permute-start(f32[72,256]{1,0:T(8,128)S(1)} %shard_map.85.mine), channel_id=1, source_target_pairs={{0,128},{32,160},{64,192},{96,224},{128,0},{160,32},{192,64},{224,... | collective-permute-start | bytes 221192 | tf_op jit(solution)/shard_map/ppermute | solution.py:300

commit v5 on v4

--- a/solution.py
+++ b/solution.py
@@ -83,7 +83,9 @@
         fetch_rows(g_hbm, g3, gsem.at[3], z, core, SECOND),
     ]
     for c in small + tcopies:
-        c.start()
+        c.start(priority=0)
+    for c in gcopies[0] + gcopies[2] + gcopies[1] + gcopies[3]:
+        c.start(priority=1)
     for c in small:
         c.wait()
     a_lo = 14388000.0 / jnp.full((1, 512), edges[0, 0].astype(F32))
@@ -96,9 +98,6 @@
     lo, hi = edge_terms(a_lo), edge_terms(a_hi)
     for i in range(4):
         tcopies[i].wait()
-        if i == 0:
-            for c in gcopies[0] + gcopies[1] + gcopies[2] + gcopies[3]:
-                c.start()
 
         @pl.loop(0, part // 16)
         def _(j):

time: 50.9 us -> 50.3 us (0.988)
  Pallas kernels: 8.68 us -> 8.11 us
    pallas_call x1, Pallas kernels: 4.76 us -> 4.19 us  [body(): call(first_kernel, 4, [sds(PART + ROWS, orbits), sds(orbits, panels, dtyp...]
where the time goes in v5:
time: 50.3 us; the launch traced here: 50.2 us
  starting transfers between devices  27.1 us (54%)
  waiting for transfers between devices  14.3 us (28%)
  Pallas kernels  8.11 us (16%)
  between operations  0.74 us (1%)
    ppermute x3, starting transfers between devices, body(): x_a = [lax.ppermute(s_a[d], 'row', XS[d]) for d in (2, 1, 3)]  8.36 us
    ppermute x3, starting transfers between devices, body(): y_in = [lax.ppermute(zsum, 'band', YS[d]) for d in (1, 2, 3)]  5.9 us
    ppermute x1, starting transfers between devices, body(): other = lax.ppermute(mine, 'band', HI)  4.4 us
    ppermute x3, starting transfers between devices, body(): x_b = [lax.ppermute(s_b[d], 'row', XS[d]) for d in (2, 1, 3)]  4.25 us
    pallas_call x1, Pallas kernels, body(): call(first_kernel, 4, [sds(PART + ROWS, orbits), sds(orbits, panels, dtyp...  4.19 us
    ppermute x1, waiting for transfers between devices, body(): other = lax.ppermute(mine, 'band', HI)  3.46 us
    ppermute x3, waiting for transfers between devices, body(): x_a = [lax.ppermute(s_a[d], 'row', XS[d]) for d in (2, 1, 3)]  3.4 us
    ppermute x3, waiting for transfers between devices, body(): y_in = [lax.ppermute(zsum, 'band', YS[d]) for d in (1, 2, 3)]  3 us
  transfers between devices with their start and end apart: 16, of which 10 were waited for; matrix products, arithmetic and copies ran while one was open for 0% of the time, Pallas kernels for 6%

profile of v5, /device:TPU:6, one launch (start us, length us, event | category | flops | bytes accessed | tf_op | source)
XLA Modules:
  0.0 50.2 jit_solution(12057979509347106322)
XLA Ops:
  0.6 4.2 %shard_map.77 = (f32[576,256]{1,0:T(8,128)S(1)}, bf16[256,2048]{1,0:T(8,128)(2,1)S(1)}, bf16[2,4,64,2048]{3,2,1,0:T(8,128)(2,1)S(1)}, bf16[2,4,64,2048]{3,2,1,0:...) custom-call(s32[1,2]{1,0:T(1,128)} %edges_hbm.1, ...), custom_call_target="tpu_custom_call" | custom-call | flops 33554432 | tf_op jit(solution)/shard_map/pallas_call | solution.py:264
  4.8 0.1 collective-permute-start.1
  4.9 0.7 %shard_map.78.refs_0_.t = f32[512,256]{1,0:T(8,128)S(1)} custom-call(bf16[256,2048]{1,0:T(8,128)(2,1)S(1)} %get-tuple-element.24.p, bf16[2,4,64,2048]{3,2,1,0:T(8,128)(2,1)S(1)} %get-tuple-element.27.g), custom_call_target="tpu_custom_call" | custom-call | flops 33554432 | tf_op jit(solution)/shard_map/pallas_call | solution.py:281
  5.7 0.7 %shard_map.79 = f32[512,256]{1,0:T(8,128)S(1)} custom-call(bf16[256,2048]{1,0:T(8,128)(2,1)S(1)} %get-tuple-element.24.p, bf16[2,4,64,2048]{3,2,1,0:T(8,128)(2,1)S(1)} %get-tuple-element.26.g, f32[512,256]{1,0:T(8,128)S(1)} %shard_map.78.refs_0_.t), custom_call_target="tpu_custom_call" | custom-call | flops 33554432 | tf_op jit(solution)/shard_map/pallas_call | solution.py:282
  6.4 0.6 %collective-permute-start = (f32[512,256]{1,0:T(8,128)S(1)}, f32[512,256]{1,0:T(8,128)S(1)}, u32[]{:S(2)}, u32[]{:S(2)}) collective-permute-start(f32[512,256]{1,0:T(8,128)S(1)} %shard_map.79), channel_id=1, source_target_pairs={{0,1},{1,0},{2,3},{3,2},{4,5},{5,4},{6,7},{7,6},{8,9},{9,8},{10,11... | collective-permute-start | bytes 1572872 | tf_op jit(solution)/shard_map/ppermute | solution.py:283
  7.0 0.1 shard_map.80
  7.1 1.5 %collective-permute-start.5 = (f32[128,256]{1,0:T(8,128)S(1)}, f32[128,256]{1,0:T(8,128)S(1)}, u32[]{:S(2)}, u32[]{:S(2)}) collective-permute-start(f32[128,256]{1,0:T(8,128)S(1)} %get-tuple-element.35), channel_id=1, source_target_pairs={{0,4},{1,5},{2,6},{3,7},{4,0},{5,1},{6,2},{7,3},{8,12},{9,13},{10,... | collective-permute-start | bytes 393224 | tf_op jit(solution)/shard_map/ppermute | solution.py:285
  8.6 1.0 %collective-permute-start.8 = (f32[64,256]{1,0:T(8,128)S(1)}, f32[64,256]{1,0:T(8,128)S(1)}, u32[]{:S(2)}, u32[]{:S(2)}) collective-permute-start(f32[64,256]{1,0:T(8,128)S(1)} %get-tuple-element.38.window), channel_id=1, source_target_pairs={{0,159},{1,2},{2,1},{3,4},{4,3},{5,6},{6,5},{7,8},{8,7},{9,10},{10... | collective-permute-start | bytes 196616 | tf_op jit(solution)/shard_map/ppermute | solution.py:286
  9.6 6.9 %collective-permute-start.6 = (f32[128,256]{1,0:T(8,128)S(1)}, f32[128,256]{1,0:T(8,128)S(1)}, u32[]{:S(2)}, u32[]{:S(2)}) collective-permute-start(f32[128,256]{1,0:T(8,128)S(1)} %get-tuple-element.36), channel_id=1, source_target_pairs={{0,2},{1,3},{2,4},{3,5},{4,6},{5,7},{6,0},{7,1},{8,10},{9,11},{10,... | collective-permute-start | bytes 393224 | tf_op jit(solution)/shard_map/ppermute | solution.py:285
  16.5 0.8 %shard_map.81 = (f32[128,256]{1,0:T(8,128)S(1)}, f32[128,256]{1,0:T(8,128)S(1)}, f32[128,256]{1,0:T(8,128)S(1)}, f32[128,256]{1,0:T(8,128)S(1)}) custom-call(bf16[256,2048]{1,0:T(8,128)(2,1)S(1)} %get-tuple-element.24.p, bf16[2,4,64,2048]{3,2,1,0:T(8,128)(2,1)S(1)} %get-tuple-element.25.g, f32[512,256]{1,0:T(8,128)S(1)} %collective-permute-done.u, ...), custom_call_target="tpu_custom_call" | custom-call | flops 33554432 | tf_op jit(solution)/shard_map/pallas_call | solution.py:287
  17.3 1.5 %collective-permute-start.2 = (f32[128,256]{1,0:T(8,128)S(1)}, f32[128,256]{1,0:T(8,128)S(1)}, u32[]{:S(2)}, u32[]{:S(2)}) collective-permute-start(f32[128,256]{1,0:T(8,128)S(1)} %get-tuple-element.31), channel_id=1, source_target_pairs={{0,4},{1,5},{2,6},{3,7},{4,0},{5,1},{6,2},{7,3},{8,12},{9,13},{10,... | collective-permute-start | bytes 393224 | tf_op jit(solution)/shard_map/ppermute | solution.py:290
  18.8 1.9 %collective-permute-start.3 = (f32[128,256]{1,0:T(8,128)S(1)}, f32[128,256]{1,0:T(8,128)S(1)}, u32[]{:S(2)}, u32[]{:S(2)}) collective-permute-start(f32[128,256]{1,0:T(8,128)S(1)} %get-tuple-element.32), channel_id=1, source_target_pairs={{0,2},{1,3},{2,4},{3,5},{4,6},{5,7},{6,0},{7,1},{8,10},{9,11},{10,... | collective-permute-start | bytes 393224 | tf_op jit(solution)/shard_map/ppermute | solution.py:290
  20.7 0.8 %collective-permute-start.4 = (f32[128,256]{1,0:T(8,128)S(1)}, f32[128,256]{1,0:T(8,128)S(1)}, u32[]{:S(2)}, u32[]{:S(2)}) collective-permute-start(f32[128,256]{1,0:T(8,128)S(1)} %get-tuple-element.33), channel_id=1, source_target_pairs={{0,6},{1,7},{2,0},{3,1},{4,2},{5,3},{6,4},{7,5},{8,14},{9,15},{10,... | collective-permute-start | bytes 393224 | tf_op jit(solution)/shard_map/ppermute | solution.py:290
  21.6 3.4 %collective-permute-done.7.d = f32[128,256]{1,0:T(8,128)S(1)} collective-permute-done((f32[128,256]{1,0:T(8,128)S(1)}, f32[128,256]{1,0:T(8,128)S(1)}, u32[]{:S(2)}, u32[]{:S(2)}) %collective-permute-start.7) | collective-permute-done | bytes 131104 | tf_op jit(solution)/shard_map/ppermute | solution.py:285
  25.0 0.1 collective-permute-start.10
  25.1 0.1 collective-permute-start.9
  25.2 0.7 %collective-permute-done.3.c = f32[128,256]{1,0:T(8,128)S(1)} collective-permute-done((f32[128,256]{1,0:T(8,128)S(1)}, f32[128,256]{1,0:T(8,128)S(1)}, u32[]{:S(2)}, u32[]{:S(2)}) %collective-permute-start.3) | collective-permute-done | bytes 131104 | tf_op jit(solution)/shard_map/ppermute | solution.py:290
  25.9 1.0 %collective-permute-done.4.d = f32[128,256]{1,0:T(8,128)S(1)} collective-permute-done((f32[128,256]{1,0:T(8,128)S(1)}, f32[128,256]{1,0:T(8,128)S(1)}, u32[]{:S(2)}, u32[]{:S(2)}) %collective-permute-start.4) | collective-permute-done | bytes 131104 | tf_op jit(solution)/shard_map/ppermute | solution.py:290
  26.9 2.3 %collective-permute-start.11 = (f32[64,256]{1,0:T(8,128)S(1)}, f32[64,256]{1,0:T(8,128)S(1)}, u32[]{:S(2)}, u32[]{:S(2)}) collective-permute-start(f32[64,256]{1,0:T(8,128)S(1)} %get-tuple-element.41), channel_id=1, source_target_pairs={{0,24},{1,25},{2,26},{3,27},{4,28},{5,29},{6,30},{7,31},{8,0},{9,1... | collective-permute-start | bytes 196616 | tf_op jit(solution)/shard_map/ppermute | solution.py:295
  29.3 1.0 %collective-permute-done.10.c = f32[64,256]{1,0:T(8,128)S(1)} collective-permute-done((f32[64,256]{1,0:T(8,128)S(1)}, f32[64,256]{1,0:T(8,128)S(1)}, u32[]{:S(2)}, u32[]{:S(2)}) %collective-permute-start.10) | collective-permute-done | bytes 65568 | tf_op jit(solution)/shard_map/ppermute | solution.py:292
  30.2 1.5 %collective-permute-done.9.b = f32[64,256]{1,0:T(8,128)S(1)} collective-permute-done((f32[64,256]{1,0:T(8,128)S(1)}, f32[64,256]{1,0:T(8,128)S(1)}, u32[]{:S(2)}, u32[]{:S(2)}) %collective-permute-start.9) | collective-permute-done | bytes 65568 | tf_op jit(solution)/shard_map/ppermute | solution.py:293
  31.7 0.2 collective-permute-done.11.d
  32.0 1.7 %collective-permute-start.12 = (f32[72,256]{1,0:T(8,128)S(1)}, f32[72,256]{1,0:T(8,128)S(1)}, u32[]{:S(2)}, u32[]{:S(2)}) collective-permute-start(f32[72,256]{1,0:T(8,128)S(1)} %shard_map.84.a), channel_id=1, source_target_pairs={{0,32},{32,64},{64,96},{96,0},{128,160},{160,192},{192,224},{224,1... | collective-permute-start | bytes 221192 | tf_op jit(solution)/shard_map/ppermute | solution.py:297
  33.6 2.9 %collective-permute-start.13 = (f32[72,256]{1,0:T(8,128)S(1)}, f32[72,256]{1,0:T(8,128)S(1)}, u32[]{:S(2)}, u32[]{:S(2)}) collective-permute-start(f32[72,256]{1,0:T(8,128)S(1)} %shard_map.84.a), channel_id=1, source_target_pairs={{0,64},{32,96},{64,0},{96,32},{128,192},{160,224},{192,128},{224,1... | collective-permute-start | bytes 221192 | tf_op jit(solution)/shard_map/ppermute | solution.py:297
  36.5 1.3 %collective-permute-start.14 = (f32[72,256]{1,0:T(8,128)S(1)}, f32[72,256]{1,0:T(8,128)S(1)}, u32[]{:S(2)}, u32[]{:S(2)}) collective-permute-start(f32[72,256]{1,0:T(8,128)S(1)} %shard_map.84.a), channel_id=1, source_target_pairs={{0,96},{32,0},{64,32},{96,64},{128,224},{160,128},{192,160},{224,1... | collective-permute-start | bytes 221192 | tf_op jit(solution)/shard_map/ppermute | solution.py:297
  37.9 0.1 collective-permute-done.12.b
  37.9 1.7 %collective-permute-done.13.c = f32[72,256]{1,0:T(8,128)S(1)} collective-permute-done((f32[72,256]{1,0:T(8,128)S(1)}, f32[72,256]{1,0:T(8,128)S(1)}, u32[]{:S(2)}, u32[]{:S(2)}) %collective-permute-start.13) | collective-permute-done | bytes 73760 | tf_op jit(solution)/shard_map/ppermute | solution.py:297
  39.6 1.2 %collective-permute-done.14.d = f32[72,256]{1,0:T(8,128)S(1)} collective-permute-done((f32[72,256]{1,0:T(8,128)S(1)}, f32[72,256]{1,0:T(8,128)S(1)}, u32[]{:S(2)}, u32[]{:S(2)}) %collective-permute-start.14) | collective-permute-done | bytes 73760 | tf_op jit(solution)/shard_map/ppermute | solution.py:297
  40.9 4.4 %collective-permute-start.15 = (f32[72,256]{1,0:T(8,128)S(1)}, f32[72,256]{1,0:T(8,128)S(1)}, u32[]{:S(2)}, u32[]{:S(2)}) collective-permute-start(f32[72,256]{1,0:T(8,128)S(1)} %shard_map.85.mine), channel_id=1, source_target_pairs={{0,128},{32,160},{64,192},{96,224},{128,0},{160,32},{192,64},{224,... | collective-permute-start | bytes 221192 | tf_op jit(solution)/shard_map/ppermute | solution.py:299
  45.3 0.5 shard_map.86.side
  45.8 3.5 %collective-permute-done.15.other = f32[72,256]{1,0:T(8,128)S(1)} collective-permute-done((f32[72,256]{1,0:T(8,128)S(1)}, f32[72,256]{1,0:T(8,128)S(1)}, u32[]{:S(2)}, u32[]{:S(2)}) %collective-permute-start.15) | collective-permute-done | bytes 73760 | tf_op jit(solution)/shard_map/ppermute | solution.py:299
  49.3 1.0 %shard_map.87 = (f32[64,256]{1,0:T(8,128)}, f32[64,256]{1,0:T(8,128)}) custom-call(f32[72,256]{1,0:T(8,128)S(1)} %shard_map.85.mine, f32[72,256]{1,0:T(8,128)S(1)} %collective-permute-done.15.other, f32[64,256]{1,0:T(8,128)S(1)} %shard_map.86.side, f32[64,256]{1,0:T(8,128)S(1)} %get-tuple-element.38.window), custom_call_target="tpu_custom_call" | custom-call | tf_op jit(solution)/shard_map/pallas_call | solution.py:303
  (15 shorter events, 0.1 us)
Async XLA Ops:
  4.8 2.2 %collective-permute-start.1 = (f32[576,256]{1,0:T(8,128)S(1)}, f32[576,256]{1,0:T(8,128)S(1)}, u32[]{:S(2)}, u32[]{:S(2)}) collective-permute-start(f32[576,256]{1,0:T(8,128)S(1)} %get-tuple-element.28), channel_id=1, source_target_pairs={{0,1},{1,0},{2,3},{3,2},{4,5},{5,4},{6,7},{7,6},{8,9},{9,8},{10,11... | collective-permute-start | bytes 1769480 | tf_op jit(solution)/shard_map/ppermute | solution.py:280
  6.4 10.1 %collective-permute-start = (f32[512,256]{1,0:T(8,128)S(1)}, f32[512,256]{1,0:T(8,128)S(1)}, u32[]{:S(2)}, u32[]{:S(2)}) collective-permute-start(f32[512,256]{1,0:T(8,128)S(1)} %shard_map.79), channel_id=1, source_target_pairs={{0,1},{1,0},{2,3},{3,2},{4,5},{5,4},{6,7},{7,6},{8,9},{9,8},{10,11... | collective-permute-start | bytes 1572872 | tf_op jit(solution)/shard_map/ppermute | solution.py:283
  7.1 13.6 %collective-permute-start.5 = (f32[128,256]{1,0:T(8,128)S(1)}, f32[128,256]{1,0:T(8,128)S(1)}, u32[]{:S(2)}, u32[]{:S(2)}) collective-permute-start(f32[128,256]{1,0:T(8,128)S(1)} %get-tuple-element.35), channel_id=1, source_target_pairs={{0,4},{1,5},{2,6},{3,7},{4,0},{5,1},{6,2},{7,3},{8,12},{9,13},{10,... | collective-permute-start | bytes 393224 | tf_op jit(solution)/shard_map/ppermute | solution.py:285
  8.6 10.2 %collective-permute-start.8 = (f32[64,256]{1,0:T(8,128)S(1)}, f32[64,256]{1,0:T(8,128)S(1)}, u32[]{:S(2)}, u32[]{:S(2)}) collective-permute-start(f32[64,256]{1,0:T(8,128)S(1)} %get-tuple-element.38.window), channel_id=1, source_target_pairs={{0,159},{1,2},{2,1},{3,4},{4,3},{5,6},{6,5},{7,8},{8,7},{9,10},{10... | collective-permute-start | bytes 196616 | tf_op jit(solution)/shard_map/ppermute | solution.py:286
  9.6 11.9 %collective-permute-start.6 = (f32[128,256]{1,0:T(8,128)S(1)}, f32[128,256]{1,0:T(8,128)S(1)}, u32[]{:S(2)}, u32[]{:S(2)}) collective-permute-start(f32[128,256]{1,0:T(8,128)S(1)} %get-tuple-element.36), channel_id=1, source_target_pairs={{0,2},{1,3},{2,4},{3,5},{4,6},{5,7},{6,0},{7,1},{8,10},{9,11},{10,... | collective-permute-start | bytes 393224 | tf_op jit(solution)/shard_map/ppermute | solution.py:285
  16.5 8.5 %collective-permute-start.7 = (f32[128,256]{1,0:T(8,128)S(1)}, f32[128,256]{1,0:T(8,128)S(1)}, u32[]{:S(2)}, u32[]{:S(2)}) collective-permute-start(f32[128,256]{1,0:T(8,128)S(1)} %get-tuple-element.37), channel_id=1, source_target_pairs={{0,6},{1,7},{2,0},{3,1},{4,2},{5,3},{6,4},{7,5},{8,14},{9,15},{10,... | collective-permute-start | bytes 393224 | tf_op jit(solution)/shard_map/ppermute | solution.py:285
  16.5 28.8 %copy-start = (s32[64,4]{0,1:T(4,128)S(1)}, s32[64,4]{0,1:T(4,128)}, u32[]{:S(2)}) copy-start(s32[64,4]{0,1:T(4,128)} %param.11) | copy-start | bytes 3076
  16.5 28.8 %copy-start.1 = (f32[64]{0:T(128)S(1)}, f32[64]{0:T(128)}, u32[]{:S(2)}) copy-start(f32[64]{0:T(128)} %param.10) | copy-start | bytes 772
  17.3 7.9 %collective-permute-start.2 = (f32[128,256]{1,0:T(8,128)S(1)}, f32[128,256]{1,0:T(8,128)S(1)}, u32[]{:S(2)}, u32[]{:S(2)}) collective-permute-start(f32[128,256]{1,0:T(8,128)S(1)} %get-tuple-element.31), channel_id=1, source_target_pairs={{0,4},{1,5},{2,6},{3,7},{4,0},{5,1},{6,2},{7,3},{8,12},{9,13},{10,... | collective-permute-start | bytes 393224 | tf_op jit(solution)/shard_map/ppermute | solution.py:290
  18.8 7.0 %collective-permute-start.3 = (f32[128,256]{1,0:T(8,128)S(1)}, f32[128,256]{1,0:T(8,128)S(1)}, u32[]{:S(2)}, u32[]{:S(2)}) collective-permute-start(f32[128,256]{1,0:T(8,128)S(1)} %get-tuple-element.32), channel_id=1, source_target_pairs={{0,2},{1,3},{2,4},{3,5},{4,6},{5,7},{6,0},{7,1},{8,10},{9,11},{10,... | collective-permute-start | bytes 393224 | tf_op jit(solution)/shard_map/ppermute | solution.py:290
  20.7 6.2 %collective-permute-start.4 = (f32[128,256]{1,0:T(8,128)S(1)}, f32[128,256]{1,0:T(8,128)S(1)}, u32[]{:S(2)}, u32[]{:S(2)}) collective-permute-start(f32[128,256]{1,0:T(8,128)S(1)} %get-tuple-element.33), channel_id=1, source_target_pairs={{0,6},{1,7},{2,0},{3,1},{4,2},{5,3},{6,4},{7,5},{8,14},{9,15},{10,... | collective-permute-start | bytes 393224 | tf_op jit(solution)/shard_map/ppermute | solution.py:290
  25.0 5.3 %collective-permute-start.10 = (f32[64,256]{1,0:T(8,128)S(1)}, f32[64,256]{1,0:T(8,128)S(1)}, u32[]{:S(2)}, u32[]{:S(2)}) collective-permute-start(f32[64,256]{1,0:T(8,128)S(1)} %get-tuple-element.40), channel_id=1, source_target_pairs={{0,16},{1,17},{2,18},{3,19},{4,20},{5,21},{6,22},{7,23},{8,24},{9,... | collective-permute-start | bytes 196616 | tf_op jit(solution)/shard_map/ppermute | solution.py:292
  25.1 6.6 %collective-permute-start.9 = (f32[64,256]{1,0:T(8,128)S(1)}, f32[64,256]{1,0:T(8,128)S(1)}, u32[]{:S(2)}, u32[]{:S(2)}) collective-permute-start(f32[64,256]{1,0:T(8,128)S(1)} %get-tuple-element.39), channel_id=1, source_target_pairs={{0,8},{1,9},{2,10},{3,11},{4,12},{5,13},{6,14},{7,15},{8,16},{9,17... | collective-permute-start | bytes 196616 | tf_op jit(solution)/shard_map/ppermute | solution.py:293
  26.9 5.0 %collective-permute-start.11 = (f32[64,256]{1,0:T(8,128)S(1)}, f32[64,256]{1,0:T(8,128)S(1)}, u32[]{:S(2)}, u32[]{:S(2)}) collective-permute-start(f32[64,256]{1,0:T(8,128)S(1)} %get-tuple-element.41), channel_id=1, source_target_pairs={{0,24},{1,25},{2,26},{3,27},{4,28},{5,29},{6,30},{7,31},{8,0},{9,1... | collective-permute-start | bytes 196616 | tf_op jit(solution)/shard_map/ppermute | solution.py:295
  32.0 6.0 %collective-permute-start.12 = (f32[72,256]{1,0:T(8,128)S(1)}, f32[72,256]{1,0:T(8,128)S(1)}, u32[]{:S(2)}, u32[]{:S(2)}) collective-permute-start(f32[72,256]{1,0:T(8,128)S(1)} %shard_map.84.a), channel_id=1, source_target_pairs={{0,32},{32,64},{64,96},{96,0},{128,160},{160,192},{192,224},{224,1... | collective-permute-start | bytes 221192 | tf_op jit(solution)/shard_map/ppermute | solution.py:297
  33.6 6.0 %collective-permute-start.13 = (f32[72,256]{1,0:T(8,128)S(1)}, f32[72,256]{1,0:T(8,128)S(1)}, u32[]{:S(2)}, u32[]{:S(2)}) collective-permute-start(f32[72,256]{1,0:T(8,128)S(1)} %shard_map.84.a), channel_id=1, source_target_pairs={{0,64},{32,96},{64,0},{96,32},{128,192},{160,224},{192,128},{224,1... | collective-permute-start | bytes 221192 | tf_op jit(solution)/shard_map/ppermute | solution.py:297
  36.5 4.4 %collective-permute-start.14 = (f32[72,256]{1,0:T(8,128)S(1)}, f32[72,256]{1,0:T(8,128)S(1)}, u32[]{:S(2)}, u32[]{:S(2)}) collective-permute-start(f32[72,256]{1,0:T(8,128)S(1)} %shard_map.84.a), channel_id=1, source_target_pairs={{0,96},{32,0},{64,32},{96,64},{128,224},{160,128},{192,160},{224,1... | collective-permute-start | bytes 221192 | tf_op jit(solution)/shard_map/ppermute | solution.py:297
  40.9 8.3 %collective-permute-start.15 = (f32[72,256]{1,0:T(8,128)S(1)}, f32[72,256]{1,0:T(8,128)S(1)}, u32[]{:S(2)}, u32[]{:S(2)}) collective-permute-start(f32[72,256]{1,0:T(8,128)S(1)} %shard_map.85.mine), channel_id=1, source_target_pairs={{0,128},{32,160},{64,192},{96,224},{128,0},{160,32},{192,64},{224,... | collective-permute-start | bytes 221192 | tf_op jit(solution)/shard_map/ppermute | solution.py:299

commit v6 on v3

--- a/solution.py
+++ b/solution.py
@@ -12,9 +12,7 @@
 F32 = jnp.float32
 VMEM = pltpu.VMEM
 PART = 2 * NX * ROWS
-FIRST, SECOND = (2, 1), (3, 0)
 PRODUCT_FLOPS = 2 * PART * 2048 * 16
-PAUSE_FLOPS = 4 * 10**9
 POWER_SCALE = 6.0 * 15.0 / math.pi**4 / 300.0**4
 LOG2E = 1.0 / math.log(2.0)
 PARAMS = dict(vmem_limit_bytes=24 * 2**20)
@@ -31,6 +29,14 @@
 def place():
     row = lax.axis_index("row")
     return row // (2 * NX), (row // 2) % NX, row % 2
+
+
+def ahead(core):
+    return 1 + 2 * core
+
+
+def z_offsets(core):
+    return (2, ahead(core)), (4 - ahead(core), 0)
 
 
 def edge_terms(a):
@@ -78,13 +84,15 @@
         for i in range(4)
     ]
     gcopies = [
-        fetch_rows(g_hbm, gbuf, gsem.at[0], z, 1 - core, FIRST),
-        fetch_rows(g_hbm, g1, gsem.at[1], z, 1 - core, SECOND),
-        fetch_rows(g_hbm, g2, gsem.at[2], z, core, FIRST),
-        fetch_rows(g_hbm, g3, gsem.at[3], z, core, SECOND),
+        fetch_rows(g_hbm, gbuf, gsem.at[0], z, 1 - core, z_offsets(1 - core)[0]),
+        fetch_rows(g_hbm, g1, gsem.at[1], z, 1 - core, z_offsets(1 - core)[1]),
+        fetch_rows(g_hbm, g2, gsem.at[2], z, core, z_offsets(core)[0]),
+        fetch_rows(g_hbm, g3, gsem.at[3], z, core, z_offsets(core)[1]),
     ]
     for c in small + tcopies:
         c.start()
+    for c in gcopies[0] + gcopies[2] + gcopies[1] + gcopies[3]:
+        c.start(priority=1)
     for c in small:
         c.wait()
     a_lo = 14388000.0 / jnp.full((1, 512), edges[0, 0].astype(F32))
@@ -97,9 +105,6 @@
     lo, hi = edge_terms(a_lo), edge_terms(a_hi)
     for i in range(4):
         tcopies[i].wait()
-        if i == 1:
-            for c in gcopies[0] + gcopies[1] + gcopies[2] + gcopies[3]:
-                c.start()
 
         @pl.loop(0, part // 16)
         def _(j):
@@ -127,14 +132,15 @@
 
 def spread(value, outs):
     z, x, core = place()
-    for d in range(NX):
+    for out, d in zip(outs, (0, ahead(core), 2, 4 - ahead(core))):
         for i in range(2):
             rows = pl.ds(pl.multiple_of((i * NX + (x + d) % NX) * ROWS, ROWS), ROWS)
-            outs[d][i * ROWS : (i + 1) * ROWS] = value(rows)
+            out[i * ROWS : (i + 1) * ROWS] = value(rows)
 
 
 def add_kernel(t, u, *outs):
-    spread(lambda rows: t[rows] + u[rows], outs)
+    spread(lambda rows: t[rows] + u[rows], outs[:NX])
+    outs[1][2 * ROWS :] = u[PART:]
     outs[NX][...] = u[PART:]
 
 
@@ -144,19 +150,27 @@
     spread(lambda rows: t[rows] + u[rows], outs)
 
 
-def x_sum_carry_kernel(a, b, c, d, win, *outs):
-    x_sum_kernel(a, b, c, d, *outs)
-    outs[2][...] = win[...]
-
-
 def x_sum_kernel(a, b, c, d, *outs):
     for i in range(2):
         rows = pl.ds(i * ROWS, ROWS)
-        outs[i][...] = (a[rows] + b[rows]) + (c[rows] + d[rows])
-
-
-def z_sum_kernel(a, b, c, d, par, cross, out):
-    out[:ROWS] = (a[...] + b[...]) + (c[...] + d[...])
+        outs[i][:ROWS] = (a[rows] + b[rows]) + (c[rows] + d[rows])
+
+
+def x_sum_carry_kernel(a, b, c, d, *outs):
+    x_sum_kernel(a, b, c, d, *outs)
+    outs[1][ROWS:] = b[2 * ROWS :]
+
+
+def x_sum_rest_kernel(a, b, c, d, after, *outs):
+    x_sum_kernel(a, b, c, d, *outs)
+
+
+def z_part_kernel(a, b, c, out):
+    out[...] = (a[...] + b[:ROWS]) + c[...]
+
+
+def z_sum_kernel(a, b, par, out):
+    out[:ROWS] = a[...] + b[...]
     out[ROWS:] = par[...]
 
 
@@ -181,7 +195,7 @@
     return total
 
 
-def side_kernel(neighbours, conductance, swapped, window, cross, mine, out):
+def side_kernel(neighbours, conductance, swapped, window, by_x, by_z, mine, out):
     z, x, core = place()
     me = (z * NX + x) * 2 + core
     total = 32 * ROWS
@@ -190,8 +204,9 @@
     local = jnp.where(local >= total, local - total, local)
     row = lax.broadcasted_iota(jnp.int32, (ROWS, ROWS), 0)
     lane = lax.broadcasted_iota(jnp.int32, (ROWS, ROWS), 1)
-    low = jnp.where(core == 0, cross[...], swapped[...])
-    high = jnp.where(core == 0, swapped[...], cross[...])
+    cross = jnp.where(x == 3 * core, by_z[ROWS:], by_x[2 * ROWS :])
+    low = jnp.where(core == 0, cross, swapped[...])
+    high = jnp.where(core == 0, swapped[...], cross)
     acc = -emitted(mine[ROWS:], window[...])
     for i, block in enumerate((low, window[...], high)):
         count = jnp.where(row == lane, -4.0, 0.0) if i == 1 else jnp.zeros((ROWS, ROWS), F32)
@@ -236,9 +251,12 @@
 
 
 CORE = row_perm(lambda z, x, c: (z, x, 1 - c))
-XS = [row_perm(lambda z, x, c, d=d: (z, (x + d) % NX, c)) for d in range(NX)]
-ZS = [row_perm(lambda z, x, c, d=d: ((z + d) % NZ, x, c)) for d in range(NZ)]
-CROSS = [(i, (i + 1 if i % 2 else i - 1) % 32) for i in range(32)]
+X2 = row_perm(lambda z, x, c: (z, (x + 2) % NX, c))
+XF = row_perm(lambda z, x, c: (z, (x + 1 + 2 * c) % NX, c))
+XB = row_perm(lambda z, x, c: (z, (x + 3 - 2 * c) % NX, c))
+Z2 = row_perm(lambda z, x, c: ((z + 2) % NZ, x, c))
+ZF = row_perm(lambda z, x, c: ((z + 1 + 2 * c) % NZ, x, c))
+ZB = row_perm(lambda z, x, c: ((z + 3 - 2 * c) % NZ, x, c))
 YS = [[(h * NY + y, h * NY + (y + d) % NY) for h in range(2) for y in range(NY)] for d in range(NY)]
 HI = [(i, (i + NY) % (2 * NY)) for i in range(2 * NY)]
 
@@ -255,7 +273,6 @@
     rows = sds(2, NX, ROWS, panels, dtype=bf)
     pair = sds(2 * ROWS, orbits)
     cost = pl.CostEstimate(flops=PRODUCT_FLOPS, bytes_accessed=0, transcendentals=0)
-    pause = pl.CostEstimate(flops=PAUSE_FLOPS, bytes_accessed=0, transcendentals=0)
     far = [
         pltpu.with_memory_space_constraint(a, pltpu.HBM)
         for a in (band_edges, emissivity, temps, g)
@@ -280,24 +297,27 @@
     t_a = call(product_kernel, 2, sds(PART, orbits), cost=cost)(p, g2)
     u_b = call(product_kernel, 3, sds(PART, orbits), cost=cost)(p, g1, t_a)
     u_b = lax.ppermute(u_b, "row", CORE)
-    *s_a, swapped = call(add_kernel, 2, [pair] * NX + [block])(t_a, u_a)
-    x_a = [lax.ppermute(s_a[d], "row", XS[d]) for d in (2, 1, 3)]
+    long = sds(3 * ROWS, orbits)
+    *s_a, swapped = call(add_kernel, 2, [pair, long, pair, pair, block])(t_a, u_a)
+    x_a = [lax.ppermute(s_a[i], "row", perm) for i, perm in ((2, X2), (1, XF), (3, XB))]
     s_b = call(product_add_kernel, 4, [pair] * NX, scratch=[VMEM((PART, orbits), F32)], cost=cost)(
         p, g3, u_b, s_a[0]
     )
-    x_b = [lax.ppermute(s_b[d], "row", XS[d]) for d in (2, 1, 3)]
-    z2, z1, win = call(x_sum_carry_kernel, 5, [block] * 3)(s_a[0], *x_a, win)
-    z2 = lax.ppermute(z2, "row", ZS[2])
-    z1 = lax.ppermute(z1, "row", ZS[1])
-    cross = lax.ppermute(win, "row", CROSS)
-    z3, z0 = call(x_sum_kernel, 4, [block] * 2, cost=pause)(s_b[0], *x_b)
-    z3 = lax.ppermute(z3, "row", ZS[3])
-    zsum = call(z_sum_kernel, 6, message)(z0, z1, z2, z3, par, cross)
-    y_in = [lax.ppermute(zsum, "band", YS[d]) for d in (1, 2, 3)]
+    x_b = [lax.ppermute(s_b[i], "row", perm) for i, perm in ((2, X2), (1, XF), (3, XB))]
+    z2, zf = call(x_sum_carry_kernel, 4, [block, pair])(s_a[0], x_a[1], x_a[0], x_a[2])
+    z2_out = z2
+    z2 = lax.ppermute(z2, "row", Z2)
+    zf = lax.ppermute(zf, "row", ZF)
+    zb, z0 = call(x_sum_rest_kernel, 5, [block] * 2)(s_b[0], x_b[1], x_b[0], x_b[2], z2_out)
+    zb = lax.ppermute(zb, "row", ZB)
+    zsum = call(z_part_kernel, 3, block)(z0, zf, z2)
+    zsum = call(z_sum_kernel, 3, message)(zsum, zb, par)
+    y_in = [lax.ppermute(zsum, "band", YS[d]) for d in (3, 1, 2)]
+
     mine = call(y_sum_kernel, 4, message)(zsum, *y_in)
     other = lax.ppermute(mine, "band", HI)
-    side = call(side_kernel, 6, block)(
-        neighbours.T, conductance.reshape(1, ROWS), swapped, win, cross, mine
+    side = call(side_kernel, 7, block)(
+        neighbours.T, conductance.reshape(1, ROWS), swapped, win, x_a[1], zf, mine
     )
     absorbed, heating = call(last_kernel, 4, [block] * 2)(mine, other, side, win)
     return absorbed.T, heating.T

time: 51.2 us -> 49.9 us (0.975)
  the two profiles are of different devices: /device:TPU:6 before, /device:TPU:28 now
where the time goes in v6:
time: 49.9 us; the launch traced here: 49.8 us
  starting transfers between devices  27.1 us (54%)
  waiting for transfers between devices  13.9 us (28%)
  Pallas kernels  8.1 us (16%)
  between operations  0.72 us (1%)
    ppermute x3, starting transfers between devices, body(): lax.ppermute(s_b[i], 'row', perm)  6.67 us
    ppermute x3, waiting for transfers between devices, body(): y_in = [lax.ppermute(zsum, 'band', YS[d]) for d in (3, 1, 2)]  5.56 us
    ppermute x1, starting transfers between devices, body(): other = lax.ppermute(mine, 'band', HI)  5.31 us
    pallas_call x1, Pallas kernels, body(): call(first_kernel, 4, [sds(PART + ROWS, orbits), sds(orbits, panels, dtyp...  4.18 us
    ppermute x3, starting transfers between devices, body(): y_in = [lax.ppermute(zsum, 'band', YS[d]) for d in (3, 1, 2)]  3.51 us
    ppermute x1, waiting for transfers between devices, body(): other = lax.ppermute(mine, 'band', HI)  3.27 us
    ppermute x1, starting transfers between devices, body(): z2 = lax.ppermute(z2, 'row', Z2)  3.27 us
    ppermute x1, starting transfers between devices, body(): zb = lax.ppermute(zb, 'row', ZB)  2.98 us
  transfers between devices with their start and end apart: 15, of which 7 were waited for; matrix products, arithmetic and copies ran while one was open for 0% of the time, Pallas kernels for 6%

profile of v6, /device:TPU:28, one launch (start us, length us, event | category | flops | bytes accessed | tf_op | source)
XLA Modules:
  0.0 49.8 jit_solution(714594434522431320)
XLA Ops:
  0.6 4.2 %shard_map.77 = (f32[576,256]{1,0:T(8,128)S(1)}, bf16[256,2048]{1,0:T(8,128)(2,1)S(1)}, bf16[2,4,64,2048]{3,2,1,0:T(8,128)(2,1)S(1)}, bf16[2,4,64,2048]{3,2,1,0:...) custom-call(s32[1,2]{1,0:T(1,128)} %edges_hbm.1, ...), custom_call_target="tpu_custom_call" | custom-call | flops 33554432 | tf_op jit(solution)/shard_map/pallas_call | solution.py:280
  4.8 0.1 collective-permute-start.1
  4.9 0.7 %shard_map.78.refs_0_.t = f32[512,256]{1,0:T(8,128)S(1)} custom-call(bf16[256,2048]{1,0:T(8,128)(2,1)S(1)} %get-tuple-element.24.p, bf16[2,4,64,2048]{3,2,1,0:T(8,128)(2,1)S(1)} %get-tuple-element.27.g), custom_call_target="tpu_custom_call" | custom-call | flops 33554432 | tf_op jit(solution)/shard_map/pallas_call | solution.py:297
  5.7 0.7 %shard_map.79 = f32[512,256]{1,0:T(8,128)S(1)} custom-call(bf16[256,2048]{1,0:T(8,128)(2,1)S(1)} %get-tuple-element.24.p, bf16[2,4,64,2048]{3,2,1,0:T(8,128)(2,1)S(1)} %get-tuple-element.26.g, f32[512,256]{1,0:T(8,128)S(1)} %shard_map.78.refs_0_.t), custom_call_target="tpu_custom_call" | custom-call | flops 33554432 | tf_op jit(solution)/shard_map/pallas_call | solution.py:298
  6.4 0.6 %collective-permute-start = (f32[512,256]{1,0:T(8,128)S(1)}, f32[512,256]{1,0:T(8,128)S(1)}, u32[]{:S(2)}, u32[]{:S(2)}) collective-permute-start(f32[512,256]{1,0:T(8,128)S(1)} %shard_map.79), channel_id=1, source_target_pairs={{0,1},{1,0},{2,3},{3,2},{4,5},{5,4},{6,7},{7,6},{8,9},{9,8},{10,11... | collective-permute-start | bytes 1572872 | tf_op jit(solution)/shard_map/ppermute | solution.py:299
  7.0 0.0 collective-permute-done.1.u
  7.0 0.1 shard_map.80
  7.1 0.6 %collective-permute-start.6 = (f32[128,256]{1,0:T(8,128)S(1)}, f32[128,256]{1,0:T(8,128)S(1)}, u32[]{:S(2)}, u32[]{:S(2)}) collective-permute-start(f32[128,256]{1,0:T(8,128)S(1)} %get-tuple-element.35), channel_id=1, source_target_pairs={{0,4},{1,5},{2,6},{3,7},{4,0},{5,1},{6,2},{7,3},{8,12},{9,13},{10,... | collective-permute-start | bytes 393224 | tf_op jit(solution)/shard_map/ppermute | solution.py:302
  7.7 2.1 %collective-permute-start.5 = (f32[192,256]{1,0:T(8,128)S(1)}, f32[192,256]{1,0:T(8,128)S(1)}, u32[]{:S(2)}, u32[]{:S(2)}) collective-permute-start(f32[192,256]{1,0:T(8,128)S(1)} %get-tuple-element.34), channel_id=1, source_target_pairs={{0,2},{1,7},{2,4},{3,1},{4,6},{5,3},{6,0},{7,5},{8,10},{9,15},{10,... | collective-permute-start | bytes 589832 | tf_op jit(solution)/shard_map/ppermute | solution.py:302
  9.8 0.1 collective-permute-start.7
  9.8 0.0 collective-permute-done.u
  9.9 0.8 %shard_map.81 = (f32[128,256]{1,0:T(8,128)S(1)}, f32[128,256]{1,0:T(8,128)S(1)}, f32[128,256]{1,0:T(8,128)S(1)}, f32[128,256]{1,0:T(8,128)S(1)}) custom-call(bf16[256,2048]{1,0:T(8,128)(2,1)S(1)} %get-tuple-element.24.p, bf16[2,4,64,2048]{3,2,1,0:T(8,128)(2,1)S(1)} %get-tuple-element.25.g, f32[512,256]{1,0:T(8,128)S(1)} %collective-permute-done.u, ...), custom_call_target="tpu_custom_call" | custom-call | flops 33554432 | tf_op jit(solution)/shard_map/pallas_call | solution.py:303
  10.6 2.1 %collective-permute-start.2 = (f32[128,256]{1,0:T(8,128)S(1)}, f32[128,256]{1,0:T(8,128)S(1)}, u32[]{:S(2)}, u32[]{:S(2)}) collective-permute-start(f32[128,256]{1,0:T(8,128)S(1)} %get-tuple-element.31), channel_id=1, source_target_pairs={{0,2},{1,7},{2,4},{3,1},{4,6},{5,3},{6,0},{7,5},{8,10},{9,15},{10,... | collective-permute-start | bytes 393224 | tf_op jit(solution)/shard_map/ppermute | solution.py:306
  12.8 2.1 %collective-permute-start.3 = (f32[128,256]{1,0:T(8,128)S(1)}, f32[128,256]{1,0:T(8,128)S(1)}, u32[]{:S(2)}, u32[]{:S(2)}) collective-permute-start(f32[128,256]{1,0:T(8,128)S(1)} %get-tuple-element.32), channel_id=1, source_target_pairs={{0,4},{1,5},{2,6},{3,7},{4,0},{5,1},{6,2},{7,3},{8,12},{9,13},{10,... | collective-permute-start | bytes 393224 | tf_op jit(solution)/shard_map/ppermute | solution.py:306
  14.9 0.1 collective-permute-done.6.c
  15.1 2.4 %collective-permute-start.4 = (f32[128,256]{1,0:T(8,128)S(1)}, f32[128,256]{1,0:T(8,128)S(1)}, u32[]{:S(2)}, u32[]{:S(2)}) collective-permute-start(f32[128,256]{1,0:T(8,128)S(1)} %get-tuple-element.33), channel_id=1, source_target_pairs={{0,6},{1,3},{2,0},{3,5},{4,2},{5,7},{6,4},{7,1},{8,14},{9,11},{10,... | collective-permute-start | bytes 393224 | tf_op jit(solution)/shard_map/ppermute | solution.py:306
  17.5 2.2 %collective-permute-done.5.b.by_x = f32[192,256]{1,0:T(8,128)S(1)} collective-permute-done((f32[192,256]{1,0:T(8,128)S(1)}, f32[192,256]{1,0:T(8,128)S(1)}, u32[]{:S(2)}, u32[]{:S(2)}) %collective-permute-start.5) | collective-permute-done | bytes 196640 | tf_op jit(solution)/shard_map/ppermute | solution.py:302
  19.7 2.0 %collective-permute-start.8 = (f32[128,256]{1,0:T(8,128)S(1)}, f32[128,256]{1,0:T(8,128)S(1)}, u32[]{:S(2)}, u32[]{:S(2)}) collective-permute-start(f32[128,256]{1,0:T(8,128)S(1)} %get-tuple-element.39), channel_id=1, source_target_pairs={{0,8},{1,25},{2,10},{3,27},{4,12},{5,29},{6,14},{7,31},{8,16},{9,1... | collective-permute-start | bytes 393224 | tf_op jit(solution)/shard_map/ppermute | solution.py:310
  21.7 3.3 %collective-permute-start.9 = (f32[64,256]{1,0:T(8,128)S(1)}, f32[64,256]{1,0:T(8,128)S(1)}, u32[]{:S(2)}, u32[]{:S(2)}) collective-permute-start(f32[64,256]{1,0:T(8,128)S(1)} %get-tuple-element.37.after), channel_id=1, source_target_pairs={{0,16},{1,17},{2,18},{3,19},{4,20},{5,21},{6,22},{7,23},{8,24},{9,... | collective-permute-start | bytes 196616 | tf_op jit(solution)/shard_map/ppermute | solution.py:309
  25.0 3.0 %collective-permute-start.10 = (f32[64,256]{1,0:T(8,128)S(1)}, f32[64,256]{1,0:T(8,128)S(1)}, u32[]{:S(2)}, u32[]{:S(2)}) collective-permute-start(f32[64,256]{1,0:T(8,128)S(1)} %get-tuple-element.40), channel_id=1, source_target_pairs={{0,24},{1,9},{2,26},{3,11},{4,28},{5,13},{6,30},{7,15},{8,0},{9,17... | collective-permute-start | bytes 196616 | tf_op jit(solution)/shard_map/ppermute | solution.py:312
  28.0 2.3 %collective-permute-done.9.c = f32[64,256]{1,0:T(8,128)S(1)} collective-permute-done((f32[64,256]{1,0:T(8,128)S(1)}, f32[64,256]{1,0:T(8,128)S(1)}, u32[]{:S(2)}, u32[]{:S(2)}) %collective-permute-start.9) | collective-permute-done | bytes 65568 | tf_op jit(solution)/shard_map/ppermute | solution.py:309
  30.3 0.0 collective-permute-done.8.b.by_z
  30.3 0.4 collective-permute-done.10.b
  30.7 1.3 %collective-permute-start.13 = (f32[72,256]{1,0:T(8,128)S(1)}, f32[72,256]{1,0:T(8,128)S(1)}, u32[]{:S(2)}, u32[]{:S(2)}) collective-permute-start(f32[72,256]{1,0:T(8,128)S(1)} %shard_map.85.a), channel_id=1, source_target_pairs={{0,64},{32,96},{64,0},{96,32},{128,192},{160,224},{192,128},{224,1... | collective-permute-start | bytes 221192 | tf_op jit(solution)/shard_map/ppermute | solution.py:315
  32.0 2.2 %collective-permute-start.12 = (f32[72,256]{1,0:T(8,128)S(1)}, f32[72,256]{1,0:T(8,128)S(1)}, u32[]{:S(2)}, u32[]{:S(2)}) collective-permute-start(f32[72,256]{1,0:T(8,128)S(1)} %shard_map.85.a), channel_id=1, source_target_pairs={{0,32},{32,64},{64,96},{96,0},{128,160},{160,192},{192,224},{224,1... | collective-permute-start | bytes 221192 | tf_op jit(solution)/shard_map/ppermute | solution.py:315
  34.2 3.1 %collective-permute-done.13.d = f32[72,256]{1,0:T(8,128)S(1)} collective-permute-done((f32[72,256]{1,0:T(8,128)S(1)}, f32[72,256]{1,0:T(8,128)S(1)}, u32[]{:S(2)}, u32[]{:S(2)}) %collective-permute-start.13) | collective-permute-done | bytes 73760 | tf_op jit(solution)/shard_map/ppermute | solution.py:315
  37.4 0.0 collective-permute-done.12.c
  37.4 2.4 %collective-permute-done.11.b = f32[72,256]{1,0:T(8,128)S(1)} collective-permute-done((f32[72,256]{1,0:T(8,128)S(1)}, f32[72,256]{1,0:T(8,128)S(1)}, u32[]{:S(2)}, u32[]{:S(2)}) %collective-permute-start.11) | collective-permute-done | bytes 73760 | tf_op jit(solution)/shard_map/ppermute | solution.py:315
  39.8 5.3 %collective-permute-start.14 = (f32[72,256]{1,0:T(8,128)S(1)}, f32[72,256]{1,0:T(8,128)S(1)}, u32[]{:S(2)}, u32[]{:S(2)}) collective-permute-start(f32[72,256]{1,0:T(8,128)S(1)} %shard_map.86.mine), channel_id=1, source_target_pairs={{0,128},{32,160},{64,192},{96,224},{128,0},{160,32},{192,64},{224,... | collective-permute-start | bytes 221192 | tf_op jit(solution)/shard_map/ppermute | solution.py:318
  45.1 0.5 shard_map.87.side
  45.6 3.3 %collective-permute-done.14.other = f32[72,256]{1,0:T(8,128)S(1)} collective-permute-done((f32[72,256]{1,0:T(8,128)S(1)}, f32[72,256]{1,0:T(8,128)S(1)}, u32[]{:S(2)}, u32[]{:S(2)}) %collective-permute-start.14) | collective-permute-done | bytes 73760 | tf_op jit(solution)/shard_map/ppermute | solution.py:318
  48.9 1.0 %shard_map.88 = (f32[64,256]{1,0:T(8,128)}, f32[64,256]{1,0:T(8,128)}) custom-call(f32[72,256]{1,0:T(8,128)S(1)} %shard_map.86.mine, f32[72,256]{1,0:T(8,128)S(1)} %collective-permute-done.14.other, f32[64,256]{1,0:T(8,128)S(1)} %shard_map.87.side, f32[64,256]{1,0:T(8,128)S(1)} %get-tuple-element.43.window), custom_call_target="tpu_custom_call" | custom-call | tf_op jit(solution)/shard_map/pallas_call | solution.py:322
  (14 shorter events, 0.1 us)
Async XLA Ops:
  4.8 2.2 %collective-permute-start.1 = (f32[576,256]{1,0:T(8,128)S(1)}, f32[576,256]{1,0:T(8,128)S(1)}, u32[]{:S(2)}, u32[]{:S(2)}) collective-permute-start(f32[576,256]{1,0:T(8,128)S(1)} %get-tuple-element.28), channel_id=1, source_target_pairs={{0,1},{1,0},{2,3},{3,2},{4,5},{5,4},{6,7},{7,6},{8,9},{9,8},{10,11... | collective-permute-start | bytes 1769480 | tf_op jit(solution)/shard_map/ppermute | solution.py:296
  6.4 3.4 %collective-permute-start = (f32[512,256]{1,0:T(8,128)S(1)}, f32[512,256]{1,0:T(8,128)S(1)}, u32[]{:S(2)}, u32[]{:S(2)}) collective-permute-start(f32[512,256]{1,0:T(8,128)S(1)} %shard_map.79), channel_id=1, source_target_pairs={{0,1},{1,0},{2,3},{3,2},{4,5},{5,4},{6,7},{7,6},{8,9},{9,8},{10,11... | collective-permute-start | bytes 1572872 | tf_op jit(solution)/shard_map/ppermute | solution.py:299
  7.1 8.0 %collective-permute-start.6 = (f32[128,256]{1,0:T(8,128)S(1)}, f32[128,256]{1,0:T(8,128)S(1)}, u32[]{:S(2)}, u32[]{:S(2)}) collective-permute-start(f32[128,256]{1,0:T(8,128)S(1)} %get-tuple-element.35), channel_id=1, source_target_pairs={{0,4},{1,5},{2,6},{3,7},{4,0},{5,1},{6,2},{7,3},{8,12},{9,13},{10,... | collective-permute-start | bytes 393224 | tf_op jit(solution)/shard_map/ppermute | solution.py:302
  7.7 12.0 %collective-permute-start.5 = (f32[192,256]{1,0:T(8,128)S(1)}, f32[192,256]{1,0:T(8,128)S(1)}, u32[]{:S(2)}, u32[]{:S(2)}) collective-permute-start(f32[192,256]{1,0:T(8,128)S(1)} %get-tuple-element.34), channel_id=1, source_target_pairs={{0,2},{1,7},{2,4},{3,1},{4,6},{5,3},{6,0},{7,5},{8,10},{9,15},{10,... | collective-permute-start | bytes 589832 | tf_op jit(solution)/shard_map/ppermute | solution.py:302
  9.8 7.7 %collective-permute-start.7 = (f32[128,256]{1,0:T(8,128)S(1)}, f32[128,256]{1,0:T(8,128)S(1)}, u32[]{:S(2)}, u32[]{:S(2)}) collective-permute-start(f32[128,256]{1,0:T(8,128)S(1)} %get-tuple-element.36), channel_id=1, source_target_pairs={{0,6},{1,3},{2,0},{3,5},{4,2},{5,7},{6,4},{7,1},{8,14},{9,11},{10,... | collective-permute-start | bytes 393224 | tf_op jit(solution)/shard_map/ppermute | solution.py:302
  9.8 35.3 %copy-start = (s32[64,4]{0,1:T(4,128)S(1)}, s32[64,4]{0,1:T(4,128)}, u32[]{:S(2)}) copy-start(s32[64,4]{0,1:T(4,128)} %param.11) | copy-start | bytes 3076
  9.8 35.3 %copy-start.1 = (f32[64]{0:T(128)S(1)}, f32[64]{0:T(128)}, u32[]{:S(2)}) copy-start(f32[64]{0:T(128)} %param.10) | copy-start | bytes 772
  10.6 14.4 %collective-permute-start.2 = (f32[128,256]{1,0:T(8,128)S(1)}, f32[128,256]{1,0:T(8,128)S(1)}, u32[]{:S(2)}, u32[]{:S(2)}) collective-permute-start(f32[128,256]{1,0:T(8,128)S(1)} %get-tuple-element.31), channel_id=1, source_target_pairs={{0,2},{1,7},{2,4},{3,1},{4,6},{5,3},{6,0},{7,5},{8,10},{9,15},{10,... | collective-permute-start | bytes 393224 | tf_op jit(solution)/shard_map/ppermute | solution.py:306
  12.8 12.2 %collective-permute-start.3 = (f32[128,256]{1,0:T(8,128)S(1)}, f32[128,256]{1,0:T(8,128)S(1)}, u32[]{:S(2)}, u32[]{:S(2)}) collective-permute-start(f32[128,256]{1,0:T(8,128)S(1)} %get-tuple-element.32), channel_id=1, source_target_pairs={{0,4},{1,5},{2,6},{3,7},{4,0},{5,1},{6,2},{7,3},{8,12},{9,13},{10,... | collective-permute-start | bytes 393224 | tf_op jit(solution)/shard_map/ppermute | solution.py:306
  15.1 9.9 %collective-permute-start.4 = (f32[128,256]{1,0:T(8,128)S(1)}, f32[128,256]{1,0:T(8,128)S(1)}, u32[]{:S(2)}, u32[]{:S(2)}) collective-permute-start(f32[128,256]{1,0:T(8,128)S(1)} %get-tuple-element.33), channel_id=1, source_target_pairs={{0,6},{1,3},{2,0},{3,5},{4,2},{5,7},{6,4},{7,1},{8,14},{9,11},{10,... | collective-permute-start | bytes 393224 | tf_op jit(solution)/shard_map/ppermute | solution.py:306
  19.7 10.6 %collective-permute-start.8 = (f32[128,256]{1,0:T(8,128)S(1)}, f32[128,256]{1,0:T(8,128)S(1)}, u32[]{:S(2)}, u32[]{:S(2)}) collective-permute-start(f32[128,256]{1,0:T(8,128)S(1)} %get-tuple-element.39), channel_id=1, source_target_pairs={{0,8},{1,25},{2,10},{3,27},{4,12},{5,29},{6,14},{7,31},{8,16},{9,1... | collective-permute-start | bytes 393224 | tf_op jit(solution)/shard_map/ppermute | solution.py:310
  21.7 8.6 %collective-permute-start.9 = (f32[64,256]{1,0:T(8,128)S(1)}, f32[64,256]{1,0:T(8,128)S(1)}, u32[]{:S(2)}, u32[]{:S(2)}) collective-permute-start(f32[64,256]{1,0:T(8,128)S(1)} %get-tuple-element.37.after), channel_id=1, source_target_pairs={{0,16},{1,17},{2,18},{3,19},{4,20},{5,21},{6,22},{7,23},{8,24},{9,... | collective-permute-start | bytes 196616 | tf_op jit(solution)/shard_map/ppermute | solution.py:309
  25.0 5.6 %collective-permute-start.10 = (f32[64,256]{1,0:T(8,128)S(1)}, f32[64,256]{1,0:T(8,128)S(1)}, u32[]{:S(2)}, u32[]{:S(2)}) collective-permute-start(f32[64,256]{1,0:T(8,128)S(1)} %get-tuple-element.40), channel_id=1, source_target_pairs={{0,24},{1,9},{2,26},{3,11},{4,28},{5,13},{6,30},{7,15},{8,0},{9,17... | collective-permute-start | bytes 196616 | tf_op jit(solution)/shard_map/ppermute | solution.py:312
  30.7 6.7 %collective-permute-start.13 = (f32[72,256]{1,0:T(8,128)S(1)}, f32[72,256]{1,0:T(8,128)S(1)}, u32[]{:S(2)}, u32[]{:S(2)}) collective-permute-start(f32[72,256]{1,0:T(8,128)S(1)} %shard_map.85.a), channel_id=1, source_target_pairs={{0,64},{32,96},{64,0},{96,32},{128,192},{160,224},{192,128},{224,1... | collective-permute-start | bytes 221192 | tf_op jit(solution)/shard_map/ppermute | solution.py:315
  32.0 5.3 %collective-permute-start.12 = (f32[72,256]{1,0:T(8,128)S(1)}, f32[72,256]{1,0:T(8,128)S(1)}, u32[]{:S(2)}, u32[]{:S(2)}) collective-permute-start(f32[72,256]{1,0:T(8,128)S(1)} %shard_map.85.a), channel_id=1, source_target_pairs={{0,32},{32,64},{64,96},{96,0},{128,160},{160,192},{192,224},{224,1... | collective-permute-start | bytes 221192 | tf_op jit(solution)/shard_map/ppermute | solution.py:315
  34.2 5.6 %collective-permute-start.11 = (f32[72,256]{1,0:T(8,128)S(1)}, f32[72,256]{1,0:T(8,128)S(1)}, u32[]{:S(2)}, u32[]{:S(2)}) collective-permute-start(f32[72,256]{1,0:T(8,128)S(1)} %shard_map.85.a), channel_id=1, source_target_pairs={{0,96},{32,0},{64,32},{96,64},{128,224},{160,128},{192,160},{224,1... | collective-permute-start | bytes 221192 | tf_op jit(solution)/shard_map/ppermute | solution.py:315
  39.8 9.1 %collective-permute-start.14 = (f32[72,256]{1,0:T(8,128)S(1)}, f32[72,256]{1,0:T(8,128)S(1)}, u32[]{:S(2)}, u32[]{:S(2)}) collective-permute-start(f32[72,256]{1,0:T(8,128)S(1)} %shard_map.86.mine), channel_id=1, source_target_pairs={{0,128},{32,160},{64,192},{96,224},{128,0},{160,32},{192,64},{224,... | collective-permute-start | bytes 221192 | tf_op jit(solution)/shard_map/ppermute | solution.py:318

commit v7 on v6

--- a/solution.py
+++ b/solution.py
@@ -312,7 +312,7 @@
     zb = lax.ppermute(zb, "row", ZB)
     zsum = call(z_part_kernel, 3, block)(z0, zf, z2)
     zsum = call(z_sum_kernel, 3, message)(zsum, zb, par)
-    y_in = [lax.ppermute(zsum, "band", YS[d]) for d in (3, 1, 2)]
+    y_in = [lax.ppermute(zsum, "band", YS[d]) for d in (3, 2, 1)]
 
     mine = call(y_sum_kernel, 4, message)(zsum, *y_in)
     other = lax.ppermute(mine, "band", HI)

time: 49.9 us -> 49.8 us (level)
  the two profiles are of different devices: /device:TPU:28 before, /device:TPU:6 now
where the time goes in v7:
time: 49.8 us; the launch traced here: 49 us
  starting transfers between devices  29.5 us (59%)
  waiting for transfers between devices  10.6 us (21%)
  Pallas kernels  8.11 us (16%)
  between operations  0.73 us (1%)
    ppermute x3, starting transfers between devices, body(): y_in = [lax.ppermute(zsum, 'band', YS[d]) for d in (3, 2, 1)]  5.9 us
    ppermute x1, starting transfers between devices, body(): other = lax.ppermute(mine, 'band', HI)  5.4 us
    ppermute x3, starting transfers between devices, body(): lax.ppermute(s_b[i], 'row', perm)  4.36 us
    ppermute x1, starting transfers between devices, body(): zb = lax.ppermute(zb, 'row', ZB)  4.3 us
    pallas_call x1, Pallas kernels, body(): call(first_kernel, 4, [sds(PART + ROWS, orbits), sds(orbits, panels, dtyp...  4.18 us
    ppermute x3, starting transfers between devices, body(): lax.ppermute(s_a[i], 'row', perm)  3.59 us
    ppermute x1, starting transfers between devices, body(): z2 = lax.ppermute(z2, 'row', Z2)  3.28 us
    ppermute x1, waiting for transfers between devices, body(): other = lax.ppermute(mine, 'band', HI)  3.25 us
  transfers between devices with their start and end apart: 15, of which 7 were waited for; matrix products, arithmetic and copies ran while one was open for 0% of the time, Pallas kernels for 6%

profile of v7, /device:TPU:6, one launch (start us, length us, event | category | flops | bytes accessed | tf_op | source)
XLA Modules:
  0.0 49.0 jit_solution(6144069491925052892)
XLA Ops:
  0.6 4.2 %shard_map.77 = (f32[576,256]{1,0:T(8,128)S(1)}, bf16[256,2048]{1,0:T(8,128)(2,1)S(1)}, bf16[2,4,64,2048]{3,2,1,0:T(8,128)(2,1)S(1)}, bf16[2,4,64,2048]{3,2,1,0:...) custom-call(s32[1,2]{1,0:T(1,128)} %edges_hbm.1, ...), custom_call_target="tpu_custom_call" | custom-call | flops 33554432 | tf_op jit(solution)/shard_map/pallas_call | solution.py:280
  4.8 0.1 collective-permute-start.1
  4.9 0.7 %shard_map.78.refs_0_.t = f32[512,256]{1,0:T(8,128)S(1)} custom-call(bf16[256,2048]{1,0:T(8,128)(2,1)S(1)} %get-tuple-element.24.p, bf16[2,4,64,2048]{3,2,1,0:T(8,128)(2,1)S(1)} %get-tuple-element.27.g), custom_call_target="tpu_custom_call" | custom-call | flops 33554432 | tf_op jit(solution)/shard_map/pallas_call | solution.py:297
  5.7 0.7 %shard_map.79 = f32[512,256]{1,0:T(8,128)S(1)} custom-call(bf16[256,2048]{1,0:T(8,128)(2,1)S(1)} %get-tuple-element.24.p, bf16[2,4,64,2048]{3,2,1,0:T(8,128)(2,1)S(1)} %get-tuple-element.26.g, f32[512,256]{1,0:T(8,128)S(1)} %shard_map.78.refs_0_.t), custom_call_target="tpu_custom_call" | custom-call | flops 33554432 | tf_op jit(solution)/shard_map/pallas_call | solution.py:298
  6.4 0.6 %collective-permute-start = (f32[512,256]{1,0:T(8,128)S(1)}, f32[512,256]{1,0:T(8,128)S(1)}, u32[]{:S(2)}, u32[]{:S(2)}) collective-permute-start(f32[512,256]{1,0:T(8,128)S(1)} %shard_map.79), channel_id=1, source_target_pairs={{0,1},{1,0},{2,3},{3,2},{4,5},{5,4},{6,7},{7,6},{8,9},{9,8},{10,11... | collective-permute-start | bytes 1572872 | tf_op jit(solution)/shard_map/ppermute | solution.py:299
  7.0 0.1 shard_map.80
  7.1 1.5 %collective-permute-start.6 = (f32[128,256]{1,0:T(8,128)S(1)}, f32[128,256]{1,0:T(8,128)S(1)}, u32[]{:S(2)}, u32[]{:S(2)}) collective-permute-start(f32[128,256]{1,0:T(8,128)S(1)} %get-tuple-element.35), channel_id=1, source_target_pairs={{0,4},{1,5},{2,6},{3,7},{4,0},{5,1},{6,2},{7,3},{8,12},{9,13},{10,... | collective-permute-start | bytes 393224 | tf_op jit(solution)/shard_map/ppermute | solution.py:302
  8.6 2.1 %collective-permute-start.5 = (f32[192,256]{1,0:T(8,128)S(1)}, f32[192,256]{1,0:T(8,128)S(1)}, u32[]{:S(2)}, u32[]{:S(2)}) collective-permute-start(f32[192,256]{1,0:T(8,128)S(1)} %get-tuple-element.34), channel_id=1, source_target_pairs={{0,2},{1,7},{2,4},{3,1},{4,6},{5,3},{6,0},{7,5},{8,10},{9,15},{10,... | collective-permute-start | bytes 589832 | tf_op jit(solution)/shard_map/ppermute | solution.py:302
  10.7 0.0 collective-permute-start.7
  10.7 0.0 collective-permute-done.u
  10.7 0.0 copy-start.1
  10.7 0.8 %shard_map.81 = (f32[128,256]{1,0:T(8,128)S(1)}, f32[128,256]{1,0:T(8,128)S(1)}, f32[128,256]{1,0:T(8,128)S(1)}, f32[128,256]{1,0:T(8,128)S(1)}) custom-call(bf16[256,2048]{1,0:T(8,128)(2,1)S(1)} %get-tuple-element.24.p, bf16[2,4,64,2048]{3,2,1,0:T(8,128)(2,1)S(1)} %get-tuple-element.25.g, f32[512,256]{1,0:T(8,128)S(1)} %collective-permute-done.u, ...), custom_call_target="tpu_custom_call" | custom-call | flops 33554432 | tf_op jit(solution)/shard_map/pallas_call | solution.py:303
  11.5 3.3 %collective-permute-start.2 = (f32[128,256]{1,0:T(8,128)S(1)}, f32[128,256]{1,0:T(8,128)S(1)}, u32[]{:S(2)}, u32[]{:S(2)}) collective-permute-start(f32[128,256]{1,0:T(8,128)S(1)} %get-tuple-element.31), channel_id=1, source_target_pairs={{0,2},{1,7},{2,4},{3,1},{4,6},{5,3},{6,0},{7,5},{8,10},{9,15},{10,... | collective-permute-start | bytes 393224 | tf_op jit(solution)/shard_map/ppermute | solution.py:306
  14.8 0.4 collective-permute-start.3
  15.2 0.0 collective-permute-done.6.c
  15.2 0.6 %collective-permute-start.4 = (f32[128,256]{1,0:T(8,128)S(1)}, f32[128,256]{1,0:T(8,128)S(1)}, u32[]{:S(2)}, u32[]{:S(2)}) collective-permute-start(f32[128,256]{1,0:T(8,128)S(1)} %get-tuple-element.33), channel_id=1, source_target_pairs={{0,6},{1,3},{2,0},{3,5},{4,2},{5,7},{6,4},{7,1},{8,14},{9,11},{10,... | collective-permute-start | bytes 393224 | tf_op jit(solution)/shard_map/ppermute | solution.py:306
  15.9 2.5 %collective-permute-done.7.d = f32[128,256]{1,0:T(8,128)S(1)} collective-permute-done((f32[128,256]{1,0:T(8,128)S(1)}, f32[128,256]{1,0:T(8,128)S(1)}, u32[]{:S(2)}, u32[]{:S(2)}) %collective-permute-start.7) | collective-permute-done | bytes 131104 | tf_op jit(solution)/shard_map/ppermute | solution.py:302
  18.4 2.0 %collective-permute-start.8 = (f32[128,256]{1,0:T(8,128)S(1)}, f32[128,256]{1,0:T(8,128)S(1)}, u32[]{:S(2)}, u32[]{:S(2)}) collective-permute-start(f32[128,256]{1,0:T(8,128)S(1)} %get-tuple-element.39), channel_id=1, source_target_pairs={{0,8},{1,25},{2,10},{3,27},{4,12},{5,29},{6,14},{7,31},{8,16},{9,1... | collective-permute-start | bytes 393224 | tf_op jit(solution)/shard_map/ppermute | solution.py:310
  20.4 3.3 %collective-permute-start.9 = (f32[64,256]{1,0:T(8,128)S(1)}, f32[64,256]{1,0:T(8,128)S(1)}, u32[]{:S(2)}, u32[]{:S(2)}) collective-permute-start(f32[64,256]{1,0:T(8,128)S(1)} %get-tuple-element.37.after), channel_id=1, source_target_pairs={{0,16},{1,17},{2,18},{3,19},{4,20},{5,21},{6,22},{7,23},{8,24},{9,... | collective-permute-start | bytes 196616 | tf_op jit(solution)/shard_map/ppermute | solution.py:309
  23.7 4.3 %collective-permute-start.10 = (f32[64,256]{1,0:T(8,128)S(1)}, f32[64,256]{1,0:T(8,128)S(1)}, u32[]{:S(2)}, u32[]{:S(2)}) collective-permute-start(f32[64,256]{1,0:T(8,128)S(1)} %get-tuple-element.40), channel_id=1, source_target_pairs={{0,24},{1,9},{2,26},{3,11},{4,28},{5,13},{6,30},{7,15},{8,0},{9,17... | collective-permute-start | bytes 196616 | tf_op jit(solution)/shard_map/ppermute | solution.py:312
  28.0 1.1 %collective-permute-done.9.c = f32[64,256]{1,0:T(8,128)S(1)} collective-permute-done((f32[64,256]{1,0:T(8,128)S(1)}, f32[64,256]{1,0:T(8,128)S(1)}, u32[]{:S(2)}, u32[]{:S(2)}) %collective-permute-start.9) | collective-permute-done | bytes 65568 | tf_op jit(solution)/shard_map/ppermute | solution.py:309
  29.1 0.8 %collective-permute-done.10.b = f32[64,256]{1,0:T(8,128)S(1)} collective-permute-done((f32[64,256]{1,0:T(8,128)S(1)}, f32[64,256]{1,0:T(8,128)S(1)}, u32[]{:S(2)}, u32[]{:S(2)}) %collective-permute-start.10) | collective-permute-done | bytes 65568 | tf_op jit(solution)/shard_map/ppermute | solution.py:312
  29.9 1.7 %collective-permute-start.13 = (f32[72,256]{1,0:T(8,128)S(1)}, f32[72,256]{1,0:T(8,128)S(1)}, u32[]{:S(2)}, u32[]{:S(2)}) collective-permute-start(f32[72,256]{1,0:T(8,128)S(1)} %shard_map.85.a), channel_id=1, source_target_pairs={{0,32},{32,64},{64,96},{96,0},{128,160},{160,192},{192,224},{224,1... | collective-permute-start | bytes 221192 | tf_op jit(solution)/shard_map/ppermute | solution.py:315
  31.6 2.9 %collective-permute-start.12 = (f32[72,256]{1,0:T(8,128)S(1)}, f32[72,256]{1,0:T(8,128)S(1)}, u32[]{:S(2)}, u32[]{:S(2)}) collective-permute-start(f32[72,256]{1,0:T(8,128)S(1)} %shard_map.85.a), channel_id=1, source_target_pairs={{0,64},{32,96},{64,0},{96,32},{128,192},{160,224},{192,128},{224,1... | collective-permute-start | bytes 221192 | tf_op jit(solution)/shard_map/ppermute | solution.py:315
  34.5 1.3 %collective-permute-start.11 = (f32[72,256]{1,0:T(8,128)S(1)}, f32[72,256]{1,0:T(8,128)S(1)}, u32[]{:S(2)}, u32[]{:S(2)}) collective-permute-start(f32[72,256]{1,0:T(8,128)S(1)} %shard_map.85.a), channel_id=1, source_target_pairs={{0,96},{32,0},{64,32},{96,64},{128,224},{160,128},{192,160},{224,1... | collective-permute-start | bytes 221192 | tf_op jit(solution)/shard_map/ppermute | solution.py:315
  35.8 0.5 %collective-permute-done.13.d = f32[72,256]{1,0:T(8,128)S(1)} collective-permute-done((f32[72,256]{1,0:T(8,128)S(1)}, f32[72,256]{1,0:T(8,128)S(1)}, u32[]{:S(2)}, u32[]{:S(2)}) %collective-permute-start.13) | collective-permute-done | bytes 73760 | tf_op jit(solution)/shard_map/ppermute | solution.py:315
  36.3 1.2 %collective-permute-done.12.c = f32[72,256]{1,0:T(8,128)S(1)} collective-permute-done((f32[72,256]{1,0:T(8,128)S(1)}, f32[72,256]{1,0:T(8,128)S(1)}, u32[]{:S(2)}, u32[]{:S(2)}) %collective-permute-start.12) | collective-permute-done | bytes 73760 | tf_op jit(solution)/shard_map/ppermute | solution.py:315
  37.6 1.2 %collective-permute-done.11.b = f32[72,256]{1,0:T(8,128)S(1)} collective-permute-done((f32[72,256]{1,0:T(8,128)S(1)}, f32[72,256]{1,0:T(8,128)S(1)}, u32[]{:S(2)}, u32[]{:S(2)}) %collective-permute-start.11) | collective-permute-done | bytes 73760 | tf_op jit(solution)/shard_map/ppermute | solution.py:315
  38.8 5.4 %collective-permute-start.14 = (f32[72,256]{1,0:T(8,128)S(1)}, f32[72,256]{1,0:T(8,128)S(1)}, u32[]{:S(2)}, u32[]{:S(2)}) collective-permute-start(f32[72,256]{1,0:T(8,128)S(1)} %shard_map.86.mine), channel_id=1, source_target_pairs={{0,128},{32,160},{64,192},{96,224},{128,0},{160,32},{192,64},{224,... | collective-permute-start | bytes 221192 | tf_op jit(solution)/shard_map/ppermute | solution.py:318
  44.2 0.5 shard_map.87.side
  44.7 3.2 %collective-permute-done.14.other = f32[72,256]{1,0:T(8,128)S(1)} collective-permute-done((f32[72,256]{1,0:T(8,128)S(1)}, f32[72,256]{1,0:T(8,128)S(1)}, u32[]{:S(2)}, u32[]{:S(2)}) %collective-permute-start.14) | collective-permute-done | bytes 73760 | tf_op jit(solution)/shard_map/ppermute | solution.py:318
  48.0 1.0 %shard_map.88 = (f32[64,256]{1,0:T(8,128)}, f32[64,256]{1,0:T(8,128)}) custom-call(f32[72,256]{1,0:T(8,128)S(1)} %shard_map.86.mine, f32[72,256]{1,0:T(8,128)S(1)} %collective-permute-done.14.other, f32[64,256]{1,0:T(8,128)S(1)} %shard_map.87.side, f32[64,256]{1,0:T(8,128)S(1)} %get-tuple-element.43.window), custom_call_target="tpu_custom_call" | custom-call | tf_op jit(solution)/shard_map/pallas_call | solution.py:322
  (14 shorter events, 0.1 us)
Async XLA Ops:
  4.8 2.2 %collective-permute-start.1 = (f32[576,256]{1,0:T(8,128)S(1)}, f32[576,256]{1,0:T(8,128)S(1)}, u32[]{:S(2)}, u32[]{:S(2)}) collective-permute-start(f32[576,256]{1,0:T(8,128)S(1)} %get-tuple-element.28), channel_id=1, source_target_pairs={{0,1},{1,0},{2,3},{3,2},{4,5},{5,4},{6,7},{7,6},{8,9},{9,8},{10,11... | collective-permute-start | bytes 1769480 | tf_op jit(solution)/shard_map/ppermute | solution.py:296
  6.4 4.3 %collective-permute-start = (f32[512,256]{1,0:T(8,128)S(1)}, f32[512,256]{1,0:T(8,128)S(1)}, u32[]{:S(2)}, u32[]{:S(2)}) collective-permute-start(f32[512,256]{1,0:T(8,128)S(1)} %shard_map.79), channel_id=1, source_target_pairs={{0,1},{1,0},{2,3},{3,2},{4,5},{5,4},{6,7},{7,6},{8,9},{9,8},{10,11... | collective-permute-start | bytes 1572872 | tf_op jit(solution)/shard_map/ppermute | solution.py:299
  7.1 8.1 %collective-permute-start.6 = (f32[128,256]{1,0:T(8,128)S(1)}, f32[128,256]{1,0:T(8,128)S(1)}, u32[]{:S(2)}, u32[]{:S(2)}) collective-permute-start(f32[128,256]{1,0:T(8,128)S(1)} %get-tuple-element.35), channel_id=1, source_target_pairs={{0,4},{1,5},{2,6},{3,7},{4,0},{5,1},{6,2},{7,3},{8,12},{9,13},{10,... | collective-permute-start | bytes 393224 | tf_op jit(solution)/shard_map/ppermute | solution.py:302
  8.6 9.7 %collective-permute-start.5 = (f32[192,256]{1,0:T(8,128)S(1)}, f32[192,256]{1,0:T(8,128)S(1)}, u32[]{:S(2)}, u32[]{:S(2)}) collective-permute-start(f32[192,256]{1,0:T(8,128)S(1)} %get-tuple-element.34), channel_id=1, source_target_pairs={{0,2},{1,7},{2,4},{3,1},{4,6},{5,3},{6,0},{7,5},{8,10},{9,15},{10,... | collective-permute-start | bytes 589832 | tf_op jit(solution)/shard_map/ppermute | solution.py:302
  10.7 7.6 %collective-permute-start.7 = (f32[128,256]{1,0:T(8,128)S(1)}, f32[128,256]{1,0:T(8,128)S(1)}, u32[]{:S(2)}, u32[]{:S(2)}) collective-permute-start(f32[128,256]{1,0:T(8,128)S(1)} %get-tuple-element.36), channel_id=1, source_target_pairs={{0,6},{1,3},{2,0},{3,5},{4,2},{5,7},{6,4},{7,1},{8,14},{9,11},{10,... | collective-permute-start | bytes 393224 | tf_op jit(solution)/shard_map/ppermute | solution.py:302
  10.7 33.6 %copy-start = (s32[64,4]{0,1:T(4,128)S(1)}, s32[64,4]{0,1:T(4,128)}, u32[]{:S(2)}) copy-start(s32[64,4]{0,1:T(4,128)} %param.11) | copy-start | bytes 3076
  10.7 33.5 %copy-start.1 = (f32[64]{0:T(128)S(1)}, f32[64]{0:T(128)}, u32[]{:S(2)}) copy-start(f32[64]{0:T(128)} %param.10) | copy-start | bytes 772
  11.5 12.1 %collective-permute-start.2 = (f32[128,256]{1,0:T(8,128)S(1)}, f32[128,256]{1,0:T(8,128)S(1)}, u32[]{:S(2)}, u32[]{:S(2)}) collective-permute-start(f32[128,256]{1,0:T(8,128)S(1)} %get-tuple-element.31), channel_id=1, source_target_pairs={{0,2},{1,7},{2,4},{3,1},{4,6},{5,3},{6,0},{7,5},{8,10},{9,15},{10,... | collective-permute-start | bytes 393224 | tf_op jit(solution)/shard_map/ppermute | solution.py:306
  14.8 8.8 %collective-permute-start.3 = (f32[128,256]{1,0:T(8,128)S(1)}, f32[128,256]{1,0:T(8,128)S(1)}, u32[]{:S(2)}, u32[]{:S(2)}) collective-permute-start(f32[128,256]{1,0:T(8,128)S(1)} %get-tuple-element.32), channel_id=1, source_target_pairs={{0,4},{1,5},{2,6},{3,7},{4,0},{5,1},{6,2},{7,3},{8,12},{9,13},{10,... | collective-permute-start | bytes 393224 | tf_op jit(solution)/shard_map/ppermute | solution.py:306
  15.2 8.4 %collective-permute-start.4 = (f32[128,256]{1,0:T(8,128)S(1)}, f32[128,256]{1,0:T(8,128)S(1)}, u32[]{:S(2)}, u32[]{:S(2)}) collective-permute-start(f32[128,256]{1,0:T(8,128)S(1)} %get-tuple-element.33), channel_id=1, source_target_pairs={{0,6},{1,3},{2,0},{3,5},{4,2},{5,7},{6,4},{7,1},{8,14},{9,11},{10,... | collective-permute-start | bytes 393224 | tf_op jit(solution)/shard_map/ppermute | solution.py:306
  18.4 10.7 %collective-permute-start.8 = (f32[128,256]{1,0:T(8,128)S(1)}, f32[128,256]{1,0:T(8,128)S(1)}, u32[]{:S(2)}, u32[]{:S(2)}) collective-permute-start(f32[128,256]{1,0:T(8,128)S(1)} %get-tuple-element.39), channel_id=1, source_target_pairs={{0,8},{1,25},{2,10},{3,27},{4,12},{5,29},{6,14},{7,31},{8,16},{9,1... | collective-permute-start | bytes 393224 | tf_op jit(solution)/shard_map/ppermute | solution.py:310
  20.4 8.7 %collective-permute-start.9 = (f32[64,256]{1,0:T(8,128)S(1)}, f32[64,256]{1,0:T(8,128)S(1)}, u32[]{:S(2)}, u32[]{:S(2)}) collective-permute-start(f32[64,256]{1,0:T(8,128)S(1)} %get-tuple-element.37.after), channel_id=1, source_target_pairs={{0,16},{1,17},{2,18},{3,19},{4,20},{5,21},{6,22},{7,23},{8,24},{9,... | collective-permute-start | bytes 196616 | tf_op jit(solution)/shard_map/ppermute | solution.py:309
  23.7 6.2 %collective-permute-start.10 = (f32[64,256]{1,0:T(8,128)S(1)}, f32[64,256]{1,0:T(8,128)S(1)}, u32[]{:S(2)}, u32[]{:S(2)}) collective-permute-start(f32[64,256]{1,0:T(8,128)S(1)} %get-tuple-element.40), channel_id=1, source_target_pairs={{0,24},{1,9},{2,26},{3,11},{4,28},{5,13},{6,30},{7,15},{8,0},{9,17... | collective-permute-start | bytes 196616 | tf_op jit(solution)/shard_map/ppermute | solution.py:312
  29.9 6.4 %collective-permute-start.13 = (f32[72,256]{1,0:T(8,128)S(1)}, f32[72,256]{1,0:T(8,128)S(1)}, u32[]{:S(2)}, u32[]{:S(2)}) collective-permute-start(f32[72,256]{1,0:T(8,128)S(1)} %shard_map.85.a), channel_id=1, source_target_pairs={{0,32},{32,64},{64,96},{96,0},{128,160},{160,192},{192,224},{224,1... | collective-permute-start | bytes 221192 | tf_op jit(solution)/shard_map/ppermute | solution.py:315
  31.6 6.0 %collective-permute-start.12 = (f32[72,256]{1,0:T(8,128)S(1)}, f32[72,256]{1,0:T(8,128)S(1)}, u32[]{:S(2)}, u32[]{:S(2)}) collective-permute-start(f32[72,256]{1,0:T(8,128)S(1)} %shard_map.85.a), channel_id=1, source_target_pairs={{0,64},{32,96},{64,0},{96,32},{128,192},{160,224},{192,128},{224,1... | collective-permute-start | bytes 221192 | tf_op jit(solution)/shard_map/ppermute | solution.py:315
  34.5 4.4 %collective-permute-start.11 = (f32[72,256]{1,0:T(8,128)S(1)}, f32[72,256]{1,0:T(8,128)S(1)}, u32[]{:S(2)}, u32[]{:S(2)}) collective-permute-start(f32[72,256]{1,0:T(8,128)S(1)} %shard_map.85.a), channel_id=1, source_target_pairs={{0,96},{32,0},{64,32},{96,64},{128,224},{160,128},{192,160},{224,1... | collective-permute-start | bytes 221192 | tf_op jit(solution)/shard_map/ppermute | solution.py:315
  38.8 9.1 %collective-permute-start.14 = (f32[72,256]{1,0:T(8,128)S(1)}, f32[72,256]{1,0:T(8,128)S(1)}, u32[]{:S(2)}, u32[]{:S(2)}) collective-permute-start(f32[72,256]{1,0:T(8,128)S(1)} %shard_map.86.mine), channel_id=1, source_target_pairs={{0,128},{32,160},{64,192},{96,224},{128,0},{160,32},{192,64},{224,... | collective-permute-start | bytes 221192 | tf_op jit(solution)/shard_map/ppermute | solution.py:318
